TPU v7x, 32 devices: a whole 2x2x4 slice. The times are simulated.
32 devices in a mesh: groups: 2 (over x), gx: 16 (over z, y, core).
Axes of the slice: x: 2, y: 2, z: 4, core: 2. Of those that a mesh axis runs over, the one named last changes fastest.
Arguments:
- residual: bfloat16 [256, 18432], P('groups', 'gx'), parts along dimension 0, may hold values from -10.1 to 10.1
- norm_gain: float32 [18432], P('gx'), may hold values from 0.5 to 1.5
- w_query: bfloat16 [18432, 6144], P('gx'), may hold values from -0.046875 to 0.046875
- w_keyval: bfloat16 [18432, 512], P('gx'), may hold values from -0.09375 to 0.09375
- w_output: bfloat16 [6144, 18432], P(None, 'gx'), may hold values from -0.078125 to 0.078125
- key_cache: bfloat16 [256, 512, 256], P(('groups', 'gx')), parts along dimension 0, may hold values from -266 to 266
- value_cache: bfloat16 [256, 512, 256], P(('groups', 'gx')), parts along dimension 0, may hold values from -18 to 18
- lengths: int32 [256], P(('groups', 'gx')), parts along dimension 0, may hold values from 2 to 512, as said below
- positions: int32 [256], P(('groups', 'gx')), parts along dimension 0, may hold values from 2 to 767, as said below
Outputs:
- updated: float32 [256, 18432], P('groups', 'gx'), parts along dimension 0
- new_keyval: float32 [256, 512], P(('groups', 'gx')), parts along dimension 0
There are 2 independent parts, one for each index of `groups`. A program takes and returns all parts, laid end to end along the dimension named above; an argument that names none is the same for every part. Nothing has to cross between parts.
Inputs may be any that keep to these rules, and one draw needn't show every extreme that they name: Slots 0 to lengths[b] - 1 of request b's cache are filled; some request has all 512 slots filled. `positions`: each request's position is its length plus 0 to 255; some request has position 767.
All inputs are finite; a program needn't handle non-finite values.
Results may differ from a plain program's by a relative error of at most 0.011.
Values may be sent and summed in bfloat16 or wider, within the bound.
No kernel may reach another device: no remote copies, remote signals or barrier semaphores. Data moves between devices by JAX's collectives and lax.ppermute only.
A program may use at most 128 MiB of HBM per device.

v0:
```python
import math

import jax
import jax.numpy as jnp
from jax import lax
from jax.sharding import PartitionSpec as P

D = 18432
HD = 256


EPSILON = 1e-05


def rope_tables(position_rows):
    half_width = HD // 2
    inverse_freq = 10000.0 ** (-(jnp.arange(half_width, dtype=jnp.float32) * 2.0 / HD))
    angles = position_rows.astype(jnp.float32)[:, None] * inverse_freq[None, :]
    return (jnp.cos(angles), jnp.sin(angles))


def rotate_pairs(values, cosine, sine_part):
    half_width = values.shape[-1] // 2
    first = values[..., :half_width]
    second = values[..., half_width:]
    return jnp.concatenate(
        [first * cosine - second * sine_part, second * cosine + first * sine_part], axis=-1
    )


def attend_rows(projected, key_block, value_block, length_rows, position_rows):
    row_total = projected.shape[0]
    query_width = projected.shape[1] - 2 * HD
    queries = projected[:, :query_width].reshape(row_total, query_width // HD, HD)
    new_key = projected[:, query_width : query_width + HD]
    new_value = projected[:, query_width + HD :]
    cosine, sine_part = rope_tables(position_rows)
    rotated_q = rotate_pairs(queries, cosine[:, None, :], sine_part[:, None, :]).astype(
        jnp.bfloat16
    )
    rotated_k = rotate_pairs(new_key, cosine, sine_part)
    new_keyval = jnp.concatenate([rotated_k, new_value], axis=1)
    key_rounded = rotated_k.astype(jnp.bfloat16)
    value_rounded = new_value.astype(jnp.bfloat16)
    scale_factor = 1.0 / math.sqrt(HD)
    scores = (
        jnp.einsum("rhd,rkd->rhk", rotated_q, key_block, preferred_element_type=jnp.float32)
        * scale_factor
    )
    own_score = (
        jnp.einsum("rhd,rd->rh", rotated_q, key_rounded, preferred_element_type=jnp.float32)
        * scale_factor
    )
    slot_ids = jnp.arange(key_block.shape[1], dtype=jnp.int32)
    valid = slot_ids[None, None, :] < length_rows[:, None, None]
    masked = jnp.where(valid, scores, -jnp.inf)
    highest = jnp.maximum(jnp.max(masked, axis=-1), own_score)
    exps = jnp.exp(masked - highest[..., None])
    own_exp = jnp.exp(own_score - highest)
    denominator = jnp.sum(exps, axis=-1) + own_exp
    weights = (exps / denominator[..., None]).astype(jnp.bfloat16)
    own_weight = (own_exp / denominator).astype(jnp.bfloat16)
    attended = jnp.einsum("rhk,rkd->rhd", weights, value_block, preferred_element_type=jnp.float32)
    attended = (
        attended
        + own_weight.astype(jnp.float32)[..., None] * value_rounded.astype(jnp.float32)[:, None, :]
    )
    return (attended.astype(jnp.bfloat16).reshape(row_total, query_width), new_keyval)


def local(
    residual, norm_gain, w_query, w_keyval, w_output, key_cache, value_cache, lengths, positions
):
    stream = residual.astype(jnp.float32)
    moments = lax.psum((jnp.sum(stream, axis=1), jnp.sum(stream * stream, axis=1)), "gx")
    row_mean = moments[0][:, None] / D
    row_square = moments[1][:, None] / D
    normed = (
        (stream - row_mean)
        * lax.rsqrt(row_square - row_mean * row_mean + EPSILON)
        * norm_gain[None, :]
    ).astype(jnp.bfloat16)
    projected = lax.psum_scatter(
        jnp.concatenate(
            [
                jnp.dot(normed, w_query, preferred_element_type=jnp.float32),
                jnp.dot(normed, w_keyval, preferred_element_type=jnp.float32),
            ],
            axis=1,
        ),
        "gx",
        scatter_dimension=0,
        tiled=True,
    )
    attended, new_keyval = attend_rows(projected, key_cache, value_cache, lengths, positions)
    mixed = jnp.dot(
        lax.all_gather(attended, "gx", axis=0, tiled=True),
        w_output,
        preferred_element_type=jnp.float32,
    )
    updated = stream + mixed
    return (updated, new_keyval)


def solution(mesh):
    in_specs = (
        P("groups", "gx"),
        P("gx"),
        P("gx", None),
        P("gx", None),
        P(None, "gx"),
        P(("groups", "gx"), None, None),
        P(("groups", "gx"), None, None),
        P(("groups", "gx")),
        P(("groups", "gx")),
    )
    out_specs = (P("groups", "gx"), P(("groups", "gx"), None))
    return jax.shard_map(local, mesh=mesh, in_specs=in_specs, out_specs=out_specs, check_vma=False)
```

profile of v0, /device:TPU:0, one launch (start us, length us, event | category | flops | bytes accessed | tf_op | source)
XLA Modules:
  0.0 176.5 jit_solution(14969257848123049543)
XLA Ops:
  7.2 0.0 copy-start
  7.2 0.0 reduce-scatter.2.cloned.1.call-start
  7.2 1.3 convert_reduce_fusion
  8.5 34.9 %all-reduce = (f32[128]{0:T(128)S(1)}, f32[128]{0:T(128)S(1)}) all-reduce(f32[128]{0:T(128)S(1)} %get-tuple-element.3, f32[128]{0:T(128)S(1)} %get-tuple-element.2), channel_id=1, replica_groups=mesh['groups'=2,'gx'=16] {'gx'}, use_global_device_ids=true, to_apply=%region_3.0 | all-reduce | flops 256 | bytes 2048 | tf_op jit(solution)/shard_map/psum | solution.py:75
  43.4 0.0 copy-start.4
  43.4 7.5 %fusion.18 = f32[128,6144]{1,0:T(8,128)S(1)} fusion(bf16[1152,6144]{1,0:T(8,128)(2,1)} %param.11, bf16[128,1152]{1,0:T(8,128)(2,1)} %param.9, f32[1152]{0:T(1024)} %param.10, f32[128]{0:T(128)S(1)} %get-tuple-element.21, f32[128]{0:T(128)S(1)} %get-tuple-element.20), kind=kOutput, calls=%fused_computation.43 | convolution fusion | flops 1812676608 | bytes 17602048 | tf_op jit(solution)/shard_map/dot_general | solution.py:86
  51.0 0.4 fusion.16
  51.4 2.0 %pad_maximum_fusion = f32[128,6656]{1,0:T(8,128)} fusion(f32[128,512]{1,0:T(8,128)S(1)} %fusion.16, f32[128,6144]{1,0:T(8,128)S(1)} %fusion.18), kind=kLoop, calls=%fused_computation | loop fusion | flops 851968 | bytes 6815744 | tf_op jit(solution)/shard_map/concatenate | solution.py:84
  53.4 0.0 reduce-scatter.2.cloned.1.call-update
  53.4 0.0 all-gather.2.cloned.1.call-start
  53.5 0.6 copy-done.7
  54.1 0.1 iota_compare_fusion
  54.2 63.9 %reduce-scatter.2.cloned.1.call-done = f32[8,6656]{1,0:T(8,128)} async-done(((f32[128,6656]{1,0:T(8,128)}), f32[8,6656]{1,0:T(8,128)}) %reduce-scatter.2.cloned.1.call-update) | async-done | bytes 213008 | tf_op jit(solution)/shard_map/reduce_scatter | solution.py:83
  118.1 0.9 slice.27
  119.1 0.9 fusion.20
  120.1 0.1 fusion.10
  120.2 0.8 fusion.23
  121.0 0.2 fusion.7
  121.2 0.5 fusion.2
  121.7 0.7 copy.17
  122.4 0.0 all-gather.2.cloned.1.call-update
  122.4 0.6 pad_maximum_fusion.4
  123.0 38.1 %all-gather.2.cloned.1.call-done = bf16[128,6144]{1,0:T(8,128)(2,1)} async-done(((bf16[8,6144]{1,0:T(8,128)(2,1)}), bf16[128,6144]{1,0:T(8,128)(2,1)}) %all-gather.2.cloned.1.call-update) | async-done | bytes 1572880 | tf_op jit(solution)/shard_map/all_gather | solution.py:97
  161.1 8.5 %convolution_add_fusion = f32[128,1152]{1,0:T(8,128)} fusion(bf16[128,6144]{1,0:T(8,128)(2,1)} %all-gather.2.cloned.1.call-done, bf16[6144,1152]{1,0:T(8,128)(2,1)} %param.13, bf16[128,1152]{1,0:T(8,128)(2,1)S(1)} %copy-done.1), kind=kOutput, calls=%fused_computation.1 | convolution fusion | flops 1812234240 | bytes 16613376 | tf_op jit(solution)/shard_map/dot_general | solution.py:96
  (24 shorter events, 0.1 us)
Async XLA Ops:
  7.2 113.0 %copy-start = (bf16[8,512,256]{2,1,0:T(8,128)(2,1)S(1)}, bf16[8,512,256]{2,1,0:T(8,128)(2,1)}, u32[]{:S(2)}) copy-start(bf16[8,512,256]{2,1,0:T(8,128)(2,1)} %param.14) | copy-start | bytes 6291460
  7.2 110.9 %reduce-scatter.2.cloned.1.call-start = ((), (), s32[]{:S(2)}) async-start(), calls=%async_computation.1 | async-start | bytes 3620864 | tf_op jit(solution)/shard_map/reduce_scatter | solution.py:83
  43.4 7.6 %copy-start.1 = (bf16[128,1152]{1,0:T(8,128)(2,1)S(1)}, bf16[128,1152]{1,0:T(8,128)(2,1)}, u32[]{:S(2)}) copy-start(bf16[128,1152]{1,0:T(8,128)(2,1)} %param.9) | copy-start | bytes 884740
  43.4 7.6 %copy-start.2 = (bf16[1152,512]{1,0:T(8,128)(2,1)S(1)}, bf16[1152,512]{1,0:T(8,128)(2,1)}, u32[]{:S(2)}) copy-start(bf16[1152,512]{1,0:T(8,128)(2,1)} %param.12) | copy-start | bytes 3538948
  43.4 7.6 %copy-start.4 = (f32[1152]{0:T(1024)S(1)}, f32[1152]{0:T(1024)}, u32[]{:S(2)}) copy-start(f32[1152]{0:T(1024)} %param.10) | copy-start | bytes 13828
  53.4 0.7 copy-start.7
  53.4 0.7 copy-start.5
  53.4 107.7 %all-gather.2.cloned.1.call-start = ((), (), s32[]{:S(2)}) async-start(), calls=%async_computation.2 | async-start | bytes 1671168 | tf_op jit(solution)/shard_map/all_gather | solution.py:97
  119.0 2.2 %copy-start.3 = (f32[8,6656]{1,0:T(8,128)S(1)}, f32[8,6656]{1,0:T(8,128)}, u32[]{:S(2)}) copy-start(f32[8,6656]{1,0:T(8,128)} %reduce-scatter.2.cloned.1.call-done) | copy-start | bytes 638980
  119.0 2.2 %copy-start.6 = (bf16[8,512,256]{2,1,0:T(8,128)(2,1)S(1)}, bf16[8,512,256]{2,1,0:T(8,128)(2,1)}, u32[]{:S(2)}) copy-start(bf16[8,512,256]{2,1,0:T(8,128)(2,1)} %param.15) | copy-start | bytes 6291460
  121.0 1.4 slice-start
Sparse Core Ops, SparseCore 0:
  53.6 64.4 reduce-scatter.1
  122.5 38.5 all-gather.1
where the time goes:
time: 177 us; the launch traced here: 176 us
  waiting for transfers between devices  102 us (58%)
  blocking collectives  34.9 us (20%)
  matrix products  17.8 us (10%)
  between operations  14.2 us (8%)
  other arithmetic  5.18 us (3%)
  local copies, waits for them, and re-layouts  2.24 us (1%)
    reduce_scatter x1, waiting for transfers between devices, local(): lax.psum_scatter(jnp.concatenate([jnp.dot(normed, w_query, preferred_elem...  63.9 us
    all_gather x1, waiting for transfers between devices, local(): lax.all_gather(attended, 'gx', axis=0, tiled=True)  38.1 us
    psum x1, blocking collectives, local(): lax.psum((jnp.sum(stream, axis=1), jnp.sum(stream * stream, axis=1)), 'gx')  34.9 us
    dot_general x1, matrix products, local(): jnp.dot(lax.all_gather(attended, 'gx', axis=0, tiled=True), w_output, pre...  8.54 us
    dot_general x1, matrix products, local(): jnp.dot(normed, w_query, preferred_element_type=jnp.float32)  7.53 us
  transfers between devices with their start and end apart: 2, of which 2 were waited for; matrix products, arithmetic and copies ran while one was open for 0% of the time, Pallas kernels for 0%

commit v1 on v0

v1 whole, which is shorter than its diff:
```python
import functools
import math

import jax
import jax.numpy as jnp
from jax import lax
from jax.experimental import pallas as pl
from jax.experimental.pallas import tpu as pltpu
from jax.sharding import PartitionSpec as P

HD = 256
LANES = 128
BLOCK = 8
TILE = 512
EPSILON = 1e-05
VMEM = pl.BlockSpec(memory_space=pltpu.VMEM)
SMEM = pl.BlockSpec(memory_space=pltpu.SMEM)


def rope_tables(position_rows):
    half_width = HD // 2
    inverse_freq = 10000.0 ** (-(jnp.arange(half_width, dtype=jnp.float32) * 2.0 / HD))
    angles = position_rows.astype(jnp.float32)[:, None] * inverse_freq[None, :]
    return (jnp.cos(angles), jnp.sin(angles))


def exchange(value, mask, count):
    return lax.ppermute(value, "gx", [(i, i ^ mask) for i in range(count)])


def block_order(masks):
    order = [0]
    for mask in reversed(masks):
        order = order + [b | mask for b in order]
    return order


def struct(shape, dtype):
    return jax.ShapeDtypeStruct(shape, dtype)


def lane_ids(rows):
    return lax.broadcasted_iota(jnp.int32, (rows, LANES), 1)


def pack_stats(stats):
    high = stats.astype(jnp.bfloat16).astype(jnp.float32)
    middle = (stats - high).astype(jnp.bfloat16).astype(jnp.float32)
    low = stats - high - middle
    lane = lane_ids(stats.shape[0])
    return jnp.where(lane < 2, high, jnp.where(lane < 4, middle, low)).astype(jnp.bfloat16)


def unpack_stats(packed):
    parts = packed.astype(jnp.float32)
    mean = parts[:, 0:1] + parts[:, 2:3] + parts[:, 4:5]
    square = parts[:, 1:2] + parts[:, 3:4] + parts[:, 5:6]
    return jnp.where(lane_ids(parts.shape[0]) % 2 == 0, mean, square)


def project_kernel(order, me_ref, x_ref, gain_ref, wq_ref, wkv_ref, keep_ref, send_ref, stats_ref,
                   side_ref, rows_ref, lhs_ref):
    step = pl.program_id(0)
    total = x_ref.shape[0]
    half = total // 2
    me = me_ref[0]

    @pl.when(step == 0)
    def _():
        rows_ref[...] = x_ref[...].astype(jnp.float32)
        gain = gain_ref[...]
        high = gain.astype(jnp.bfloat16).astype(jnp.float32)
        low = gain - high
        row = lax.broadcasted_iota(jnp.int32, (16, gain.shape[1]), 0)
        lhs_ref[2 * total :, :] = jnp.where(
            row == 0, high, jnp.where(row == 1, low, 0.0)
        ).astype(jnp.bfloat16)
        lane = lane_ids(2 * BLOCK)
        side_ref[...] = jnp.zeros_like(side_ref)
        for pair in range(len(order) // 2):
            pieces = []
            for b in order[2 * pair : 2 * pair + 2]:
                start = pl.multiple_of((me ^ b) * BLOCK, BLOCK)
                pieces.append(rows_ref[pl.ds(start, BLOCK), :])
            x = jnp.concatenate(pieces, axis=0)
            mean = jnp.mean(x, axis=1, keepdims=True)
            square = jnp.mean(x * x, axis=1, keepdims=True)
            at = pair * 2 * BLOCK
            value = (x - mean) * gain
            rounded = value.astype(jnp.bfloat16)
            lhs_ref[at : at + 2 * BLOCK, :] = rounded
            lhs_ref[total + at : total + at + 2 * BLOCK, :] = (
                value - rounded.astype(jnp.float32)
            ).astype(jnp.bfloat16)
            stats_ref[at : at + 2 * BLOCK, :] = jnp.where(lane % 2 == 0, mean, square)

    def tile(weights):
        out = jnp.dot(lhs_ref[...], weights, preferred_element_type=jnp.float32)
        keep_ref[...] = out[:half] + out[total : total + half]
        send_ref[...] = (out[half:total] + out[total + half : 2 * total]).astype(jnp.bfloat16)
        gained = out[2 * total : 2 * total + 1] + out[2 * total + 1 : 2 * total + 2]
        for k in range(TILE // LANES):
            side_ref[pl.ds(step * (TILE // LANES) + k, 1), :] = gained[:, k * LANES : (k + 1) * LANES]

    @pl.when(step == 0)
    def _():
        tile(wkv_ref[...])

    @pl.when(step > 0)
    def _():
        tile(wq_ref[...])


def project(me, order, residual, gain, w_query, w_keyval):
    total, depth = residual.shape
    width = w_query.shape[1] + w_keyval.shape[1]
    half = total // 2
    chunks = width // LANES
    return pl.pallas_call(
        functools.partial(project_kernel, order),
        grid=(width // TILE,),
        in_specs=[
            SMEM,
            pl.BlockSpec((total, depth), lambda j: (0, 0)),
            pl.BlockSpec((1, depth), lambda j: (0, 0)),
            pl.BlockSpec((depth, TILE), lambda j: (0, jnp.maximum(j - 1, 0))),
            pl.BlockSpec((depth, TILE), lambda j: (0, 0)),
        ],
        out_specs=[
            pl.BlockSpec((half, TILE), lambda j: (0, j)),
            pl.BlockSpec((half, TILE), lambda j: (0, j)),
            pl.BlockSpec((total, LANES), lambda j: (0, 0)),
            pl.BlockSpec((chunks, LANES), lambda j: (0, 0)),
        ],
        out_shape=[
            struct((half, width), jnp.float32),
            struct((half, width), jnp.bfloat16),
            struct((total, LANES), jnp.float32),
            struct((chunks, LANES), jnp.float32),
        ],
        scratch_shapes=[
            pltpu.VMEM((total, depth), jnp.float32),
            pltpu.VMEM((2 * total + 16, depth), jnp.bfloat16),
        ],
        compiler_params=pltpu.CompilerParams(vmem_limit_bytes=24 * 2**20),
        name="project",
    )(me, residual, gain, w_query, w_keyval)


def first_kernel(keep_ref, recv_ref, stats_ref, other_stats_ref, side_ref, other_side_ref,
                 keep_a, keep_b, send_a, send_b, stats_a, stats_b, side_a, side_b):
    half, width = keep_ref.shape
    cut = width // 2
    chunks = cut // LANES
    half_a, quarter = half // 2, half // 4
    own = stats_ref[:half, :]
    other = other_stats_ref[...]
    merged = 0.5 * (own + other)
    shift = 0.5 * (own[:, 0:1] - other[:, 0:1])
    stats_a[...] = merged[:half_a]
    packed = pack_stats(merged)
    send_a[:, cut:] = packed[half_a:]
    for k in range(2):
        stats_b[k * quarter : (k + 1) * quarter, :] = merged[2 * k * quarter : (2 * k + 1) * quarter]
        send_b[k * quarter : (k + 1) * quarter, cut:] = packed[
            (2 * k + 1) * quarter : (2 * k + 2) * quarter
        ]
    for c in range(2 * chunks):
        columns = slice(c * LANES, (c + 1) * LANES)
        change = side_ref[c : c + 1, :] - other_side_ref[c : c + 1, :]
        total = keep_ref[:, columns] + recv_ref[:, columns].astype(jnp.float32) + shift * change
        if c < chunks:
            keep_a[:, columns] = total[:half_a]
            send_a[:, columns] = total[half_a:].astype(jnp.bfloat16)
        else:
            columns = slice((c - chunks) * LANES, (c - chunks + 1) * LANES)
            for k in range(2):
                at = slice(k * quarter, (k + 1) * quarter)
                keep_b[at, columns] = total[2 * k * quarter : (2 * k + 1) * quarter]
                send_b[at, columns] = total[
                    (2 * k + 1) * quarter : (2 * k + 2) * quarter
                ].astype(jnp.bfloat16)
    side_a[...] = side_ref[:chunks, :] + other_side_ref[:chunks, :]
    side_b[...] = side_ref[chunks:, :] + other_side_ref[chunks:, :]


def first_combine(keep, recv, stats, other_stats, side, other_side):
    half, width = keep.shape
    cut = width // 2
    rows = half // 2
    chunks = cut // LANES
    return pl.pallas_call(
        first_kernel,
        in_specs=[VMEM] * 6,
        out_specs=[VMEM] * 8,
        out_shape=[struct((rows, cut), jnp.float32)] * 2
        + [struct((rows, cut + LANES), jnp.bfloat16)] * 2
        + [struct((rows, LANES), jnp.float32)] * 2
        + [struct((chunks, LANES), jnp.float32)] * 2,
        compiler_params=pltpu.CompilerParams(vmem_limit_bytes=24 * 2**20),
        name="first_combine",
    )(keep, recv, stats, other_stats, side, other_side)


def middle_kernel(*refs):
    inputs, outputs = refs[:10], refs[10:]
    packed_output = len(outputs) == 4
    for half in range(2):
        keep, recv, stats, side, other_side = inputs[half::2]
        rows, cut = keep.shape
        low = rows // 2
        chunks = cut // LANES
        own = stats[...]
        other = unpack_stats(recv[:, cut:])
        merged = 0.5 * (own + other)
        shift = 0.5 * (own[:, 0:1] - other[:, 0:1])
        at = slice(0, low)
        if packed_output:
            keep_out, send_out, stats_out, side_out = outputs
            at = slice(half * low, (half + 1) * low)
            side_at = slice(half * chunks, (half + 1) * chunks)
        else:
            keep_out, send_out, stats_out, side_out = outputs[half::2]
            side_at = slice(0, chunks)
        stats_out[at, :] = merged[:low]
        for c in range(chunks):
            columns = slice(c * LANES, (c + 1) * LANES)
            change = side[c : c + 1, :] - other_side[c : c + 1, :]
            total = keep[:, columns] + recv[:, columns].astype(jnp.float32) + shift * change
            keep_out[at, columns] = total[:low]
            send_out[at, columns] = total[low:].astype(send_out.dtype)
        send_out[at, cut:] = pack_stats(merged[low:]).astype(send_out.dtype)
        side_out[side_at, :] = side[...] + other_side[...]


def middle_combine(keep, recv, stats, side, other_side):
    rows, cut = keep[0].shape
    low = rows // 2
    chunks = cut // LANES
    if low == BLOCK:
        out_shape = [
            struct((2 * low, cut), jnp.float32),
            struct((2 * low, cut + LANES), jnp.bfloat16),
            struct((2 * low, LANES), jnp.float32),
            struct((2 * chunks, LANES), jnp.float32),
        ]
    else:
        out_shape = (
            [struct((low, cut), jnp.float32)] * 2
            + [struct((low, cut + LANES), jnp.bfloat16)] * 2
            + [struct((low, LANES), jnp.float32)] * 2
            + [struct((chunks, LANES), jnp.float32)] * 2
        )
    return pl.pallas_call(
        middle_kernel,
        in_specs=[VMEM] * 10,
        out_specs=[VMEM] * len(out_shape),
        out_shape=out_shape,
        compiler_params=pltpu.CompilerParams(vmem_limit_bytes=24 * 2**20),
        name="middle_combine",
    )(*keep, *recv, *stats, *side, *other_side)


def attend_kernel(heads, length_ref, keep_ref, recv_ref, stats_ref, side_ref, other_side_ref,
                  cos_ref, sin_ref, key_ref, value_ref, attended_ref, keyval_ref, q_ref, out_ref):
    cut = keep_ref.shape[1]
    chunks = cut // LANES
    slots = key_ref.shape[1]
    own = stats_ref[...]
    other = unpack_stats(recv_ref[:, cut:])
    merged = 0.5 * (own + other)
    shift = 0.5 * (own[:, 0:1] - other[:, 0:1])
    mean, square = merged[:, 0:1], merged[:, 1:2]
    scale = lax.rsqrt(square - mean * mean + EPSILON)
    cosine, sine = cos_ref[...], sin_ref[...]
    upper = lax.broadcasted_iota(jnp.int32, (2 * BLOCK, LANES), 0) >= BLOCK
    new_key = new_value = None
    for c in range(0, chunks, 2):
        pair = []
        for d in (c, c + 1):
            columns = slice(d * LANES, (d + 1) * LANES)
            change = jnp.where(
                upper,
                side_ref[chunks + d : chunks + d + 1, :] - other_side_ref[chunks + d : chunks + d + 1, :],
                side_ref[d : d + 1, :] - other_side_ref[d : d + 1, :],
            )
            total = keep_ref[:, columns] + recv_ref[:, columns].astype(jnp.float32) + shift * change
            pair.append(total * scale)
        for half in range(2):
            u1, u2 = (v[half * BLOCK : (half + 1) * BLOCK] for v in pair)
            number = half * (chunks // 2) + c // 2 - 2
            if number == -1:
                new_value = jnp.concatenate([u1, u2], axis=1)
                continue
            turned = jnp.concatenate([u1 * cosine - u2 * sine, u2 * cosine + u1 * sine], axis=1)
            if number == -2:
                new_key = turned
            else:
                for k in range(2):
                    q_ref[k, number * BLOCK : (number + 1) * BLOCK, :] = turned[
                        :, k * LANES : (k + 1) * LANES
                    ]
    keyval_ref[:, :HD] = new_key
    keyval_ref[:, HD:] = new_value
    factor = 1.0 / math.sqrt(HD)
    slot = lax.broadcasted_iota(jnp.int32, (heads, slots), 1)
    for r in range(BLOCK):
        queries = jnp.concatenate(
            [q_ref.at[k][pl.ds(r, heads, stride=BLOCK), :] for k in range(2)], axis=1
        ).astype(jnp.bfloat16)
        key_row = new_key[r : r + 1].astype(jnp.bfloat16).astype(jnp.float32)
        value_row = new_value[r : r + 1].astype(jnp.bfloat16).astype(jnp.float32)
        scores = (
            lax.dot_general(
                queries, key_ref[r], (((1,), (1,)), ((), ())), preferred_element_type=jnp.float32
            )
            * factor
        )
        own_score = (
            jnp.sum(queries.astype(jnp.float32) * key_row, axis=1, keepdims=True) * factor
        )
        masked = jnp.where(slot < length_ref[r], scores, -jnp.inf)
        highest = jnp.maximum(jnp.max(masked, axis=1, keepdims=True), own_score)
        exps = jnp.exp(masked - highest)
        own_exp = jnp.exp(own_score - highest)
        denominator = jnp.sum(exps, axis=1, keepdims=True) + own_exp
        weights = (exps / denominator).astype(jnp.bfloat16)
        own_weight = (own_exp / denominator).astype(jnp.bfloat16).astype(jnp.float32)
        mixed = jnp.dot(weights, value_ref[r], preferred_element_type=jnp.float32)
        mixed = mixed + own_weight * value_row
        for k in range(2):
            out_ref.at[k][pl.ds(r, heads, stride=BLOCK), :] = mixed[:, k * LANES : (k + 1) * LANES]
    for h in range(heads // 2):
        upper_head = h + heads // 2
        for k in range(2):
            at = h * HD + k * LANES
            attended_ref[:, at : at + LANES] = jnp.concatenate(
                [out_ref[k, g * BLOCK : (g + 1) * BLOCK, :] for g in (h, upper_head)], axis=0
            ).astype(jnp.bfloat16)


def attend(lengths, keep, recv, stats, side, other_side, tables, key_cache, value_cache, heads):
    return pl.pallas_call(
        functools.partial(attend_kernel, heads),
        in_specs=[SMEM] + [VMEM] * 9,
        out_specs=[VMEM] * 2,
        out_shape=[
            struct((2 * BLOCK, heads * HD // 2), jnp.bfloat16),
            struct((BLOCK, 2 * HD), jnp.float32),
        ],
        scratch_shapes=[
            pltpu.VMEM((2, heads * BLOCK, LANES), jnp.float32),
            pltpu.VMEM((2, heads * BLOCK, LANES), jnp.float32),
        ],
        compiler_params=pltpu.CompilerParams(vmem_limit_bytes=24 * 2**20),
        name="attend",
    )(lengths, keep, recv, stats, side, other_side, *tables, key_cache, value_cache)


def output_kernel(order, me_ref, a_own, a_other, b_own, b_other, x_ref, w_ref, out_ref, lhs_ref,
                  acc_ref, rows_ref):
    step = pl.program_id(0)
    total = x_ref.shape[0]
    half = total // 2
    quarter = half // 4
    cut = a_own.shape[1]
    me = me_ref[0]

    @pl.when(step == 0)
    def _():
        lhs_ref[:half, :cut] = a_own[...]
        lhs_ref[half:, :cut] = a_other[...]
        for side, b in enumerate((b_own, b_other)):
            for k, source in enumerate((0, 2, 1, 3)):
                at = side * half + k * quarter
                lhs_ref[at : at + quarter, cut:] = b[source * quarter : (source + 1) * quarter, :]
        acc_ref[...] = jnp.zeros_like(acc_ref)
        rows_ref[...] = x_ref[...].astype(jnp.float32)

    depth = w_ref.shape[0]
    columns = pl.ds(pl.multiple_of(step * depth, depth), depth)
    acc_ref[...] += jnp.dot(lhs_ref[:, columns], w_ref[...], preferred_element_type=jnp.float32)

    @pl.when(step == pl.num_programs(0) - 1)
    def _():
        for p, b in enumerate(order):
            at = pl.ds(pl.multiple_of((me ^ b) * BLOCK, BLOCK), BLOCK)
            out_ref[at, :] = rows_ref[at, :] + acc_ref[p * BLOCK : (p + 1) * BLOCK, :]


def output(me, order, pieces, residual, w_output):
    total, width = residual.shape
    depth = w_output.shape[0]
    half, cut = pieces[0].shape
    steps = 6
    whole = lambda j: (0, 0)
    return pl.pallas_call(
        functools.partial(output_kernel, order),
        grid=(steps,),
        in_specs=[SMEM]
        + [pl.BlockSpec((half, cut), whole)] * 4
        + [
            pl.BlockSpec((total, width), whole),
            pl.BlockSpec((depth // steps, width), lambda j: (j, 0)),
        ],
        out_specs=pl.BlockSpec((total, width), whole),
        out_shape=struct((total, width), jnp.float32),
        scratch_shapes=[
            pltpu.VMEM((total, depth), jnp.bfloat16),
            pltpu.VMEM((total, width), jnp.float32),
            pltpu.VMEM((total, width), jnp.float32),
        ],
        compiler_params=pltpu.CompilerParams(vmem_limit_bytes=30 * 2**20),
        name="output",
    )(me, *pieces, residual, w_output)


def local(
    residual, norm_gain, w_query, w_keyval, w_output, key_cache, value_cache, lengths, positions
):
    count = lax.axis_size("gx")
    me = lax.axis_index("gx").astype(jnp.int32).reshape(1)
    heads = w_query.shape[1] // HD
    masks = [1 << k for k in range(count.bit_length() - 1)]
    paths = (masks, [masks[0], masks[2], masks[1]] + masks[3:])
    order = block_order(masks)
    half = count * BLOCK // 2
    tables = rope_tables(positions)

    keep, send, stats, side = project(
        me, order, residual, norm_gain[None, :], w_query, w_keyval
    )
    recv = exchange(send, masks[0], count)
    other_stats = exchange(stats[half:], masks[0], count)
    other_side = exchange(side, masks[0], count)
    state = first_combine(keep, recv, stats, other_stats, side, other_side)
    for level in range(1, len(masks) - 1):
        keep, send, stats, side = (state[k : k + 2] for k in range(0, 8, 2))
        recv = [exchange(v, path[level], count) for v, path in zip(send, paths)]
        other_side = [exchange(v, path[level], count) for v, path in zip(side, paths)]
        state = middle_combine(keep, recv, stats, side, other_side)
    keep, send, stats, side = state
    recv = exchange(send, masks[-1], count)
    other_side = exchange(side, masks[-1], count)
    attended, new_keyval = attend(
        lengths, keep, recv, stats, side, other_side, tables, key_cache, value_cache, heads
    )

    far = exchange(attended, masks[-1], count)
    pieces = []
    for path, rows in zip(paths, (slice(0, BLOCK), slice(BLOCK, 2 * BLOCK))):
        part = jnp.concatenate([attended[rows], far[rows]])
        for mask in path[-2:0:-1]:
            part = jnp.concatenate([part, exchange(part, mask, count)])
        pieces += [part, exchange(part, masks[0], count)]
    updated = output(me, order, pieces, residual, w_output)
    return (updated, new_keyval)


def solution(mesh):
    in_specs = (
        P("groups", "gx"),
        P("gx"),
        P("gx", None),
        P("gx", None),
        P(None, "gx"),
        P(("groups", "gx"), None, None),
        P(("groups", "gx"), None, None),
        P(("groups", "gx")),
        P(("groups", "gx")),
    )
    out_specs = (P("groups", "gx"), P(("groups", "gx"), None))
    return jax.shard_map(local, mesh=mesh, in_specs=in_specs, out_specs=out_specs, check_vma=False)
```

time: 177 us -> 75.2 us (0.42)
  waiting for transfers between devices: 102 us -> 30.7 us
  blocking collectives: 34.9 us -> 0 us
  Pallas kernels: 0 us -> 18.1 us
  matrix products: 17.8 us -> 0 us
  starting transfers between devices: 0.08 us -> 17.1 us
  between operations: 14.2 us -> 0.82 us
  local copies, waits for them, and re-layouts: 2.24 us -> 8.02 us
  other arithmetic: 5.18 us -> 0.22 us
    reduce_scatter x1 -> x0, waiting for transfers between devices: 63.9 us -> none  [local(): lax.psum_scatter(jnp.concatenate([jnp.dot(normed, w_query, preferred_elem...]
    all_gather x1 -> x0, waiting for transfers between devices: 38.1 us -> none  [local(): lax.all_gather(attended, 'gx', axis=0, tiled=True)]
    psum x1 -> x0, blocking collectives: 34.9 us -> none  [local(): lax.psum((jnp.sum(stream, axis=1), jnp.sum(stream * stream, axis=1)), 'gx')]
    ppermute x0 -> x20, waiting for transfers between devices: none -> 30.7 us  [exchange(): return lax.ppermute(value, 'gx', [(i, i ^ mask) for i in range(count)])]
    pallas_call x0 -> x6, Pallas kernels: none -> 18.1 us  [the longest x1 8.8 us: project(): pl.pallas_call(functools.partial(project_kernel, order), grid=(width // T...]
    dot_general x6 -> x0, matrix products: 17.8 us -> none  [the longest x1 8.54 us: local(): jnp.dot(lax.all_gather(attended, 'gx', axis=0, tiled=True), w_output, pre...]
    ppermute x0 -> x20, starting transfers between devices: none -> 17.1 us  [exchange(): return lax.ppermute(value, 'gx', [(i, i ^ mask) for i in range(count)])]
    unnamed x17 -> x24, local copies, waits for them, and re-layouts: 1.28 us -> 7.3 us
  transfers between devices with their start and end apart: 2 -> 20, of which waited for: 2 -> 12; matrix products, arithmetic and copies ran while one was open for 0% -> 0% of each run, Pallas kernels for 0% -> 0%
where the time goes in v1:
time: 75.2 us; the launch traced here: 75 us
  waiting for transfers between devices  30.7 us (41%)
  Pallas kernels  18.1 us (24%)
  starting transfers between devices  17.1 us (23%)
  local copies, waits for them, and re-layouts  8.02 us (11%)
  between operations  0.82 us (1%)
    ppermute x20, waiting for transfers between devices, exchange(): return lax.ppermute(value, 'gx', [(i, i ^ mask) for i in range(count)])  30.7 us
    ppermute x20, starting transfers between devices, exchange(): return lax.ppermute(value, 'gx', [(i, i ^ mask) for i in range(count)])  17.1 us
    pallas_call x1, Pallas kernels, project(): pl.pallas_call(functools.partial(project_kernel, order), grid=(width // T...  8.8 us
    unnamed x24, local copies, waits for them, and re-layouts  7.3 us
    pallas_call x1, Pallas kernels, output(): pl.pallas_call(functools.partial(output_kernel, order), grid=(steps,), in...  4.29 us
    pallas_call x1, Pallas kernels, attend(): pl.pallas_call(functools.partial(attend_kernel, heads), in_specs=[SMEM] +...  4.08 us
  transfers between devices with their start and end apart: 20, of which 12 were waited for; matrix products, arithmetic and copies ran while one was open for 0% of the time, Pallas kernels for 0%

profile of v1, /device:TPU:0, one launch (start us, length us, event | category | flops | bytes accessed | tf_op | source)
XLA Modules:
  0.0 75.0 jit_solution(90593179937966034)
XLA Ops:
  1.3 5.0 %copy-done = bf16[1152,6144]{1,0:T(8,128)(2,1)S(1)} copy-done((bf16[1152,6144]{1,0:T(8,128)(2,1)S(1)}, bf16[1152,6144]{1,0:T(8,128)(2,1)}, u32[]{:S(2)}) %copy-start) | copy-done | bytes 14155800
  6.4 1.3 %copy-done.3 = bf16[1152,512]{1,0:T(8,128)(2,1)S(1)} copy-done((bf16[1152,512]{1,0:T(8,128)(2,1)S(1)}, bf16[1152,512]{1,0:T(8,128)(2,1)}, u32[]{:S(2)}) %copy-start.3) | copy-done | bytes 1179672
  7.6 1.0 %copy-done.4 = bf16[128,1152]{1,0:T(8,128)(2,1)S(1)} copy-done((bf16[128,1152]{1,0:T(8,128)(2,1)S(1)}, bf16[128,1152]{1,0:T(8,128)(2,1)}, u32[]{:S(2)}) %copy-start.4) | copy-done | bytes 294936
  8.6 8.8 %project.1 = (f32[64,6656]{1,0:T(8,128)S(1)}, bf16[64,6656]{1,0:T(8,128)(2,1)S(1)}, f32[128,128]{1,0:T(8,128)S(1)}, f32[52,128]{1,0:T(8,128)S(1)}) custom-call(s32[1]{0:T(128)} %bitcast.me_ref, bf16[128,1152]{1,0:T(8,128)(2,1)S(1)} %copy-done.4, f32[1,1152]{1,0:T(1,128)S(1)} %broadcast_in_dim.2.gain_ref, bf16[1152,6144]{1,0:T(8,128)(2,1)S(1)} %copy-done, ...), custom_call_target="tpu_custom_call" | custom-call | tf_op jit(solution)/shard_map/project/pallas_call | solution.py:119
  18.4 1.6 %collective-permute-done.2.other_side_ref = f32[52,128]{1,0:T(8,128)S(1)} collective-permute-done((f32[52,128]{1,0:T(8,128)S(1)}, f32[52,128]{1,0:T(8,128)S(1)}, u32[]{:S(2)}, u32[]{:S(2)}) %collective-permute-start.2) | collective-permute-done | bytes 26656 | tf_op jit(solution)/shard_map/ppermute | solution.py:28
  20.4 3.0 %collective-permute-start.3 = (bf16[32,3456]{1,0:T(8,128)(2,1)S(1)}, bf16[32,3456]{1,0:T(8,128)(2,1)S(1)}, u32[]{:S(2)}, u32[]{:S(2)}) collective-permute-start(bf16[32,3456]{1,0:T(8,128)(2,1)S(1)} %get-tuple-element.34), channel_id=1, source_target_pairs={{0,2},{1,3},{2,0},{3,1},{4,6},{5,7},{6,4},{7,5},{8,10},{9,11},{10,... | collective-permute-start | bytes 663560 | tf_op jit(solution)/shard_map/ppermute | solution.py:28
  23.3 1.6 %collective-permute-start.4 = (bf16[32,3456]{1,0:T(8,128)(2,1)S(1)}, bf16[32,3456]{1,0:T(8,128)(2,1)S(1)}, u32[]{:S(2)}, u32[]{:S(2)}) collective-permute-start(bf16[32,3456]{1,0:T(8,128)(2,1)S(1)} %get-tuple-element.35), channel_id=1, source_target_pairs={{0,4},{1,5},{2,6},{3,7},{4,0},{5,1},{6,2},{7,3},{8,12},{9,13},{10,... | collective-permute-start | bytes 663560 | tf_op jit(solution)/shard_map/ppermute | solution.py:28
  25.4 4.0 %collective-permute-done.5.refs_8_ = f32[26,128]{1,0:T(8,128)S(1)} collective-permute-done((f32[26,128]{1,0:T(8,128)S(1)}, f32[26,128]{1,0:T(8,128)S(1)}, u32[]{:S(2)}, u32[]{:S(2)}) %collective-permute-start.5) | collective-permute-done | bytes 13344 | tf_op jit(solution)/shard_map/ppermute | solution.py:28
  29.4 1.5 %collective-permute-done.6.refs_9_ = f32[26,128]{1,0:T(8,128)S(1)} collective-permute-done((f32[26,128]{1,0:T(8,128)S(1)}, f32[26,128]{1,0:T(8,128)S(1)}, u32[]{:S(2)}, u32[]{:S(2)}) %collective-permute-start.6) | collective-permute-done | bytes 13344 | tf_op jit(solution)/shard_map/ppermute | solution.py:28
  31.2 1.6 %collective-permute-start.7 = (bf16[16,3456]{1,0:T(8,128)(2,1)S(1)}, bf16[16,3456]{1,0:T(8,128)(2,1)S(1)}, u32[]{:S(2)}, u32[]{:S(2)}) collective-permute-start(bf16[16,3456]{1,0:T(8,128)(2,1)S(1)} %get-tuple-element.42), channel_id=1, source_target_pairs={{0,4},{1,5},{2,6},{3,7},{4,0},{5,1},{6,2},{7,3},{8,12},{9,13},{10,... | collective-permute-start | bytes 331784 | tf_op jit(solution)/shard_map/ppermute | solution.py:28
  33.4 1.5 %collective-permute-start.10 = (f32[26,128]{1,0:T(8,128)S(1)}, f32[26,128]{1,0:T(8,128)S(1)}, u32[]{:S(2)}, u32[]{:S(2)}) collective-permute-start(f32[26,128]{1,0:T(8,128)S(1)} %get-tuple-element.47.refs_7_), channel_id=1, source_target_pairs={{0,2},{1,3},{2,0},{3,1},{4,6},{5,7},{6,4},{7,5},{8,10},{9,11},{10,... | collective-permute-start | bytes 39944 | tf_op jit(solution)/shard_map/ppermute | solution.py:28
  35.4 2.4 %collective-permute-done.10.refs_9_ = f32[26,128]{1,0:T(8,128)S(1)} collective-permute-done((f32[26,128]{1,0:T(8,128)S(1)}, f32[26,128]{1,0:T(8,128)S(1)}, u32[]{:S(2)}, u32[]{:S(2)}) %collective-permute-start.10) | collective-permute-done | bytes 13344 | tf_op jit(solution)/shard_map/ppermute | solution.py:28
  38.9 2.7 %collective-permute-start.11 = (bf16[16,3456]{1,0:T(8,128)(2,1)S(1)}, bf16[16,3456]{1,0:T(8,128)(2,1)S(1)}, u32[]{:S(2)}, u32[]{:S(2)}) collective-permute-start(bf16[16,3456]{1,0:T(8,128)(2,1)S(1)} %get-tuple-element.49), channel_id=1, source_target_pairs={{0,8},{1,9},{2,10},{3,11},{4,12},{5,13},{6,14},{7,15},{8,0},{9,1},... | collective-permute-start | bytes 331784 | tf_op jit(solution)/shard_map/ppermute | solution.py:28
  42.0 4.5 %collective-permute-done.12.other_side_ref = f32[52,128]{1,0:T(8,128)S(1)} collective-permute-done((f32[52,128]{1,0:T(8,128)S(1)}, f32[52,128]{1,0:T(8,128)S(1)}, u32[]{:S(2)}, u32[]{:S(2)}) %collective-permute-start.12) | collective-permute-done | bytes 26656 | tf_op jit(solution)/shard_map/ppermute | solution.py:28
  46.6 4.1 %attend.1 = (bf16[16,3072]{1,0:T(8,128)(2,1)S(1)}, f32[8,512]{1,0:T(8,128)}) custom-call(s32[8]{0:T(128)S(1)} %copy-done.6, f32[16,3328]{1,0:T(8,128)S(1)} %get-tuple-element.48.keep_ref, bf16[16,3456]{1,0:T(8,128)(2,1)S(1)} %collective-permute-done.11.recv_ref, f32[16,128]{1,0:T(8,128)S(1)} %get-tuple-element.50.stats_ref, ...), custom_call_target="tpu_custom_call" | custom-call | tf_op jit(solution)/shard_map/attend/pallas_call | solution.py:343
  50.7 1.2 %collective-permute-start.13 = (bf16[16,3072]{1,0:T(8,128)(2,1)S(1)}, bf16[16,3072]{1,0:T(8,128)(2,1)S(1)}, u32[]{:S(2)}, u32[]{:S(2)}) collective-permute-start(bf16[16,3072]{1,0:T(8,128)(2,1)S(1)} %get-tuple-element.52), channel_id=1, source_target_pairs={{0,8},{1,9},{2,10},{3,11},{4,12},{5,13},{6,14},{7,15},{8,0},{9,1},... | collective-permute-start | bytes 294920 | tf_op jit(solution)/shard_map/ppermute | solution.py:28
  51.9 5.3 %collective-permute-done.13 = bf16[16,3072]{1,0:T(8,128)(2,1)S(1)} collective-permute-done((bf16[16,3072]{1,0:T(8,128)(2,1)S(1)}, bf16[16,3072]{1,0:T(8,128)(2,1)S(1)}, u32[]{:S(2)}, u32[]{:S(2)}) %collective-permute-start.13) | collective-permute-done | bytes 98336 | tf_op jit(solution)/shard_map/ppermute | solution.py:28
  57.8 4.2 %collective-permute-done.17 = bf16[16,3072]{1,0:T(8,128)(2,1)S(1)} collective-permute-done((bf16[16,3072]{1,0:T(8,128)(2,1)S(1)}, bf16[16,3072]{1,0:T(8,128)(2,1)S(1)}, u32[]{:S(2)}, u32[]{:S(2)}) %collective-permute-start.17) | collective-permute-done | bytes 98336 | tf_op jit(solution)/shard_map/ppermute | solution.py:28
  62.1 1.0 %collective-permute-start.18 = (bf16[32,3072]{1,0:T(8,128)(2,1)S(1)}, bf16[32,3072]{1,0:T(8,128)(2,1)S(1)}, u32[]{:S(2)}, u32[]{:S(2)}) collective-permute-start(bf16[32,3072]{1,0:T(8,128)(2,1)S(1)} %pad_maximum_fusion.3), channel_id=1, source_target_pairs={{0,4},{1,5},{2,6},{3,7},{4,0},{5,1},{6,2},{7,3},{8,12},{9,13},{10,... | collective-permute-start | bytes 589832 | tf_op jit(solution)/shard_map/ppermute | solution.py:28
  63.1 0.9 %collective-permute-start.15 = (bf16[32,3072]{1,0:T(8,128)(2,1)S(1)}, bf16[32,3072]{1,0:T(8,128)(2,1)S(1)}, u32[]{:S(2)}, u32[]{:S(2)}) collective-permute-start(bf16[32,3072]{1,0:T(8,128)(2,1)S(1)} %pad_maximum_fusion.2), channel_id=1, source_target_pairs={{0,2},{1,3},{2,0},{3,1},{4,6},{5,7},{6,4},{7,5},{8,10},{9,11},{10,... | collective-permute-start | bytes 589832 | tf_op jit(solution)/shard_map/ppermute | solution.py:28
  64.0 3.8 %collective-permute-done.18 = bf16[32,3072]{1,0:T(8,128)(2,1)S(1)} collective-permute-done((bf16[32,3072]{1,0:T(8,128)(2,1)S(1)}, bf16[32,3072]{1,0:T(8,128)(2,1)S(1)}, u32[]{:S(2)}, u32[]{:S(2)}) %collective-permute-start.18) | collective-permute-done | bytes 196640 | tf_op jit(solution)/shard_map/ppermute | solution.py:28
  67.9 0.9 %collective-permute-done.15 = bf16[32,3072]{1,0:T(8,128)(2,1)S(1)} collective-permute-done((bf16[32,3072]{1,0:T(8,128)(2,1)S(1)}, bf16[32,3072]{1,0:T(8,128)(2,1)S(1)}, u32[]{:S(2)}, u32[]{:S(2)}) %collective-permute-start.15) | collective-permute-done | bytes 196640 | tf_op jit(solution)/shard_map/ppermute | solution.py:28
  69.6 1.0 %collective-permute-done.16.a_other = bf16[64,3072]{1,0:T(8,128)(2,1)S(1)} collective-permute-done((bf16[64,3072]{1,0:T(8,128)(2,1)S(1)}, bf16[64,3072]{1,0:T(8,128)(2,1)S(1)}, u32[]{:S(2)}, u32[]{:S(2)}) %collective-permute-start.16) | collective-permute-done | bytes 393248 | tf_op jit(solution)/shard_map/ppermute | solution.py:28
  70.7 4.3 %output.1 = f32[128,1152]{1,0:T(8,128)} custom-call(s32[1]{0:T(128)} %bitcast.me_ref, bf16[64,3072]{1,0:T(8,128)(2,1)S(1)} %pad_maximum_fusion.a_own, bf16[64,3072]{1,0:T(8,128)(2,1)S(1)} %collective-permute-done.16.a_other, bf16[64,3072]{1,0:T(8,128)(2,1)S(1)} %pad_maximum_fusion.1.b_own, bf16[64,3072]{1,0:T(8,128)(2,1)S(1)} %collective-permute-done.19.b_other, ...), custom_call_target="tpu_custom_call" | custom-call | tf_op jit(solution)/shard_map/output/pallas_call | solution.py:397
  (60 shorter events, 7.0 us)
Async XLA Ops:
  8.6 62.1 %slice-start = ((s8[14155776]{0:T(1024)(128)(4,1)}), s8[1572864]{0:T(1024)(128)(4,1)S(1)}, s32[]{:S(2)}) async-start(s8[14155776]{0:T(1024)(128)(4,1)} %bitcast.1), calls=%async_computation | async-start | bytes 3145728
  8.6 62.1 %slice-start.1 = ((s8[14155776]{0:T(1024)(128)(4,1)}), s8[4194304]{0:T(1024)(128)(4,1)S(1)}, s32[]{:S(2)}) async-start(s8[14155776]{0:T(1024)(128)(4,1)} %bitcast.1), calls=%async_computation.1 | async-start | bytes 8388608
  8.6 62.1 %slice-start.2 = ((s8[14155776]{0:T(1024)(128)(4,1)}), s8[4194304]{0:T(1024)(128)(4,1)S(1)}, s32[]{:S(2)}) async-start(s8[14155776]{0:T(1024)(128)(4,1)} %bitcast.1), calls=%async_computation.2 | async-start | bytes 8388608
  17.4 2.6 %collective-permute-start = (bf16[64,6656]{1,0:T(8,128)(2,1)S(1)}, bf16[64,6656]{1,0:T(8,128)(2,1)S(1)}, u32[]{:S(2)}, u32[]{:S(2)}) collective-permute-start(bf16[64,6656]{1,0:T(8,128)(2,1)S(1)} %get-tuple-element.29), channel_id=1, source_target_pairs={{0,1},{1,0},{2,3},{3,2},{4,5},{5,4},{6,7},{7,6},{8,9},{9,8},{10,11... | collective-permute-start | bytes 2555912 | tf_op jit(solution)/shard_map/ppermute | solution.py:28
  17.9 2.1 %collective-permute-start.1 = (f32[64,128]{1,0:T(8,128)S(1)}, f32[64,128]{1,0:T(8,128)S(1)}, u32[]{:S(2)}, u32[]{:S(2)}) collective-permute-start(f32[64,128]{1,0:T(8,128)S(1)} %slice.15), channel_id=1, source_target_pairs={{0,1},{1,0},{2,3},{3,2},{4,5},{5,4},{6,7},{7,6},{8,9},{9,8},{10,11... | collective-permute-start | bytes 98312 | tf_op jit(solution)/shard_map/ppermute | solution.py:28
  18.0 2.0 %collective-permute-start.2 = (f32[52,128]{1,0:T(8,128)S(1)}, f32[52,128]{1,0:T(8,128)S(1)}, u32[]{:S(2)}, u32[]{:S(2)}) collective-permute-start(f32[52,128]{1,0:T(8,128)S(1)} %get-tuple-element.31.side_ref), channel_id=1, source_target_pairs={{0,1},{1,0},{2,3},{3,2},{4,5},{5,4},{6,7},{7,6},{8,9},{9,8},{10,11... | collective-permute-start | bytes 79880 | tf_op jit(solution)/shard_map/ppermute | solution.py:28
  20.0 26.5 %copy-start.2 = (bf16[8,512,256]{2,1,0:T(8,128)(2,1)S(1)}, bf16[8,512,256]{2,1,0:T(8,128)(2,1)}, u32[]{:S(2)}) copy-start(bf16[8,512,256]{2,1,0:T(8,128)(2,1)} %value_ref.1) | copy-start | bytes 6291460
  20.4 10.5 %collective-permute-start.3 = (bf16[32,3456]{1,0:T(8,128)(2,1)S(1)}, bf16[32,3456]{1,0:T(8,128)(2,1)S(1)}, u32[]{:S(2)}, u32[]{:S(2)}) collective-permute-start(bf16[32,3456]{1,0:T(8,128)(2,1)S(1)} %get-tuple-element.34), channel_id=1, source_target_pairs={{0,2},{1,3},{2,0},{3,1},{4,6},{5,7},{6,4},{7,5},{8,10},{9,11},{10,... | collective-permute-start | bytes 663560 | tf_op jit(solution)/shard_map/ppermute | solution.py:28
  23.3 7.5 %collective-permute-start.4 = (bf16[32,3456]{1,0:T(8,128)(2,1)S(1)}, bf16[32,3456]{1,0:T(8,128)(2,1)S(1)}, u32[]{:S(2)}, u32[]{:S(2)}) collective-permute-start(bf16[32,3456]{1,0:T(8,128)(2,1)S(1)} %get-tuple-element.35), channel_id=1, source_target_pairs={{0,4},{1,5},{2,6},{3,7},{4,0},{5,1},{6,2},{7,3},{8,12},{9,13},{10,... | collective-permute-start | bytes 663560 | tf_op jit(solution)/shard_map/ppermute | solution.py:28
  24.9 4.5 %collective-permute-start.5 = (f32[26,128]{1,0:T(8,128)S(1)}, f32[26,128]{1,0:T(8,128)S(1)}, u32[]{:S(2)}, u32[]{:S(2)}) collective-permute-start(f32[26,128]{1,0:T(8,128)S(1)} %get-tuple-element.38.refs_6_), channel_id=1, source_target_pairs={{0,2},{1,3},{2,0},{3,1},{4,6},{5,7},{6,4},{7,5},{8,10},{9,11},{10,... | collective-permute-start | bytes 39944 | tf_op jit(solution)/shard_map/ppermute | solution.py:28
  25.4 5.4 %collective-permute-start.6 = (f32[26,128]{1,0:T(8,128)S(1)}, f32[26,128]{1,0:T(8,128)S(1)}, u32[]{:S(2)}, u32[]{:S(2)}) collective-permute-start(f32[26,128]{1,0:T(8,128)S(1)} %get-tuple-element.39.refs_7_), channel_id=1, source_target_pairs={{0,4},{1,5},{2,6},{3,7},{4,0},{5,1},{6,2},{7,3},{8,12},{9,13},{10,... | collective-permute-start | bytes 39944 | tf_op jit(solution)/shard_map/ppermute | solution.py:28
  31.2 7.4 %collective-permute-start.7 = (bf16[16,3456]{1,0:T(8,128)(2,1)S(1)}, bf16[16,3456]{1,0:T(8,128)(2,1)S(1)}, u32[]{:S(2)}, u32[]{:S(2)}) collective-permute-start(bf16[16,3456]{1,0:T(8,128)(2,1)S(1)} %get-tuple-element.42), channel_id=1, source_target_pairs={{0,4},{1,5},{2,6},{3,7},{4,0},{5,1},{6,2},{7,3},{8,12},{9,13},{10,... | collective-permute-start | bytes 331784 | tf_op jit(solution)/shard_map/ppermute | solution.py:28
  32.9 5.8 %collective-permute-start.8 = (bf16[16,3456]{1,0:T(8,128)(2,1)S(1)}, bf16[16,3456]{1,0:T(8,128)(2,1)S(1)}, u32[]{:S(2)}, u32[]{:S(2)}) collective-permute-start(bf16[16,3456]{1,0:T(8,128)(2,1)S(1)} %get-tuple-element.43), channel_id=1, source_target_pairs={{0,2},{1,3},{2,0},{3,1},{4,6},{5,7},{6,4},{7,5},{8,10},{9,11},{10,... | collective-permute-start | bytes 331784 | tf_op jit(solution)/shard_map/ppermute | solution.py:28
  33.4 4.4 %collective-permute-start.10 = (f32[26,128]{1,0:T(8,128)S(1)}, f32[26,128]{1,0:T(8,128)S(1)}, u32[]{:S(2)}, u32[]{:S(2)}) collective-permute-start(f32[26,128]{1,0:T(8,128)S(1)} %get-tuple-element.47.refs_7_), channel_id=1, source_target_pairs={{0,2},{1,3},{2,0},{3,1},{4,6},{5,7},{6,4},{7,5},{8,10},{9,11},{10,... | collective-permute-start | bytes 39944 | tf_op jit(solution)/shard_map/ppermute | solution.py:28
  34.9 3.7 %collective-permute-start.9 = (f32[26,128]{1,0:T(8,128)S(1)}, f32[26,128]{1,0:T(8,128)S(1)}, u32[]{:S(2)}, u32[]{:S(2)}) collective-permute-start(f32[26,128]{1,0:T(8,128)S(1)} %get-tuple-element.46.refs_6_), channel_id=1, source_target_pairs={{0,4},{1,5},{2,6},{3,7},{4,0},{5,1},{6,2},{7,3},{8,12},{9,13},{10,... | collective-permute-start | bytes 39944 | tf_op jit(solution)/shard_map/ppermute | solution.py:28
  38.9 7.6 %collective-permute-start.11 = (bf16[16,3456]{1,0:T(8,128)(2,1)S(1)}, bf16[16,3456]{1,0:T(8,128)(2,1)S(1)}, u32[]{:S(2)}, u32[]{:S(2)}) collective-permute-start(bf16[16,3456]{1,0:T(8,128)(2,1)S(1)} %get-tuple-element.49), channel_id=1, source_target_pairs={{0,8},{1,9},{2,10},{3,11},{4,12},{5,13},{6,14},{7,15},{8,0},{9,1},... | collective-permute-start | bytes 331784 | tf_op jit(solution)/shard_map/ppermute | solution.py:28
  41.6 4.9 %collective-permute-start.12 = (f32[52,128]{1,0:T(8,128)S(1)}, f32[52,128]{1,0:T(8,128)S(1)}, u32[]{:S(2)}, u32[]{:S(2)}) collective-permute-start(f32[52,128]{1,0:T(8,128)S(1)} %get-tuple-element.51.side_ref), channel_id=1, source_target_pairs={{0,8},{1,9},{2,10},{3,11},{4,12},{5,13},{6,14},{7,15},{8,0},{9,1},... | collective-permute-start | bytes 79880 | tf_op jit(solution)/shard_map/ppermute | solution.py:28
  50.7 6.5 %collective-permute-start.13 = (bf16[16,3072]{1,0:T(8,128)(2,1)S(1)}, bf16[16,3072]{1,0:T(8,128)(2,1)S(1)}, u32[]{:S(2)}, u32[]{:S(2)}) collective-permute-start(bf16[16,3072]{1,0:T(8,128)(2,1)S(1)} %get-tuple-element.52), channel_id=1, source_target_pairs={{0,8},{1,9},{2,10},{3,11},{4,12},{5,13},{6,14},{7,15},{8,0},{9,1},... | collective-permute-start | bytes 294920 | tf_op jit(solution)/shard_map/ppermute | solution.py:28
  57.2 4.9 %collective-permute-start.17 = (bf16[16,3072]{1,0:T(8,128)(2,1)S(1)}, bf16[16,3072]{1,0:T(8,128)(2,1)S(1)}, u32[]{:S(2)}, u32[]{:S(2)}) collective-permute-start(bf16[16,3072]{1,0:T(8,128)(2,1)S(1)} %pad_maximum_fusion.5), channel_id=1, source_target_pairs={{0,2},{1,3},{2,0},{3,1},{4,6},{5,7},{6,4},{7,5},{8,10},{9,11},{10,... | collective-permute-start | bytes 294920 | tf_op jit(solution)/shard_map/ppermute | solution.py:28
  57.7 5.4 %collective-permute-start.14 = (bf16[16,3072]{1,0:T(8,128)(2,1)S(1)}, bf16[16,3072]{1,0:T(8,128)(2,1)S(1)}, u32[]{:S(2)}, u32[]{:S(2)}) collective-permute-start(bf16[16,3072]{1,0:T(8,128)(2,1)S(1)} %pad_maximum_fusion.4), channel_id=1, source_target_pairs={{0,4},{1,5},{2,6},{3,7},{4,0},{5,1},{6,2},{7,3},{8,12},{9,13},{10,... | collective-permute-start | bytes 294920 | tf_op jit(solution)/shard_map/ppermute | solution.py:28
  62.1 5.7 %collective-permute-start.18 = (bf16[32,3072]{1,0:T(8,128)(2,1)S(1)}, bf16[32,3072]{1,0:T(8,128)(2,1)S(1)}, u32[]{:S(2)}, u32[]{:S(2)}) collective-permute-start(bf16[32,3072]{1,0:T(8,128)(2,1)S(1)} %pad_maximum_fusion.3), channel_id=1, source_target_pairs={{0,4},{1,5},{2,6},{3,7},{4,0},{5,1},{6,2},{7,3},{8,12},{9,13},{10,... | collective-permute-start | bytes 589832 | tf_op jit(solution)/shard_map/ppermute | solution.py:28
  63.1 5.7 %collective-permute-start.15 = (bf16[32,3072]{1,0:T(8,128)(2,1)S(1)}, bf16[32,3072]{1,0:T(8,128)(2,1)S(1)}, u32[]{:S(2)}, u32[]{:S(2)}) collective-permute-start(bf16[32,3072]{1,0:T(8,128)(2,1)S(1)} %pad_maximum_fusion.2), channel_id=1, source_target_pairs={{0,2},{1,3},{2,0},{3,1},{4,6},{5,7},{6,4},{7,5},{8,10},{9,11},{10,... | collective-permute-start | bytes 589832 | tf_op jit(solution)/shard_map/ppermute | solution.py:28
  67.8 1.8 %collective-permute-start.19 = (bf16[64,3072]{1,0:T(8,128)(2,1)S(1)}, bf16[64,3072]{1,0:T(8,128)(2,1)S(1)}, u32[]{:S(2)}, u32[]{:S(2)}) collective-permute-start(bf16[64,3072]{1,0:T(8,128)(2,1)S(1)} %pad_maximum_fusion.1.b_own), channel_id=1, source_target_pairs={{0,1},{1,0},{2,3},{3,2},{4,5},{5,4},{6,7},{7,6},{8,9},{9,8},{10,11... | collective-permute-start | bytes 1179656 | tf_op jit(solution)/shard_map/ppermute | solution.py:28
  68.9 1.8 %collective-permute-start.16 = (bf16[64,3072]{1,0:T(8,128)(2,1)S(1)}, bf16[64,3072]{1,0:T(8,128)(2,1)S(1)}, u32[]{:S(2)}, u32[]{:S(2)}) collective-permute-start(bf16[64,3072]{1,0:T(8,128)(2,1)S(1)} %pad_maximum_fusion.a_own), channel_id=1, source_target_pairs={{0,1},{1,0},{2,3},{3,2},{4,5},{5,4},{6,7},{7,6},{8,9},{9,8},{10,11... | collective-permute-start | bytes 1179656 | tf_op jit(solution)/shard_map/ppermute | solution.py:28
  (8 other events, 121.8 us)

commit v2 on v0

v2 whole, which is shorter than its diff:
```python
import functools
import math

import jax
import jax.numpy as jnp
from jax import lax
from jax.experimental import pallas as pl
from jax.experimental.pallas import tpu as pltpu
from jax.sharding import PartitionSpec as P

HD = 256
LANES = 128
BLOCK = 8
TILE = 512
SIDE = 32
AHEAD = 3
PACE = 2
QUAD = 4
EPSILON = 1e-05
VMEM = pl.BlockSpec(memory_space=pltpu.VMEM)
SMEM = pl.BlockSpec(memory_space=pltpu.SMEM)


def rope_tables(position_rows):
    half_width = HD // 2
    inverse_freq = 10000.0 ** (-(jnp.arange(half_width, dtype=jnp.float32) * 2.0 / HD))
    angles = position_rows.astype(jnp.float32)[:, None] * inverse_freq[None, :]
    return (jnp.cos(angles), jnp.sin(angles))


def exchange(value, mask, count):
    return lax.ppermute(value, "gx", [(i, i ^ mask) for i in range(count)])


def in_hbm(value):
    return pltpu.with_memory_space_constraint(value, pltpu.HBM)


def struct(shape, dtype):
    return jax.ShapeDtypeStruct(shape, dtype)


def lane_ids(rows):
    return lax.broadcasted_iota(jnp.int32, (rows, LANES), 1)


def pack_stats(stats):
    high = stats.astype(jnp.bfloat16).astype(jnp.float32)
    middle = (stats - high).astype(jnp.bfloat16).astype(jnp.float32)
    low = stats - high - middle
    lane = lane_ids(stats.shape[0])
    return jnp.where(lane < 2, high, jnp.where(lane < 4, middle, low)).astype(jnp.bfloat16)


def unpack_stats(packed):
    parts = packed.astype(jnp.float32)
    mean = parts[:, 0:1] + parts[:, 2:3] + parts[:, 4:5]
    square = parts[:, 1:2] + parts[:, 3:4] + parts[:, 5:6]
    return jnp.where(lane_ids(parts.shape[0]) % 2 == 0, mean, square)


def pack_side(side):
    pieces = []
    for start in range(0, SIDE, BLOCK):
        pieces.append(
            jnp.concatenate(
                [side[start : start + BLOCK], side[SIDE + start : SIDE + start + BLOCK]], axis=0
            )
        )
    return jnp.concatenate(pieces, axis=1)


def folded_row(packed, c):
    part = packed[:, c // BLOCK * LANES : (c // BLOCK + 1) * LANES]
    k = c % BLOCK
    upper = lax.broadcasted_iota(jnp.int32, (2 * BLOCK, LANES), 0) >= BLOCK
    return jnp.where(upper, part[BLOCK + k : BLOCK + k + 1], part[k : k + 1])


def merge_stats(parts):
    merged = sum(parts[1:], parts[0]) * (1.0 / len(parts))
    return merged, [p[:, 0:1] - merged[:, 0:1] for p in parts]


def project_kernel(order, me_ref, x_hbm, gain_hbm, wq_hbm, wkv_hbm, keep_ref, send_ref, stats_ref,
                   extra_ref, x_ref, gain_ref, rows_ref, lhs_ref, w_ref, in_sem, w_sem):
    total = x_ref.shape[0]
    half = total // 2
    me = me_ref[0]
    tiles = w_ref.shape[0]
    x_copy = pltpu.make_async_copy(x_hbm, x_ref, in_sem.at[0])
    gain_copy = pltpu.make_async_copy(gain_hbm, gain_ref, in_sem.at[1])
    x_copy.start()
    gain_copy.start()
    copies = []
    for t in range(tiles):
        source = wkv_hbm if t == 0 else wq_hbm.at[:, (t - 1) * TILE : t * TILE]
        copies.append(pltpu.make_async_copy(source, w_ref.at[t], w_sem.at[t]))
    x_copy.wait()
    gain_copy.wait()
    started = min(AHEAD, tiles)
    for t in range(started):
        copies[t].start()
    rows_ref[...] = x_ref[...].astype(jnp.float32)
    gain = gain_ref[...].reshape(1, gain_ref.shape[0])
    high = gain.astype(jnp.bfloat16).astype(jnp.float32)
    low = gain - high
    row = lax.broadcasted_iota(jnp.int32, (16, gain.shape[1]), 0)
    lhs_ref[total:, :] = jnp.where(
        row == 0, high, jnp.where(row == 1, low, 0.0)
    ).astype(jnp.bfloat16)
    lane = lane_ids(2 * BLOCK)
    extra_ref[half:, :] = jnp.zeros((2 * SIDE, LANES), jnp.float32)
    for pair in range(len(order) // 2):
        pieces = []
        for b in order[2 * pair : 2 * pair + 2]:
            start = pl.multiple_of((me ^ b) * BLOCK, BLOCK)
            pieces.append(rows_ref[pl.ds(start, BLOCK), :])
        x = jnp.concatenate(pieces, axis=0)
        mean = jnp.mean(x, axis=1, keepdims=True)
        square = jnp.mean(x * x, axis=1, keepdims=True)
        at = pair * 2 * BLOCK
        lhs_ref[at : at + 2 * BLOCK, :] = ((x - mean) * gain).astype(jnp.bfloat16)
        if started < tiles - 1 and pair % PACE == PACE - 1:
            copies[started].start()
            started += 1
        stats = jnp.where(lane % 2 == 0, mean, square)
        if at < half:
            stats_ref[at : at + 2 * BLOCK, :] = stats
        else:
            extra_ref[at - half : at - half + 2 * BLOCK, :] = stats

    chunks = tiles * (TILE // LANES) // 2
    for t in range(tiles):
        while started < min(tiles, t + AHEAD + 4):
            copies[started].start()
            started += 1
        copies[t].wait()
        out = jnp.dot(lhs_ref[...], w_ref[t], preferred_element_type=jnp.float32)
        columns = slice(t * TILE, (t + 1) * TILE)
        keep_ref[:, columns] = out[:half]
        send_ref[:, columns] = out[half:total].astype(jnp.bfloat16)
        gained = out[total : total + 1] + out[total + 1 : total + 2]
        for k in range(TILE // LANES):
            c = t * (TILE // LANES) + k
            at = half + c if c < chunks else half + SIDE + c - chunks
            extra_ref[at : at + 1, :] = gained[:, k * LANES : (k + 1) * LANES]


def project(me, order, residual, gain, w_query, w_keyval):
    total, depth = residual.shape
    width = w_query.shape[1] + w_keyval.shape[1]
    half = total // 2
    tiles = width // TILE
    return pl.pallas_call(
        functools.partial(project_kernel, order),
        in_specs=[SMEM] + [pl.BlockSpec(memory_space=pltpu.HBM)] * 4,
        out_specs=[VMEM] * 4,
        out_shape=[
            struct((half, width), jnp.float32),
            struct((half, width), jnp.bfloat16),
            struct((half, LANES), jnp.float32),
            struct((half + 2 * SIDE, LANES), jnp.float32),
        ],
        scratch_shapes=[
            pltpu.VMEM((total, depth), jnp.bfloat16),
            pltpu.VMEM((depth,), jnp.float32),
            pltpu.VMEM((total, depth), jnp.float32),
            pltpu.VMEM((total + 16, depth), jnp.bfloat16),
            pltpu.VMEM((tiles, depth, TILE), jnp.bfloat16),
            pltpu.SemaphoreType.DMA((2,)),
            pltpu.SemaphoreType.DMA((tiles,)),
        ],
        compiler_params=pltpu.CompilerParams(vmem_limit_bytes=24 * 2**20),
        name="project",
    )(me, *(in_hbm(v) for v in (residual, gain, w_query, w_keyval)))


def first_kernel(keep_ref, recv_ref, stats_ref, extra_ref, other_ref,
                 own_ref, far_ref, own_stats, far_stats, side_ref, *send_refs):
    half, width = keep_ref.shape
    cut = width // 2
    chunks = cut // LANES
    early, late = send_refs[: QUAD - 1], send_refs[QUAD - 1 :]
    own = stats_ref[...]
    other = other_ref[:half, :]
    merged = 0.5 * (own + other)
    shift = 0.5 * (own[:, 0:1] - other[:, 0:1])
    side = extra_ref[half:, :] + other_ref[half:, :]
    change = extra_ref[half:, :] - other_ref[half:, :]
    side_ref[...] = side
    packed_side = pack_side(side).astype(jnp.bfloat16)
    fold = 2 * BLOCK

    def target(k):
        group, q = divmod(k, QUAD)
        return group, q, slice((group - 1) * fold, group * fold)

    for k in range(half // BLOCK):
        group, q, at = target(k)
        stats = merged[k * BLOCK : (k + 1) * BLOCK]
        stats = jnp.concatenate([stats, stats], axis=0)
        if q == 0:
            if group == 0:
                own_stats[...] = stats
            else:
                far_stats[at, :] = stats
        elif group == 0:
            late[q - 1][:, cut:] = pack_stats(stats)
        else:
            early[q - 1][at, cut : cut + LANES] = pack_stats(stats)
            early[q - 1][at, cut + LANES :] = packed_side
    for c in range(chunks):
        columns = slice(c * LANES, (c + 1) * LANES)
        totals = []
        for n in range(2):
            source = slice(n * cut + c * LANES, n * cut + (c + 1) * LANES)
            row = n * SIDE + c
            totals.append(
                keep_ref[:, source]
                + recv_ref[:, source].astype(jnp.float32)
                + shift * change[row : row + 1]
            )
        for k in range(half // BLOCK):
            group, q, at = target(k)
            value = jnp.concatenate([t[k * BLOCK : (k + 1) * BLOCK] for t in totals], axis=0)
            if q == 0:
                if group == 0:
                    own_ref[:, columns] = value
                else:
                    far_ref[at, columns] = value
            elif group == 0:
                late[q - 1][:, columns] = value.astype(jnp.bfloat16)
            else:
                early[q - 1][at, columns] = value.astype(jnp.bfloat16)


def first_combine(keep, recv, stats, extra, other):
    half, width = keep.shape
    cut = width // 2
    fold = 2 * BLOCK
    groups = half // (QUAD * BLOCK)
    far = (groups - 1) * fold
    return pl.pallas_call(
        first_kernel,
        in_specs=[VMEM] * 5,
        out_specs=[VMEM] * (5 + 2 * (QUAD - 1)),
        out_shape=[
            struct((fold, cut), jnp.float32),
            struct((far, cut), jnp.float32),
            struct((fold, LANES), jnp.float32),
            struct((far, LANES), jnp.float32),
            struct((2 * SIDE, LANES), jnp.float32),
        ]
        + [struct((far, cut + LANES + SIDE // BLOCK * LANES), jnp.bfloat16)] * (QUAD - 1)
        + [struct((fold, cut + LANES), jnp.bfloat16)] * (QUAD - 1),
        compiler_params=pltpu.CompilerParams(vmem_limit_bytes=16 * 2**20),
        name="first_combine",
    )(keep, recv, stats, extra, other)


def far_kernel(far_ref, stats_ref, side_ref, *refs):
    recv, outs = refs[: QUAD - 1], refs[QUAD:]
    cut = far_ref.shape[1]
    fold = 2 * BLOCK
    packed = [r[:fold, cut + LANES :].astype(jnp.float32) for r in recv]
    packed = [pack_side(side_ref[...])] + packed
    summed = sum(packed[1:], packed[0])
    outs[0][...] = summed
    for g, out in enumerate(outs[1:]):
        at = slice(g * fold, (g + 1) * fold)
        parts = [stats_ref[at, :]] + [unpack_stats(r[at, cut : cut + LANES]) for r in recv]
        merged, shifts = merge_stats(parts)
        out[:, cut : cut + LANES] = pack_stats(merged)
        out[:, cut + LANES :] = summed.astype(jnp.bfloat16)
        for c in range(cut // LANES):
            columns = slice(c * LANES, (c + 1) * LANES)
            total = far_ref[at, columns]
            for r in recv:
                total = total + r[at, columns].astype(jnp.float32)
            for shift, side in zip(shifts, packed):
                total = total + shift * folded_row(side, c)
            out[:, columns] = total.astype(jnp.bfloat16)


def far_combine(far, stats, side, recv, after):
    cut = far.shape[1]
    fold = 2 * BLOCK
    groups = far.shape[0] // fold
    side_columns = SIDE // BLOCK * LANES
    return pl.pallas_call(
        far_kernel,
        in_specs=[VMEM] * (3 + QUAD - 1) + [pl.BlockSpec(memory_space=pl.ANY)],
        out_specs=[VMEM] * (1 + groups),
        out_shape=[struct((fold, side_columns), jnp.float32)]
        + [struct((fold, cut + LANES + side_columns), jnp.bfloat16)] * groups,
        compiler_params=pltpu.CompilerParams(vmem_limit_bytes=16 * 2**20),
        name="far_combine",
    )(far, stats, side, *recv, after)


def two_part_dot(left, right, dims):
    rows = left.shape[0]
    high = left.astype(jnp.bfloat16)
    low = (left - high.astype(jnp.float32)).astype(jnp.bfloat16)
    both = jnp.concatenate([high.astype(jnp.float32), low.astype(jnp.float32)], axis=0)
    out = lax.dot_general(
        both.astype(jnp.bfloat16), right, dims, preferred_element_type=jnp.float32
    )
    return out[:rows] + out[rows:]


def attend_kernel(heads, length_ref, own_ref, stats_ref, side_ref, summed_ref, cos_ref, sin_ref,
                  key_ref, value_ref, *refs):
    early, late = refs[: QUAD - 1], refs[QUAD - 1 : 2 * QUAD - 2]
    far, (attended_ref, keyval_ref, q_ref, out_ref) = refs[2 * QUAD - 2 : -4], refs[-4:]
    cut = own_ref.shape[1]
    chunks = cut // LANES
    slots = key_ref.shape[1]
    fold = 2 * BLOCK
    parts = [stats_ref[...]] + [unpack_stats(r[:, cut:]) for r in late]
    merged, near_shifts = merge_stats(parts)
    packed = [pack_side(side_ref[...])]
    packed += [r[:fold, cut + LANES :].astype(jnp.float32) for r in early]
    parts = [merged] + [unpack_stats(r[:, cut : cut + LANES]) for r in far]
    merged, far_shifts = merge_stats(parts)
    packed += [summed_ref[...]] + [r[:, cut + LANES :].astype(jnp.float32) for r in far]
    shifts = near_shifts + far_shifts
    mean, square = merged[:, 0:1], merged[:, 1:2]
    scale = lax.rsqrt(square - mean * mean + EPSILON)
    cosine, sine = cos_ref[...], sin_ref[...]
    new_key = new_value = None
    for c in range(0, chunks, 2):
        pair = []
        for d in (c, c + 1):
            columns = slice(d * LANES, (d + 1) * LANES)
            total = own_ref[:, columns]
            for r in (*late, *far):
                total = total + r[:, columns].astype(jnp.float32)
            for shift, side in zip(shifts, packed):
                total = total + shift * folded_row(side, d)
            pair.append(total * scale)
        for half in range(2):
            u1, u2 = (v[half * BLOCK : (half + 1) * BLOCK] for v in pair)
            number = half * (chunks // 2) + c // 2 - 2
            if number == -1:
                new_value = jnp.concatenate([u1, u2], axis=1)
                continue
            turned = (u1 * cosine - u2 * sine, u2 * cosine + u1 * sine)
            if number == -2:
                new_key = jnp.concatenate(turned, axis=1)
            else:
                for k in range(2):
                    q_ref[k, number * BLOCK : (number + 1) * BLOCK, :] = turned[k]
    keyval_ref[:, :HD] = new_key
    keyval_ref[:, HD:] = new_value
    factor = 1.0 / math.sqrt(HD)
    slot = lax.broadcasted_iota(jnp.int32, (heads, slots), 1)
    key_rounded = new_key.astype(jnp.bfloat16).astype(jnp.float32)
    value_rounded = new_value.astype(jnp.bfloat16).astype(jnp.float32)
    requests = range(BLOCK)
    queries = [
        jnp.concatenate(
            [q_ref.at[k][pl.ds(r, heads, stride=BLOCK), :] for k in range(2)], axis=1
        )
        for r in requests
    ]
    scores = [
        two_part_dot(queries[r], key_ref[r], (((1,), (1,)), ((), ()))) for r in requests
    ]
    own_scores = [
        jnp.sum(queries[r] * key_rounded[r : r + 1], axis=1, keepdims=True)
        * factor
        for r in requests
    ]
    masked = [jnp.where(slot < length_ref[r], scores[r] * factor, -jnp.inf) for r in requests]
    highest = [
        jnp.maximum(jnp.max(masked[r], axis=1, keepdims=True), own_scores[r]) for r in requests
    ]
    exps = [jnp.exp(masked[r] - highest[r]) for r in requests]
    own_exps = [jnp.exp(own_scores[r] - highest[r]) for r in requests]
    inverse = [
        1.0 / (jnp.sum(exps[r], axis=1, keepdims=True) + own_exps[r]) for r in requests
    ]
    mixed = [
        two_part_dot(exps[r], value_ref[r], (((1,), (0,)), ((), ()))) * inverse[r] for r in requests
    ]
    for r in requests:
        own_weight = own_exps[r] * inverse[r]
        result = mixed[r] + own_weight * value_rounded[r : r + 1]
        for k in range(2):
            out_ref.at[k][pl.ds(r, heads, stride=BLOCK), :] = result[:, k * LANES : (k + 1) * LANES]
    for h in range(heads // 2):
        upper_head = h + heads // 2
        for k in range(2):
            at = h * HD + k * LANES
            attended_ref[:, at : at + LANES] = jnp.concatenate(
                [out_ref[k, g * BLOCK : (g + 1) * BLOCK, :] for g in (h, upper_head)], axis=0
            ).astype(jnp.bfloat16)


def attend(lengths, own, stats, side, summed, tables, key_cache, value_cache, early, late, far,
           heads):
    return pl.pallas_call(
        functools.partial(attend_kernel, heads),
        in_specs=[SMEM] + [VMEM] * (8 + len(early) + len(late) + len(far)),
        out_specs=[VMEM] * 2,
        out_shape=[
            struct((2 * BLOCK, heads * HD // 2), jnp.bfloat16),
            struct((BLOCK, 2 * HD), jnp.float32),
        ],
        scratch_shapes=[
            pltpu.VMEM((2, heads * BLOCK, LANES), jnp.float32),
            pltpu.VMEM((2, heads * BLOCK, LANES), jnp.float32),
        ],
        compiler_params=pltpu.CompilerParams(vmem_limit_bytes=24 * 2**20),
        name="attend",
    )(
        lengths, own, stats, side, summed, *tables, key_cache, value_cache, *early, *late, *far
    )


def load_kernel(w_hbm, after_ref, out_ref, token_ref, sems):
    parts = sems.shape[0]
    rows = w_hbm.shape[0] // parts
    copies = [
        pltpu.make_async_copy(
            w_hbm.at[k * rows : (k + 1) * rows, :], out_ref.at[k * rows : (k + 1) * rows, :], sems.at[k]
        )
        for k in range(parts)
    ]
    for copy in copies:
        copy.start()
    for copy in copies:
        copy.wait()
    token_ref[...] = jnp.zeros_like(token_ref)


def load(w_output, after):
    return pl.pallas_call(
        load_kernel,
        in_specs=[pl.BlockSpec(memory_space=pltpu.HBM), pl.BlockSpec(memory_space=pl.ANY)],
        out_specs=[VMEM] * 2,
        out_shape=[struct(w_output.shape, w_output.dtype), struct((BLOCK, LANES), jnp.float32)],
        scratch_shapes=[pltpu.SemaphoreType.DMA((8,))],
        compiler_params=pltpu.CompilerParams(vmem_limit_bytes=16 * 2**20),
        cost_estimate=pl.CostEstimate(
            flops=0, bytes_accessed=2 * w_output.size, transcendentals=0
        ),
        name="load",
    )(in_hbm(w_output), after)


def unfold(lhs_ref, pieces):
    cut = pieces[0].shape[1]
    for k in range(0, len(pieces), 2):
        pair = [p[...].astype(jnp.float32) for p in pieces[k : k + 2]]
        at = slice(k * BLOCK, (k + 2) * BLOCK)
        lhs_ref[at, :cut] = jnp.concatenate([p[:BLOCK] for p in pair], axis=0).astype(jnp.bfloat16)
        lhs_ref[at, cut:] = jnp.concatenate([p[BLOCK:] for p in pair], axis=0).astype(jnp.bfloat16)


def near_output_kernel(w_ref, *refs):
    pieces, (out_ref, lhs_ref) = refs[:-2], refs[-2:]
    unfold(lhs_ref, pieces)
    out_ref[...] = jnp.dot(lhs_ref[...], w_ref[...], preferred_element_type=jnp.float32)


def near_output(pieces, w_output):
    rows = len(pieces) * BLOCK
    depth, width = w_output.shape
    return pl.pallas_call(
        near_output_kernel,
        in_specs=[VMEM] * (1 + len(pieces)),
        out_specs=VMEM,
        out_shape=struct((rows, width), jnp.float32),
        scratch_shapes=[pltpu.VMEM((rows, depth), jnp.bfloat16)],
        compiler_params=pltpu.CompilerParams(vmem_limit_bytes=24 * 2**20),
        cost_estimate=pl.CostEstimate(
            flops=2 * rows * depth * width, bytes_accessed=4 * 2**20, transcendentals=0
        ),
        name="near_output",
    )(w_output, *pieces)


def far_output_kernel(near_order, far_order, me_ref, near_ref, x_ref, w_ref, *refs):
    pieces, (out_ref, lhs_ref, rows_ref, sum_ref) = refs[:-4], refs[-4:]
    me = me_ref[0]
    rows_ref[...] = x_ref[...].astype(jnp.float32)
    for p, b in enumerate(near_order):
        at = pl.ds(pl.multiple_of((me ^ b) * BLOCK, BLOCK), BLOCK)
        out_ref[at, :] = rows_ref[at, :] + near_ref[p * BLOCK : (p + 1) * BLOCK, :]
    unfold(lhs_ref, pieces)
    sum_ref[...] = jnp.dot(lhs_ref[...], w_ref[...], preferred_element_type=jnp.float32)
    for p, b in enumerate(far_order):
        at = pl.ds(pl.multiple_of((me ^ b) * BLOCK, BLOCK), BLOCK)
        out_ref[at, :] = rows_ref[at, :] + sum_ref[p * BLOCK : (p + 1) * BLOCK, :]


def far_output(me, orders, near, pieces, residual, w_output):
    total, width = residual.shape
    rows = len(pieces) * BLOCK
    return pl.pallas_call(
        functools.partial(far_output_kernel, *orders),
        in_specs=[SMEM] + [VMEM] * (3 + len(pieces)),
        out_specs=VMEM,
        out_shape=struct((total, width), jnp.float32),
        scratch_shapes=[
            pltpu.VMEM((rows, w_output.shape[0]), jnp.bfloat16),
            pltpu.VMEM((total, width), jnp.float32),
            pltpu.VMEM((rows, width), jnp.float32),
        ],
        compiler_params=pltpu.CompilerParams(vmem_limit_bytes=24 * 2**20),
        name="far_output",
    )(me, near, residual, w_output, *pieces)


def local(
    residual, norm_gain, w_query, w_keyval, w_output, key_cache, value_cache, lengths, positions
):
    count = lax.axis_size("gx")
    me = lax.axis_index("gx").astype(jnp.int32).reshape(1)
    heads = w_query.shape[1] // HD
    groups = count // (2 * QUAD)
    quad_masks = [2 * q for q in range(1, QUAD)]
    far_masks = [2 * QUAD * g for g in range(1, groups)]
    order = [
        core + 2 * q + 2 * QUAD * g for core in range(2) for g in range(groups) for q in range(QUAD)
    ]
    tables = rope_tables(positions)

    keep, send, stats, extra = project(me, order, residual, norm_gain, w_query, w_keyval)
    recv = exchange(send, 1, count)
    other = exchange(extra, 1, count)
    own, far, own_stats, far_stats, side, *sends = first_combine(keep, recv, stats, extra, other)
    w_output, token = load(w_output, own_stats)
    early = [exchange(v, m, count) for v, m in zip(sends[: QUAD - 1], quad_masks)]
    summed, *far_sends = far_combine(far, far_stats, side, early, token)
    late = [exchange(v, m, count) for v, m in zip(sends[QUAD - 1 :], quad_masks)]
    far_sums = [exchange(v, m, count) for v, m in zip(far_sends, far_masks)]
    attended, new_keyval = attend(
        lengths, own, own_stats, side, summed, tables, key_cache, value_cache, early, late,
        far_sums, heads,
    )

    far_pieces = [exchange(attended, m, count) for m in far_masks]
    near_pieces = [attended] + [exchange(attended, m, count) for m in quad_masks]
    far_pieces = [
        piece if mask == 0 else exchange(piece, mask, count)
        for piece in far_pieces
        for mask in [0] + quad_masks
    ]
    near_order = [core + 2 * q for core in range(2) for q in range(QUAD)]
    far_order = [
        core + 2 * q + 2 * QUAD * g
        for core in range(2)
        for g in range(1, groups)
        for q in range(QUAD)
    ]
    near_pieces += [exchange(p, 1, count) for p in near_pieces]
    far_pieces += [exchange(p, 1, count) for p in far_pieces]
    near = near_output(near_pieces, w_output)
    updated = far_output(me, (near_order, far_order), near, far_pieces, residual, w_output)
    return (updated, new_keyval)


def solution(mesh):
    in_specs = (
        P("groups", "gx"),
        P("gx"),
        P("gx", None),
        P("gx", None),
        P(None, "gx"),
        P(("groups", "gx"), None, None),
        P(("groups", "gx"), None, None),
        P(("groups", "gx")),
        P(("groups", "gx")),
    )
    out_specs = (P("groups", "gx"), P(("groups", "gx"), None))
    return jax.shard_map(local, mesh=mesh, in_specs=in_specs, out_specs=out_specs, check_vma=False)
```

time: 177 us -> 58.3 us (0.33)
  waiting for transfers between devices: 102 us -> 15.2 us
  blocking collectives: 34.9 us -> 0 us
  Pallas kernels: 0 us -> 21.6 us
  starting transfers between devices: 0.08 us -> 20.3 us
  matrix products: 17.8 us -> 0 us
  between operations: 14.2 us -> 0.8 us
  other arithmetic: 5.18 us -> 0.12 us
  local copies, waits for them, and re-layouts: 2.24 us -> 0.02 us
    reduce_scatter x1 -> x0, waiting for transfers between devices: 63.9 us -> none  [local(): lax.psum_scatter(jnp.concatenate([jnp.dot(normed, w_query, preferred_elem...]
    all_gather x1 -> x0, waiting for transfers between devices: 38.1 us -> none  [local(): lax.all_gather(attended, 'gx', axis=0, tiled=True)]
    psum x1 -> x0, blocking collectives: 34.9 us -> none  [local(): lax.psum((jnp.sum(stream, axis=1), jnp.sum(stream * stream, axis=1)), 'gx')]
    pallas_call x0 -> x7, Pallas kernels: none -> 21.6 us  [the longest x1 7.29 us: project(): pl.pallas_call(functools.partial(project_kernel, order), in_specs=[SMEM]...]
    ppermute x0 -> x24, starting transfers between devices: none -> 20.3 us  [exchange(): return lax.ppermute(value, 'gx', [(i, i ^ mask) for i in range(count)])]
    dot_general x6 -> x0, matrix products: 17.8 us -> none  [the longest x1 8.54 us: local(): jnp.dot(lax.all_gather(attended, 'gx', axis=0, tiled=True), w_output, pre...]
    ppermute x0 -> x24, waiting for transfers between devices: none -> 15.2 us  [exchange(): return lax.ppermute(value, 'gx', [(i, i ^ mask) for i in range(count)])]
    concatenate x3 -> x0, other arithmetic: 2.61 us -> none  [the longest x1 2 us: local(): jnp.concatenate([jnp.dot(normed, w_query, preferred_element_type=jnp.floa...]
  transfers between devices with their start and end apart: 2 -> 24, of which waited for: 2 -> 8; matrix products, arithmetic and copies ran while one was open for 0% -> 0% of each run, Pallas kernels for 0% -> 14%
where the time goes in v2:
time: 58.3 us; the launch traced here: 58.1 us
  Pallas kernels  21.6 us (37%)
  starting transfers between devices  20.3 us (35%)
  waiting for transfers between devices  15.2 us (26%)
  between operations  0.8 us (1%)
    ppermute x24, starting transfers between devices, exchange(): return lax.ppermute(value, 'gx', [(i, i ^ mask) for i in range(count)])  20.3 us
    ppermute x24, waiting for transfers between devices, exchange(): return lax.ppermute(value, 'gx', [(i, i ^ mask) for i in range(count)])  15.2 us
    pallas_call x1, Pallas kernels, project(): pl.pallas_call(functools.partial(project_kernel, order), in_specs=[SMEM]...  7.29 us
    pallas_call x1, Pallas kernels, load(): pl.pallas_call(load_kernel, in_specs=[pl.BlockSpec(memory_space=pltpu.HBM...  5.3 us
    pallas_call x1, Pallas kernels, far_output(): pl.pallas_call(functools.partial(far_output_kernel, *orders), in_specs=[S...  3.41 us
    pallas_call x1, Pallas kernels, near_output(): pl.pallas_call(near_output_kernel, in_specs=[VMEM] * (1 + len(pieces)), o...  2.53 us
    pallas_call x1, Pallas kernels, attend(): pl.pallas_call(functools.partial(attend_kernel, heads), in_specs=[SMEM] +...  2.46 us
  transfers between devices with their start and end apart: 24, of which 8 were waited for; matrix products, arithmetic and copies ran while one was open for 0% of the time, Pallas kernels for 14%

profile of v2, /device:TPU:0, one launch (start us, length us, event | category | flops | bytes accessed | tf_op | source)
XLA Modules:
  0.0 58.1 jit_solution(14491518160989412243)
XLA Ops:
  0.6 7.3 %project.1 = (f32[64,6656]{1,0:T(8,128)S(1)}, bf16[64,6656]{1,0:T(8,128)(2,1)S(1)}, f32[64,128]{1,0:T(8,128)S(1)}, f32[128,128]{1,0:T(8,128)S(1)}) custom-call(s32[1]{0:T(128)} %bitcast.me_ref, bf16[128,1152]{1,0:T(8,128)(2,1)} %x_ref.1, f32[1152]{0:T(1024)} %gain_hbm.1, bf16[1152,6144]{1,0:T(8,128)(2,1)} %wq_hbm.1, bf16[1152,512]{1,0:T(8,128)(2,1)} %wkv_hbm.1), custom_call_target="tpu_custom_call" | custom-call | tf_op jit(solution)/shard_map/project/pallas_call | solution.py:155
  7.9 0.5 collective-permute-start
  8.5 2.0 %collective-permute-done.1.other_ref = f32[128,128]{1,0:T(8,128)S(1)} collective-permute-done((f32[128,128]{1,0:T(8,128)S(1)}, f32[128,128]{1,0:T(8,128)S(1)}, u32[]{:S(2)}, u32[]{:S(2)}) %collective-permute-start.1) | collective-permute-done | bytes 65568 | tf_op jit(solution)/shard_map/ppermute | solution.py:32
  10.9 3.0 %collective-permute-start.2 = (bf16[16,3968]{1,0:T(8,128)(2,1)S(1)}, bf16[16,3968]{1,0:T(8,128)(2,1)S(1)}, u32[]{:S(2)}, u32[]{:S(2)}) collective-permute-start(bf16[16,3968]{1,0:T(8,128)(2,1)S(1)} %get-tuple-element.33), channel_id=1, source_target_pairs={{0,2},{1,3},{2,0},{3,1},{4,6},{5,7},{6,4},{7,5},{8,10},{9,11},{10,... | collective-permute-start | bytes 380936 | tf_op jit(solution)/shard_map/ppermute | solution.py:32
  13.9 1.6 %collective-permute-start.3 = (bf16[16,3968]{1,0:T(8,128)(2,1)S(1)}, bf16[16,3968]{1,0:T(8,128)(2,1)S(1)}, u32[]{:S(2)}, u32[]{:S(2)}) collective-permute-start(bf16[16,3968]{1,0:T(8,128)(2,1)S(1)} %get-tuple-element.34), channel_id=1, source_target_pairs={{0,4},{1,5},{2,6},{3,7},{4,0},{5,1},{6,2},{7,3},{8,12},{9,13},{10,... | collective-permute-start | bytes 380936 | tf_op jit(solution)/shard_map/ppermute | solution.py:32
  15.5 2.0 %collective-permute-start.5 = (bf16[16,3456]{1,0:T(8,128)(2,1)S(1)}, bf16[16,3456]{1,0:T(8,128)(2,1)S(1)}, u32[]{:S(2)}, u32[]{:S(2)}) collective-permute-start(bf16[16,3456]{1,0:T(8,128)(2,1)S(1)} %get-tuple-element.38), channel_id=1, source_target_pairs={{0,2},{1,3},{2,0},{3,1},{4,6},{5,7},{6,4},{7,5},{8,10},{9,11},{10,... | collective-permute-start | bytes 331784 | tf_op jit(solution)/shard_map/ppermute | solution.py:32
  17.4 1.6 %collective-permute-start.6 = (bf16[16,3456]{1,0:T(8,128)(2,1)S(1)}, bf16[16,3456]{1,0:T(8,128)(2,1)S(1)}, u32[]{:S(2)}, u32[]{:S(2)}) collective-permute-start(bf16[16,3456]{1,0:T(8,128)(2,1)S(1)} %get-tuple-element.39), channel_id=1, source_target_pairs={{0,4},{1,5},{2,6},{3,7},{4,0},{5,1},{6,2},{7,3},{8,12},{9,13},{10,... | collective-permute-start | bytes 331784 | tf_op jit(solution)/shard_map/ppermute | solution.py:32
  19.0 5.3 %load.1 = (bf16[6144,1152]{1,0:T(8,128)(2,1)S(1)}, f32[8,128]{1,0:T(8,128)S(1)}) custom-call(bf16[6144,1152]{1,0:T(8,128)(2,1)} %w_hbm.1, f32[16,128]{1,0:T(8,128)S(1)} %get-tuple-element.27.after_ref.stats_ref), custom_call_target="tpu_custom_call" | custom-call | bytes 14155776 | tf_op jit(solution)/shard_map/load/pallas_call | solution.py:440
  24.8 3.0 %collective-permute-start.8 = (bf16[16,3968]{1,0:T(8,128)(2,1)S(1)}, bf16[16,3968]{1,0:T(8,128)(2,1)S(1)}, u32[]{:S(2)}, u32[]{:S(2)}) collective-permute-start(bf16[16,3968]{1,0:T(8,128)(2,1)S(1)} %get-tuple-element.41), channel_id=1, source_target_pairs={{0,8},{1,9},{2,10},{3,11},{4,12},{5,13},{6,14},{7,15},{8,0},{9,1},... | collective-permute-start | bytes 380936 | tf_op jit(solution)/shard_map/ppermute | solution.py:32
  27.9 2.7 %collective-permute-done.7.refs_5_ = bf16[16,3456]{1,0:T(8,128)(2,1)S(1)} collective-permute-done((bf16[16,3456]{1,0:T(8,128)(2,1)S(1)}, bf16[16,3456]{1,0:T(8,128)(2,1)S(1)}, u32[]{:S(2)}, u32[]{:S(2)}) %collective-permute-start.7) | collective-permute-done | bytes 110624 | tf_op jit(solution)/shard_map/ppermute | solution.py:32
  30.6 2.3 %collective-permute-done.8.refs_6_ = bf16[16,3968]{1,0:T(8,128)(2,1)S(1)} collective-permute-done((bf16[16,3968]{1,0:T(8,128)(2,1)S(1)}, bf16[16,3968]{1,0:T(8,128)(2,1)S(1)}, u32[]{:S(2)}, u32[]{:S(2)}) %collective-permute-start.8) | collective-permute-done | bytes 127008 | tf_op jit(solution)/shard_map/ppermute | solution.py:32
  33.0 2.5 %attend.1 = (bf16[16,3072]{1,0:T(8,128)(2,1)S(1)}, f32[8,512]{1,0:T(8,128)}) custom-call(s32[8]{0:T(128)S(1)} %copy-done.3, f32[16,3328]{1,0:T(8,128)S(1)} %get-tuple-element.29.own_ref, f32[16,128]{1,0:T(8,128)S(1)} %get-tuple-element.27.after_ref.stats_ref, f32[64,128]{1,0:T(8,128)S(1)} %get-tuple-element.30.side_ref, ...), custom_call_target="tpu_custom_call" | custom-call | tf_op jit(solution)/shard_map/attend/pallas_call | solution.py:404
  35.4 1.5 %collective-permute-start.9 = (bf16[16,3072]{1,0:T(8,128)(2,1)S(1)}, bf16[16,3072]{1,0:T(8,128)(2,1)S(1)}, u32[]{:S(2)}, u32[]{:S(2)}) collective-permute-start(bf16[16,3072]{1,0:T(8,128)(2,1)S(1)} %get-tuple-element.42.refs_0_), channel_id=1, source_target_pairs={{0,2},{1,3},{2,0},{3,1},{4,6},{5,7},{6,4},{7,5},{8,10},{9,11},{10,... | collective-permute-start | bytes 294920 | tf_op jit(solution)/shard_map/ppermute | solution.py:32
  37.0 0.5 collective-permute-start.10
  37.4 3.2 %collective-permute-start.16 = (bf16[16,3072]{1,0:T(8,128)(2,1)S(1)}, bf16[16,3072]{1,0:T(8,128)(2,1)S(1)}, u32[]{:S(2)}, u32[]{:S(2)}) collective-permute-start(bf16[16,3072]{1,0:T(8,128)(2,1)S(1)} %get-tuple-element.42.refs_0_), channel_id=1, source_target_pairs={{0,8},{1,9},{2,10},{3,11},{4,12},{5,13},{6,14},{7,15},{8,0},{9,1},... | collective-permute-start | bytes 294920 | tf_op jit(solution)/shard_map/ppermute | solution.py:32
  40.7 0.5 collective-permute-start.13
  41.2 2.4 %collective-permute-done.10.refs_2_ = bf16[16,3072]{1,0:T(8,128)(2,1)S(1)} collective-permute-done((bf16[16,3072]{1,0:T(8,128)(2,1)S(1)}, bf16[16,3072]{1,0:T(8,128)(2,1)S(1)}, u32[]{:S(2)}, u32[]{:S(2)}) %collective-permute-start.10) | collective-permute-done | bytes 98336 | tf_op jit(solution)/shard_map/ppermute | solution.py:32
  43.9 2.3 %collective-permute-done.11.refs_3_ = bf16[16,3072]{1,0:T(8,128)(2,1)S(1)} collective-permute-done((bf16[16,3072]{1,0:T(8,128)(2,1)S(1)}, bf16[16,3072]{1,0:T(8,128)(2,1)S(1)}, u32[]{:S(2)}, u32[]{:S(2)}) %collective-permute-start.11) | collective-permute-done | bytes 98336 | tf_op jit(solution)/shard_map/ppermute | solution.py:32
  46.3 1.9 %collective-permute-start.19 = (bf16[16,3072]{1,0:T(8,128)(2,1)S(1)}, bf16[16,3072]{1,0:T(8,128)(2,1)S(1)}, u32[]{:S(2)}, u32[]{:S(2)}) collective-permute-start(bf16[16,3072]{1,0:T(8,128)(2,1)S(1)} %collective-permute-done.16.refs_0_), channel_id=1, source_target_pairs={{0,6},{1,7},{2,4},{3,5},{4,2},{5,3},{6,0},{7,1},{8,14},{9,15},{10,... | collective-permute-start | bytes 294920 | tf_op jit(solution)/shard_map/ppermute | solution.py:32
  48.2 0.5 collective-permute-start.20
  48.8 2.0 %collective-permute-done.18.refs_2_ = bf16[16,3072]{1,0:T(8,128)(2,1)S(1)} collective-permute-done((bf16[16,3072]{1,0:T(8,128)(2,1)S(1)}, bf16[16,3072]{1,0:T(8,128)(2,1)S(1)}, u32[]{:S(2)}, u32[]{:S(2)}) %collective-permute-start.18) | collective-permute-done | bytes 98336 | tf_op jit(solution)/shard_map/ppermute | solution.py:32
  50.8 1.3 %collective-permute-done.19.refs_3_ = bf16[16,3072]{1,0:T(8,128)(2,1)S(1)} collective-permute-done((bf16[16,3072]{1,0:T(8,128)(2,1)S(1)}, bf16[16,3072]{1,0:T(8,128)(2,1)S(1)}, u32[]{:S(2)}, u32[]{:S(2)}) %collective-permute-start.19) | collective-permute-done | bytes 98336 | tf_op jit(solution)/shard_map/ppermute | solution.py:32
  52.1 2.5 %near_output.1.near_ref = f32[64,1152]{1,0:T(8,128)S(1)} custom-call(bf16[6144,1152]{1,0:T(8,128)(2,1)S(1)} %get-tuple-element.28.w_ref, bf16[16,3072]{1,0:T(8,128)(2,1)S(1)} %get-tuple-element.42.refs_0_, bf16[16,3072]{1,0:T(8,128)(2,1)S(1)} %collective-permute-done.9.refs_1_, bf16[16,3072]{1,0:T(8,128)(2,1)S(1)} %collective-permute-done.10.refs_2_, ...), custom_call_target="tpu_custom_call" | custom-call | flops 905969664 | bytes 4194304 | tf_op jit(solution)/shard_map/near_output/pallas_call | solution.py:472
  54.7 3.4 %far_output.1 = f32[128,1152]{1,0:T(8,128)} custom-call(s32[1]{0:T(128)} %bitcast.me_ref, f32[64,1152]{1,0:T(8,128)S(1)} %near_output.1.near_ref, bf16[128,1152]{1,0:T(8,128)(2,1)S(1)} %copy-done.2, bf16[6144,1152]{1,0:T(8,128)(2,1)S(1)} %get-tuple-element.28.w_ref, bf16[16,3072]{1,0:T(8,128)(2,1)S(1)} %collective-permute-done.16.refs_0_, ...), custom_call_target="tpu_custom_call" | custom-call | tf_op jit(solution)/shard_map/far_output/pallas_call | solution.py:503
  (44 shorter events, 1.6 us)
Async XLA Ops:
  7.9 2.6 %collective-permute-start = (bf16[64,6656]{1,0:T(8,128)(2,1)S(1)}, bf16[64,6656]{1,0:T(8,128)(2,1)S(1)}, u32[]{:S(2)}, u32[]{:S(2)}) collective-permute-start(bf16[64,6656]{1,0:T(8,128)(2,1)S(1)} %get-tuple-element.24), channel_id=1, source_target_pairs={{0,1},{1,0},{2,3},{3,2},{4,5},{5,4},{6,7},{7,6},{8,9},{9,8},{10,11... | collective-permute-start | bytes 2555912 | tf_op jit(solution)/shard_map/ppermute | solution.py:32
  8.5 2.1 %collective-permute-start.1 = (f32[128,128]{1,0:T(8,128)S(1)}, f32[128,128]{1,0:T(8,128)S(1)}, u32[]{:S(2)}, u32[]{:S(2)}) collective-permute-start(f32[128,128]{1,0:T(8,128)S(1)} %get-tuple-element.26.extra_ref), channel_id=1, source_target_pairs={{0,1},{1,0},{2,3},{3,2},{4,5},{5,4},{6,7},{7,6},{8,9},{9,8},{10,11... | collective-permute-start | bytes 196616 | tf_op jit(solution)/shard_map/ppermute | solution.py:32
  10.9 13.4 %collective-permute-start.2 = (bf16[16,3968]{1,0:T(8,128)(2,1)S(1)}, bf16[16,3968]{1,0:T(8,128)(2,1)S(1)}, u32[]{:S(2)}, u32[]{:S(2)}) collective-permute-start(bf16[16,3968]{1,0:T(8,128)(2,1)S(1)} %get-tuple-element.33), channel_id=1, source_target_pairs={{0,2},{1,3},{2,0},{3,1},{4,6},{5,7},{6,4},{7,5},{8,10},{9,11},{10,... | collective-permute-start | bytes 380936 | tf_op jit(solution)/shard_map/ppermute | solution.py:32
  13.9 10.6 %collective-permute-start.3 = (bf16[16,3968]{1,0:T(8,128)(2,1)S(1)}, bf16[16,3968]{1,0:T(8,128)(2,1)S(1)}, u32[]{:S(2)}, u32[]{:S(2)}) collective-permute-start(bf16[16,3968]{1,0:T(8,128)(2,1)S(1)} %get-tuple-element.34), channel_id=1, source_target_pairs={{0,4},{1,5},{2,6},{3,7},{4,0},{5,1},{6,2},{7,3},{8,12},{9,13},{10,... | collective-permute-start | bytes 380936 | tf_op jit(solution)/shard_map/ppermute | solution.py:32
  15.5 9.0 %collective-permute-start.4 = (bf16[16,3968]{1,0:T(8,128)(2,1)S(1)}, bf16[16,3968]{1,0:T(8,128)(2,1)S(1)}, u32[]{:S(2)}, u32[]{:S(2)}) collective-permute-start(bf16[16,3968]{1,0:T(8,128)(2,1)S(1)} %get-tuple-element.35), channel_id=1, source_target_pairs={{0,6},{1,7},{2,4},{3,5},{4,2},{5,3},{6,0},{7,1},{8,14},{9,15},{10,... | collective-permute-start | bytes 380936 | tf_op jit(solution)/shard_map/ppermute | solution.py:32
  15.5 12.4 %collective-permute-start.5 = (bf16[16,3456]{1,0:T(8,128)(2,1)S(1)}, bf16[16,3456]{1,0:T(8,128)(2,1)S(1)}, u32[]{:S(2)}, u32[]{:S(2)}) collective-permute-start(bf16[16,3456]{1,0:T(8,128)(2,1)S(1)} %get-tuple-element.38), channel_id=1, source_target_pairs={{0,2},{1,3},{2,0},{3,1},{4,6},{5,7},{6,4},{7,5},{8,10},{9,11},{10,... | collective-permute-start | bytes 331784 | tf_op jit(solution)/shard_map/ppermute | solution.py:32
  17.4 10.5 %collective-permute-start.6 = (bf16[16,3456]{1,0:T(8,128)(2,1)S(1)}, bf16[16,3456]{1,0:T(8,128)(2,1)S(1)}, u32[]{:S(2)}, u32[]{:S(2)}) collective-permute-start(bf16[16,3456]{1,0:T(8,128)(2,1)S(1)} %get-tuple-element.39), channel_id=1, source_target_pairs={{0,4},{1,5},{2,6},{3,7},{4,0},{5,1},{6,2},{7,3},{8,12},{9,13},{10,... | collective-permute-start | bytes 331784 | tf_op jit(solution)/shard_map/ppermute | solution.py:32
  24.3 6.3 %collective-permute-start.7 = (bf16[16,3456]{1,0:T(8,128)(2,1)S(1)}, bf16[16,3456]{1,0:T(8,128)(2,1)S(1)}, u32[]{:S(2)}, u32[]{:S(2)}) collective-permute-start(bf16[16,3456]{1,0:T(8,128)(2,1)S(1)} %get-tuple-element.40), channel_id=1, source_target_pairs={{0,6},{1,7},{2,4},{3,5},{4,2},{5,3},{6,0},{7,1},{8,14},{9,15},{10,... | collective-permute-start | bytes 331784 | tf_op jit(solution)/shard_map/ppermute | solution.py:32
  24.8 8.2 %collective-permute-start.8 = (bf16[16,3968]{1,0:T(8,128)(2,1)S(1)}, bf16[16,3968]{1,0:T(8,128)(2,1)S(1)}, u32[]{:S(2)}, u32[]{:S(2)}) collective-permute-start(bf16[16,3968]{1,0:T(8,128)(2,1)S(1)} %get-tuple-element.41), channel_id=1, source_target_pairs={{0,8},{1,9},{2,10},{3,11},{4,12},{5,13},{6,14},{7,15},{8,0},{9,1},... | collective-permute-start | bytes 380936 | tf_op jit(solution)/shard_map/ppermute | solution.py:32
  35.4 5.2 %collective-permute-start.9 = (bf16[16,3072]{1,0:T(8,128)(2,1)S(1)}, bf16[16,3072]{1,0:T(8,128)(2,1)S(1)}, u32[]{:S(2)}, u32[]{:S(2)}) collective-permute-start(bf16[16,3072]{1,0:T(8,128)(2,1)S(1)} %get-tuple-element.42.refs_0_), channel_id=1, source_target_pairs={{0,2},{1,3},{2,0},{3,1},{4,6},{5,7},{6,4},{7,5},{8,10},{9,11},{10,... | collective-permute-start | bytes 294920 | tf_op jit(solution)/shard_map/ppermute | solution.py:32
  37.0 6.6 %collective-permute-start.10 = (bf16[16,3072]{1,0:T(8,128)(2,1)S(1)}, bf16[16,3072]{1,0:T(8,128)(2,1)S(1)}, u32[]{:S(2)}, u32[]{:S(2)}) collective-permute-start(bf16[16,3072]{1,0:T(8,128)(2,1)S(1)} %get-tuple-element.42.refs_0_), channel_id=1, source_target_pairs={{0,4},{1,5},{2,6},{3,7},{4,0},{5,1},{6,2},{7,3},{8,12},{9,13},{10,... | collective-permute-start | bytes 294920 | tf_op jit(solution)/shard_map/ppermute | solution.py:32
  37.4 6.2 %collective-permute-start.16 = (bf16[16,3072]{1,0:T(8,128)(2,1)S(1)}, bf16[16,3072]{1,0:T(8,128)(2,1)S(1)}, u32[]{:S(2)}, u32[]{:S(2)}) collective-permute-start(bf16[16,3072]{1,0:T(8,128)(2,1)S(1)} %get-tuple-element.42.refs_0_), channel_id=1, source_target_pairs={{0,8},{1,9},{2,10},{3,11},{4,12},{5,13},{6,14},{7,15},{8,0},{9,1},... | collective-permute-start | bytes 294920 | tf_op jit(solution)/shard_map/ppermute | solution.py:32
  40.6 5.5 %collective-permute-start.11 = (bf16[16,3072]{1,0:T(8,128)(2,1)S(1)}, bf16[16,3072]{1,0:T(8,128)(2,1)S(1)}, u32[]{:S(2)}, u32[]{:S(2)}) collective-permute-start(bf16[16,3072]{1,0:T(8,128)(2,1)S(1)} %get-tuple-element.42.refs_0_), channel_id=1, source_target_pairs={{0,6},{1,7},{2,4},{3,5},{4,2},{5,3},{6,0},{7,1},{8,14},{9,15},{10,... | collective-permute-start | bytes 294920 | tf_op jit(solution)/shard_map/ppermute | solution.py:32
  40.6 5.6 %collective-permute-start.12 = (bf16[16,3072]{1,0:T(8,128)(2,1)S(1)}, bf16[16,3072]{1,0:T(8,128)(2,1)S(1)}, u32[]{:S(2)}, u32[]{:S(2)}) collective-permute-start(bf16[16,3072]{1,0:T(8,128)(2,1)S(1)} %get-tuple-element.42.refs_0_), channel_id=1, source_target_pairs={{0,1},{1,0},{2,3},{3,2},{4,5},{5,4},{6,7},{7,6},{8,9},{9,8},{10,11... | collective-permute-start | bytes 294920 | tf_op jit(solution)/shard_map/ppermute | solution.py:32
  40.7 7.5 %collective-permute-start.13 = (bf16[16,3072]{1,0:T(8,128)(2,1)S(1)}, bf16[16,3072]{1,0:T(8,128)(2,1)S(1)}, u32[]{:S(2)}, u32[]{:S(2)}) collective-permute-start(bf16[16,3072]{1,0:T(8,128)(2,1)S(1)} %collective-permute-done.9.refs_1_), channel_id=1, source_target_pairs={{0,1},{1,0},{2,3},{3,2},{4,5},{5,4},{6,7},{7,6},{8,9},{9,8},{10,11... | collective-permute-start | bytes 294920 | tf_op jit(solution)/shard_map/ppermute | solution.py:32
  43.6 4.6 %collective-permute-start.14 = (bf16[16,3072]{1,0:T(8,128)(2,1)S(1)}, bf16[16,3072]{1,0:T(8,128)(2,1)S(1)}, u32[]{:S(2)}, u32[]{:S(2)}) collective-permute-start(bf16[16,3072]{1,0:T(8,128)(2,1)S(1)} %collective-permute-done.10.refs_2_), channel_id=1, source_target_pairs={{0,1},{1,0},{2,3},{3,2},{4,5},{5,4},{6,7},{7,6},{8,9},{9,8},{10,11... | collective-permute-start | bytes 294920 | tf_op jit(solution)/shard_map/ppermute | solution.py:32
  43.6 5.2 %collective-permute-start.17 = (bf16[16,3072]{1,0:T(8,128)(2,1)S(1)}, bf16[16,3072]{1,0:T(8,128)(2,1)S(1)}, u32[]{:S(2)}, u32[]{:S(2)}) collective-permute-start(bf16[16,3072]{1,0:T(8,128)(2,1)S(1)} %collective-permute-done.16.refs_0_), channel_id=1, source_target_pairs={{0,2},{1,3},{2,0},{3,1},{4,6},{5,7},{6,4},{7,5},{8,10},{9,11},{10,... | collective-permute-start | bytes 294920 | tf_op jit(solution)/shard_map/ppermute | solution.py:32
  46.2 4.6 %collective-permute-start.18 = (bf16[16,3072]{1,0:T(8,128)(2,1)S(1)}, bf16[16,3072]{1,0:T(8,128)(2,1)S(1)}, u32[]{:S(2)}, u32[]{:S(2)}) collective-permute-start(bf16[16,3072]{1,0:T(8,128)(2,1)S(1)} %collective-permute-done.16.refs_0_), channel_id=1, source_target_pairs={{0,4},{1,5},{2,6},{3,7},{4,0},{5,1},{6,2},{7,3},{8,12},{9,13},{10,... | collective-permute-start | bytes 294920 | tf_op jit(solution)/shard_map/ppermute | solution.py:32
  46.3 5.8 %collective-permute-start.19 = (bf16[16,3072]{1,0:T(8,128)(2,1)S(1)}, bf16[16,3072]{1,0:T(8,128)(2,1)S(1)}, u32[]{:S(2)}, u32[]{:S(2)}) collective-permute-start(bf16[16,3072]{1,0:T(8,128)(2,1)S(1)} %collective-permute-done.16.refs_0_), channel_id=1, source_target_pairs={{0,6},{1,7},{2,4},{3,5},{4,2},{5,3},{6,0},{7,1},{8,14},{9,15},{10,... | collective-permute-start | bytes 294920 | tf_op jit(solution)/shard_map/ppermute | solution.py:32
  48.2 3.9 %collective-permute-start.15 = (bf16[16,3072]{1,0:T(8,128)(2,1)S(1)}, bf16[16,3072]{1,0:T(8,128)(2,1)S(1)}, u32[]{:S(2)}, u32[]{:S(2)}) collective-permute-start(bf16[16,3072]{1,0:T(8,128)(2,1)S(1)} %collective-permute-done.11.refs_3_), channel_id=1, source_target_pairs={{0,1},{1,0},{2,3},{3,2},{4,5},{5,4},{6,7},{7,6},{8,9},{9,8},{10,11... | collective-permute-start | bytes 294920 | tf_op jit(solution)/shard_map/ppermute | solution.py:32
  48.2 6.5 %collective-permute-start.20 = (bf16[16,3072]{1,0:T(8,128)(2,1)S(1)}, bf16[16,3072]{1,0:T(8,128)(2,1)S(1)}, u32[]{:S(2)}, u32[]{:S(2)}) collective-permute-start(bf16[16,3072]{1,0:T(8,128)(2,1)S(1)} %collective-permute-done.16.refs_0_), channel_id=1, source_target_pairs={{0,1},{1,0},{2,3},{3,2},{4,5},{5,4},{6,7},{7,6},{8,9},{9,8},{10,11... | collective-permute-start | bytes 294920 | tf_op jit(solution)/shard_map/ppermute | solution.py:32
  48.8 5.8 %collective-permute-start.21 = (bf16[16,3072]{1,0:T(8,128)(2,1)S(1)}, bf16[16,3072]{1,0:T(8,128)(2,1)S(1)}, u32[]{:S(2)}, u32[]{:S(2)}) collective-permute-start(bf16[16,3072]{1,0:T(8,128)(2,1)S(1)} %collective-permute-done.17.refs_1_), channel_id=1, source_target_pairs={{0,1},{1,0},{2,3},{3,2},{4,5},{5,4},{6,7},{7,6},{8,9},{9,8},{10,11... | collective-permute-start | bytes 294920 | tf_op jit(solution)/shard_map/ppermute | solution.py:32
  50.8 3.9 %collective-permute-start.22 = (bf16[16,3072]{1,0:T(8,128)(2,1)S(1)}, bf16[16,3072]{1,0:T(8,128)(2,1)S(1)}, u32[]{:S(2)}, u32[]{:S(2)}) collective-permute-start(bf16[16,3072]{1,0:T(8,128)(2,1)S(1)} %collective-permute-done.18.refs_2_), channel_id=1, source_target_pairs={{0,1},{1,0},{2,3},{3,2},{4,5},{5,4},{6,7},{7,6},{8,9},{9,8},{10,11... | collective-permute-start | bytes 294920 | tf_op jit(solution)/shard_map/ppermute | solution.py:32
  52.1 2.6 %collective-permute-start.23 = (bf16[16,3072]{1,0:T(8,128)(2,1)S(1)}, bf16[16,3072]{1,0:T(8,128)(2,1)S(1)}, u32[]{:S(2)}, u32[]{:S(2)}) collective-permute-start(bf16[16,3072]{1,0:T(8,128)(2,1)S(1)} %collective-permute-done.19.refs_3_), channel_id=1, source_target_pairs={{0,1},{1,0},{2,3},{3,2},{4,5},{5,4},{6,7},{7,6},{8,9},{9,8},{10,11... | collective-permute-start | bytes 294920 | tf_op jit(solution)/shard_map/ppermute | solution.py:32
  (5 other events, 52.0 us)

commit v3 on v2

--- a/solution.py
+++ b/solution.py
@@ -14,8 +14,9 @@
 TILE = 512
 SIDE = 32
 AHEAD = 3
-PACE = 2
+PACE = 1
 QUAD = 4
+PARTS = 4
 EPSILON = 1e-05
 VMEM = pl.BlockSpec(memory_space=pltpu.VMEM)
 SMEM = pl.BlockSpec(memory_space=pltpu.SMEM)
@@ -30,6 +31,10 @@
 
 def exchange(value, mask, count):
     return lax.ppermute(value, "gx", [(i, i ^ mask) for i in range(count)])
+
+
+def behind(value, first):
+    return lax.optimization_barrier((value, first))[0]
 
 
 def in_hbm(value):
@@ -96,11 +101,11 @@
     for t in range(tiles):
         source = wkv_hbm if t == 0 else wq_hbm.at[:, (t - 1) * TILE : t * TILE]
         copies.append(pltpu.make_async_copy(source, w_ref.at[t], w_sem.at[t]))
-    x_copy.wait()
-    gain_copy.wait()
     started = min(AHEAD, tiles)
     for t in range(started):
         copies[t].start()
+    x_copy.wait()
+    gain_copy.wait()
     rows_ref[...] = x_ref[...].astype(jnp.float32)
     gain = gain_ref[...].reshape(1, gain_ref.shape[0])
     high = gain.astype(jnp.bfloat16).astype(jnp.float32)
@@ -259,8 +264,24 @@
     )(keep, recv, stats, extra, other)
 
 
+def far_add_kernel(far_ref, recv_ref, out_ref):
+    cut = far_ref.shape[1]
+    out_ref[...] = far_ref[...] + recv_ref[:, :cut].astype(jnp.float32)
+
+
+def far_add(far, recv):
+    return pl.pallas_call(
+        far_add_kernel,
+        in_specs=[VMEM] * 2,
+        out_specs=VMEM,
+        out_shape=struct(far.shape, far.dtype),
+        compiler_params=pltpu.CompilerParams(vmem_limit_bytes=16 * 2**20),
+        name="far_add",
+    )(far, recv)
+
+
 def far_kernel(far_ref, stats_ref, side_ref, *refs):
-    recv, outs = refs[: QUAD - 1], refs[QUAD:]
+    recv, outs = refs[: QUAD - 1], refs[QUAD - 1 :]
     cut = far_ref.shape[1]
     fold = 2 * BLOCK
     packed = [r[:fold, cut + LANES :].astype(jnp.float32) for r in recv]
@@ -276,27 +297,27 @@
         for c in range(cut // LANES):
             columns = slice(c * LANES, (c + 1) * LANES)
             total = far_ref[at, columns]
-            for r in recv:
+            for r in recv[:-1]:
                 total = total + r[at, columns].astype(jnp.float32)
             for shift, side in zip(shifts, packed):
                 total = total + shift * folded_row(side, c)
             out[:, columns] = total.astype(jnp.bfloat16)
 
 
-def far_combine(far, stats, side, recv, after):
+def far_combine(far, stats, side, recv):
     cut = far.shape[1]
     fold = 2 * BLOCK
     groups = far.shape[0] // fold
     side_columns = SIDE // BLOCK * LANES
     return pl.pallas_call(
         far_kernel,
-        in_specs=[VMEM] * (3 + QUAD - 1) + [pl.BlockSpec(memory_space=pl.ANY)],
+        in_specs=[VMEM] * (3 + QUAD - 1),
         out_specs=[VMEM] * (1 + groups),
         out_shape=[struct((fold, side_columns), jnp.float32)]
         + [struct((fold, cut + LANES + side_columns), jnp.bfloat16)] * groups,
         compiler_params=pltpu.CompilerParams(vmem_limit_bytes=16 * 2**20),
         name="far_combine",
-    )(far, stats, side, *recv, after)
+    )(far, stats, side, *recv)
 
 
 def two_part_dot(left, right, dims):
@@ -310,7 +331,7 @@
     return out[:rows] + out[rows:]
 
 
-def attend_kernel(heads, length_ref, own_ref, stats_ref, side_ref, summed_ref, cos_ref, sin_ref,
+def attend_kernel(heads, length_ref, after_ref, own_ref, stats_ref, side_ref, summed_ref, cos_ref, sin_ref,
                   key_ref, value_ref, *refs):
     early, late = refs[: QUAD - 1], refs[QUAD - 1 : 2 * QUAD - 2]
     far, (attended_ref, keyval_ref, q_ref, out_ref) = refs[2 * QUAD - 2 : -4], refs[-4:]
@@ -399,11 +420,12 @@
             ).astype(jnp.bfloat16)
 
 
-def attend(lengths, own, stats, side, summed, tables, key_cache, value_cache, early, late, far,
+def attend(lengths, after, own, stats, side, summed, tables, key_cache, value_cache, early, late, far,
            heads):
     return pl.pallas_call(
         functools.partial(attend_kernel, heads),
-        in_specs=[SMEM] + [VMEM] * (8 + len(early) + len(late) + len(far)),
+        in_specs=[SMEM, pl.BlockSpec(memory_space=pl.ANY)]
+        + [VMEM] * (8 + len(early) + len(late) + len(far)),
         out_specs=[VMEM] * 2,
         out_shape=[
             struct((2 * BLOCK, heads * HD // 2), jnp.bfloat16),
@@ -416,13 +438,13 @@
         compiler_params=pltpu.CompilerParams(vmem_limit_bytes=24 * 2**20),
         name="attend",
     )(
-        lengths, own, stats, side, summed, *tables, key_cache, value_cache, *early, *late, *far
+        lengths, after, own, stats, side, summed, *tables, key_cache, value_cache, *early, *late, *far
     )
 
 
 def load_kernel(w_hbm, after_ref, out_ref, token_ref, sems):
     parts = sems.shape[0]
-    rows = w_hbm.shape[0] // parts
+    rows = out_ref.shape[0] // parts
     copies = [
         pltpu.make_async_copy(
             w_hbm.at[k * rows : (k + 1) * rows, :], out_ref.at[k * rows : (k + 1) * rows, :], sems.at[k]
@@ -441,11 +463,14 @@
         load_kernel,
         in_specs=[pl.BlockSpec(memory_space=pltpu.HBM), pl.BlockSpec(memory_space=pl.ANY)],
         out_specs=[VMEM] * 2,
-        out_shape=[struct(w_output.shape, w_output.dtype), struct((BLOCK, LANES), jnp.float32)],
-        scratch_shapes=[pltpu.SemaphoreType.DMA((8,))],
+        out_shape=[
+            struct((w_output.shape[0] // 2, w_output.shape[1]), w_output.dtype),
+            struct((BLOCK, LANES), jnp.float32),
+        ],
+        scratch_shapes=[pltpu.SemaphoreType.DMA((PARTS,))],
         compiler_params=pltpu.CompilerParams(vmem_limit_bytes=16 * 2**20),
         cost_estimate=pl.CostEstimate(
-            flops=0, bytes_accessed=2 * w_output.size, transcendentals=0
+            flops=0, bytes_accessed=w_output.size, transcendentals=0
         ),
         name="load",
     )(in_hbm(w_output), after)
@@ -460,30 +485,57 @@
         lhs_ref[at, cut:] = jnp.concatenate([p[BLOCK:] for p in pair], axis=0).astype(jnp.bfloat16)
 
 
-def near_output_kernel(w_ref, *refs):
-    pieces, (out_ref, lhs_ref) = refs[:-2], refs[-2:]
+def near_output_kernel(first_ref, w_hbm, *refs):
+    pieces, (out_ref, second_ref, lhs_ref, sems) = refs[:-4], refs[-4:]
+    depth = second_ref.shape[0]
+    rows = depth // PARTS
+    copies = [
+        pltpu.make_async_copy(
+            w_hbm.at[depth + k * rows : depth + (k + 1) * rows, :],
+            second_ref.at[k * rows : (k + 1) * rows, :],
+            sems.at[k],
+        )
+        for k in range(PARTS)
+    ]
+    for copy in copies:
+        copy.start()
     unfold(lhs_ref, pieces)
-    out_ref[...] = jnp.dot(lhs_ref[...], w_ref[...], preferred_element_type=jnp.float32)
-
-
-def near_output(pieces, w_output):
+    out_ref[...] = jnp.dot(
+        lhs_ref[:, :depth], first_ref[...], preferred_element_type=jnp.float32
+    )
+    for k in range(PARTS):
+        copies[k].wait()
+        out_ref[...] += jnp.dot(
+            lhs_ref[:, depth + k * rows : depth + (k + 1) * rows],
+            second_ref[k * rows : (k + 1) * rows, :],
+            preferred_element_type=jnp.float32,
+        )
+
+
+def near_output(pieces, first, w_output):
     rows = len(pieces) * BLOCK
     depth, width = w_output.shape
     return pl.pallas_call(
         near_output_kernel,
-        in_specs=[VMEM] * (1 + len(pieces)),
-        out_specs=VMEM,
-        out_shape=struct((rows, width), jnp.float32),
-        scratch_shapes=[pltpu.VMEM((rows, depth), jnp.bfloat16)],
+        in_specs=[VMEM, pl.BlockSpec(memory_space=pltpu.HBM)] + [VMEM] * len(pieces),
+        out_specs=[VMEM] * 2,
+        out_shape=[
+            struct((rows, width), jnp.float32),
+            struct((depth // 2, width), w_output.dtype),
+        ],
+        scratch_shapes=[
+            pltpu.VMEM((rows, depth), jnp.bfloat16),
+            pltpu.SemaphoreType.DMA((PARTS,)),
+        ],
         compiler_params=pltpu.CompilerParams(vmem_limit_bytes=24 * 2**20),
         cost_estimate=pl.CostEstimate(
-            flops=2 * rows * depth * width, bytes_accessed=4 * 2**20, transcendentals=0
+            flops=2 * rows * depth * width, bytes_accessed=w_output.size, transcendentals=0
         ),
         name="near_output",
-    )(w_output, *pieces)
-
-
-def far_output_kernel(near_order, far_order, me_ref, near_ref, x_ref, w_ref, *refs):
+    )(first, in_hbm(w_output), *pieces)
+
+
+def far_output_kernel(near_order, far_order, me_ref, near_ref, x_ref, first_ref, second_ref, *refs):
     pieces, (out_ref, lhs_ref, rows_ref, sum_ref) = refs[:-4], refs[-4:]
     me = me_ref[0]
     rows_ref[...] = x_ref[...].astype(jnp.float32)
@@ -491,28 +543,31 @@
         at = pl.ds(pl.multiple_of((me ^ b) * BLOCK, BLOCK), BLOCK)
         out_ref[at, :] = rows_ref[at, :] + near_ref[p * BLOCK : (p + 1) * BLOCK, :]
     unfold(lhs_ref, pieces)
-    sum_ref[...] = jnp.dot(lhs_ref[...], w_ref[...], preferred_element_type=jnp.float32)
+    depth = first_ref.shape[0]
+    sum_ref[...] = jnp.dot(
+        lhs_ref[:, :depth], first_ref[...], preferred_element_type=jnp.float32
+    ) + jnp.dot(lhs_ref[:, depth:], second_ref[...], preferred_element_type=jnp.float32)
     for p, b in enumerate(far_order):
         at = pl.ds(pl.multiple_of((me ^ b) * BLOCK, BLOCK), BLOCK)
         out_ref[at, :] = rows_ref[at, :] + sum_ref[p * BLOCK : (p + 1) * BLOCK, :]
 
 
-def far_output(me, orders, near, pieces, residual, w_output):
+def far_output(me, orders, near, pieces, residual, weights):
     total, width = residual.shape
     rows = len(pieces) * BLOCK
     return pl.pallas_call(
         functools.partial(far_output_kernel, *orders),
-        in_specs=[SMEM] + [VMEM] * (3 + len(pieces)),
+        in_specs=[SMEM] + [VMEM] * (4 + len(pieces)),
         out_specs=VMEM,
         out_shape=struct((total, width), jnp.float32),
         scratch_shapes=[
-            pltpu.VMEM((rows, w_output.shape[0]), jnp.bfloat16),
+            pltpu.VMEM((rows, 2 * weights[0].shape[0]), jnp.bfloat16),
             pltpu.VMEM((total, width), jnp.float32),
             pltpu.VMEM((rows, width), jnp.float32),
         ],
         compiler_params=pltpu.CompilerParams(vmem_limit_bytes=24 * 2**20),
         name="far_output",
-    )(me, near, residual, w_output, *pieces)
+    )(me, near, residual, *weights, *pieces)
 
 
 def local(
@@ -533,18 +588,20 @@
     recv = exchange(send, 1, count)
     other = exchange(extra, 1, count)
     own, far, own_stats, far_stats, side, *sends = first_combine(keep, recv, stats, extra, other)
-    w_output, token = load(w_output, own_stats)
     early = [exchange(v, m, count) for v, m in zip(sends[: QUAD - 1], quad_masks)]
-    summed, *far_sends = far_combine(far, far_stats, side, early, token)
+    far = far_add(far, early[-1])
+    summed, *far_sends = far_combine(far, far_stats, side, early)
     late = [exchange(v, m, count) for v, m in zip(sends[QUAD - 1 :], quad_masks)]
+    first, token = load(w_output, summed)
     far_sums = [exchange(v, m, count) for v, m in zip(far_sends, far_masks)]
     attended, new_keyval = attend(
-        lengths, own, own_stats, side, summed, tables, key_cache, value_cache, early, late,
+        lengths, token, own, own_stats, side, summed, tables, key_cache, value_cache, early, late,
         far_sums, heads,
     )
 
     far_pieces = [exchange(attended, m, count) for m in far_masks]
-    near_pieces = [attended] + [exchange(attended, m, count) for m in quad_masks]
+    copied = attended
+    near_pieces = [attended] + [exchange(copied, m, count) for m in quad_masks]
     far_pieces = [
         piece if mask == 0 else exchange(piece, mask, count)
         for piece in far_pieces
@@ -557,10 +614,15 @@
         for g in range(1, groups)
         for q in range(QUAD)
     ]
-    near_pieces += [exchange(p, 1, count) for p in near_pieces]
-    far_pieces += [exchange(p, 1, count) for p in far_pieces]
-    near = near_output(near_pieces, w_output)
-    updated = far_output(me, (near_order, far_order), near, far_pieces, residual, w_output)
+    near_pieces += [exchange(behind(p, far_pieces[0]), 1, count) for p in near_pieces]
+    near, second = near_output(near_pieces, first, w_output)
+    far_pieces += [
+        exchange(p if k % QUAD == 0 else behind(p, near), 1, count)
+        for k, p in enumerate(far_pieces)
+    ]
+    updated = far_output(
+        me, (near_order, far_order), near, far_pieces, residual, (first, second)
+    )
     return (updated, new_keyval)
 
 

time: 58.3 us -> 55.4 us (0.950)
  waiting for transfers between devices: 15.2 us -> 9.98 us
  starting transfers between devices: 20.3 us -> 24.1 us
  Pallas kernels: 21.6 us -> 20.2 us
    ppermute x24, waiting for transfers between devices: 15.2 us -> 9.98 us  [exchange(): return lax.ppermute(value, 'gx', [(i, i ^ mask) for i in range(count)])]
    ppermute x24, starting transfers between devices: 20.3 us -> 24.1 us  [exchange(): return lax.ppermute(value, 'gx', [(i, i ^ mask) for i in range(count)])]
    pallas_call x1, Pallas kernels: 5.3 us -> 3.25 us  [load(): pl.pallas_call(load_kernel, in_specs=[pl.BlockSpec(memory_space=pltpu.HBM...]
    pallas_call x3 -> x4, Pallas kernels: 5.31 us -> 6.51 us  [the longest x1 3.73 us: near_output(): pl.pallas_call(near_output_kernel, in_specs=[VMEM, pl.BlockSpec(memory_sp...]
    pallas_call x1, Pallas kernels: 7.29 us -> 6.7 us  [project(): pl.pallas_call(functools.partial(project_kernel, order), in_specs=[SMEM]...]
  transfers between devices with their start and end apart: 24 -> 24, of which waited for: 8 -> 11; matrix products, arithmetic and copies ran while one was open for 0% -> 0% of each run, Pallas kernels for 14% -> 13%
where the time goes in v3:
time: 55.4 us; the launch traced here: 55.3 us
  starting transfers between devices  24.1 us (44%)
  Pallas kernels  20.2 us (36%)
  waiting for transfers between devices  9.98 us (18%)
  between operations  0.78 us (1%)
    ppermute x24, starting transfers between devices, exchange(): return lax.ppermute(value, 'gx', [(i, i ^ mask) for i in range(count)])  24.1 us
    ppermute x24, waiting for transfers between devices, exchange(): return lax.ppermute(value, 'gx', [(i, i ^ mask) for i in range(count)])  9.98 us
    pallas_call x1, Pallas kernels, project(): pl.pallas_call(functools.partial(project_kernel, order), in_specs=[SMEM]...  6.7 us
    pallas_call x1, Pallas kernels, near_output(): pl.pallas_call(near_output_kernel, in_specs=[VMEM, pl.BlockSpec(memory_sp...  3.73 us
    pallas_call x1, Pallas kernels, far_output(): pl.pallas_call(functools.partial(far_output_kernel, *orders), in_specs=[S...  3.43 us
    pallas_call x1, Pallas kernels, load(): pl.pallas_call(load_kernel, in_specs=[pl.BlockSpec(memory_space=pltpu.HBM...  3.25 us
    pallas_call x1, Pallas kernels, attend(): pl.pallas_call(functools.partial(attend_kernel, heads), in_specs=[SMEM, p...  2.45 us
  transfers between devices with their start and end apart: 24, of which 11 were waited for; matrix products, arithmetic and copies ran while one was open for 0% of the time, Pallas kernels for 13%

profile of v3, /device:TPU:0, one launch (start us, length us, event | category | flops | bytes accessed | tf_op | source)
XLA Modules:
  0.0 55.3 jit_solution(10733468195032222971)
XLA Ops:
  0.6 6.7 %project.1 = (f32[64,6656]{1,0:T(8,128)S(1)}, bf16[64,6656]{1,0:T(8,128)(2,1)S(1)}, f32[64,128]{1,0:T(8,128)S(1)}, f32[128,128]{1,0:T(8,128)S(1)}) custom-call(s32[1]{0:T(128)} %bitcast.me_ref, bf16[128,1152]{1,0:T(8,128)(2,1)} %x_ref.1, f32[1152]{0:T(1024)} %gain_hbm.1, bf16[1152,6144]{1,0:T(8,128)(2,1)} %wq_hbm.1, bf16[1152,512]{1,0:T(8,128)(2,1)} %wkv_hbm.1), custom_call_target="tpu_custom_call" | custom-call | tf_op jit(solution)/shard_map/project/pallas_call | solution.py:160
  7.4 0.5 collective-permute-start
  8.0 2.0 %collective-permute-done.1.other_ref = f32[128,128]{1,0:T(8,128)S(1)} collective-permute-done((f32[128,128]{1,0:T(8,128)S(1)}, f32[128,128]{1,0:T(8,128)S(1)}, u32[]{:S(2)}, u32[]{:S(2)}) %collective-permute-start.1) | collective-permute-done | bytes 65568 | tf_op jit(solution)/shard_map/ppermute | solution.py:33
  10.3 4.0 %collective-permute-start.2 = (bf16[16,3968]{1,0:T(8,128)(2,1)S(1)}, bf16[16,3968]{1,0:T(8,128)(2,1)S(1)}, u32[]{:S(2)}, u32[]{:S(2)}) collective-permute-start(bf16[16,3968]{1,0:T(8,128)(2,1)S(1)} %get-tuple-element.37), channel_id=1, source_target_pairs={{0,6},{1,7},{2,4},{3,5},{4,2},{5,3},{6,0},{7,1},{8,14},{9,15},{10,... | collective-permute-start | bytes 380936 | tf_op jit(solution)/shard_map/ppermute | solution.py:33
  15.0 1.9 %collective-permute-start.5 = (bf16[16,3456]{1,0:T(8,128)(2,1)S(1)}, bf16[16,3456]{1,0:T(8,128)(2,1)S(1)}, u32[]{:S(2)}, u32[]{:S(2)}) collective-permute-start(bf16[16,3456]{1,0:T(8,128)(2,1)S(1)} %get-tuple-element.47), channel_id=1, source_target_pairs={{0,2},{1,3},{2,0},{3,1},{4,6},{5,7},{6,4},{7,5},{8,10},{9,11},{10,... | collective-permute-start | bytes 331784 | tf_op jit(solution)/shard_map/ppermute | solution.py:33
  16.8 1.6 %collective-permute-start.6 = (bf16[16,3456]{1,0:T(8,128)(2,1)S(1)}, bf16[16,3456]{1,0:T(8,128)(2,1)S(1)}, u32[]{:S(2)}, u32[]{:S(2)}) collective-permute-start(bf16[16,3456]{1,0:T(8,128)(2,1)S(1)} %get-tuple-element.48), channel_id=1, source_target_pairs={{0,4},{1,5},{2,6},{3,7},{4,0},{5,1},{6,2},{7,3},{8,12},{9,13},{10,... | collective-permute-start | bytes 331784 | tf_op jit(solution)/shard_map/ppermute | solution.py:33
  18.4 3.1 %collective-permute-start.7 = (bf16[16,3456]{1,0:T(8,128)(2,1)S(1)}, bf16[16,3456]{1,0:T(8,128)(2,1)S(1)}, u32[]{:S(2)}, u32[]{:S(2)}) collective-permute-start(bf16[16,3456]{1,0:T(8,128)(2,1)S(1)} %get-tuple-element.49), channel_id=1, source_target_pairs={{0,6},{1,7},{2,4},{3,5},{4,2},{5,3},{6,0},{7,1},{8,14},{9,15},{10,... | collective-permute-start | bytes 331784 | tf_op jit(solution)/shard_map/ppermute | solution.py:33
  22.0 2.6 %collective-permute-start.8 = (bf16[16,3968]{1,0:T(8,128)(2,1)S(1)}, bf16[16,3968]{1,0:T(8,128)(2,1)S(1)}, u32[]{:S(2)}, u32[]{:S(2)}) collective-permute-start(bf16[16,3968]{1,0:T(8,128)(2,1)S(1)} %get-tuple-element.50), channel_id=1, source_target_pairs={{0,8},{1,9},{2,10},{3,11},{4,12},{5,13},{6,14},{7,15},{8,0},{9,1},... | collective-permute-start | bytes 380936 | tf_op jit(solution)/shard_map/ppermute | solution.py:33
  24.8 3.3 %load.1 = (bf16[3072,1152]{1,0:T(8,128)(2,1)S(1)}, f32[8,128]{1,0:T(8,128)S(1)}) custom-call(bf16[6144,1152]{1,0:T(8,128)(2,1)} %w_hbm.3, f32[16,512]{1,0:T(8,128)S(1)} %get-tuple-element.42.after_ref.summed_ref), custom_call_target="tpu_custom_call" | custom-call | bytes 7077888 | tf_op jit(solution)/shard_map/load/pallas_call | solution.py:462
  28.1 2.5 %collective-permute-done.8.refs_6_ = bf16[16,3968]{1,0:T(8,128)(2,1)S(1)} collective-permute-done((bf16[16,3968]{1,0:T(8,128)(2,1)S(1)}, bf16[16,3968]{1,0:T(8,128)(2,1)S(1)}, u32[]{:S(2)}, u32[]{:S(2)}) %collective-permute-start.8) | collective-permute-done | bytes 127008 | tf_op jit(solution)/shard_map/ppermute | solution.py:33
  30.6 2.4 %attend.1 = (bf16[16,3072]{1,0:T(8,128)(2,1)S(1)}, f32[8,512]{1,0:T(8,128)}) custom-call(s32[8]{0:T(128)S(1)} %copy-done.3, f32[8,128]{1,0:T(8,128)S(1)} %get-tuple-element.44.after_ref, f32[16,3328]{1,0:T(8,128)S(1)} %get-tuple-element.45.own_ref, f32[16,128]{1,0:T(8,128)S(1)} %get-tuple-element.46.stats_ref, f32[64,128]{1,0:T(8,128)S(1)} %get-tuple-element.39.side_ref, ...), custom_call_target="tpu_custom_call" | custom-call | tf_op jit(solution)/shard_map/attend/pallas_call | solution.py:425
  33.4 2.8 %collective-permute-start.11 = (bf16[16,3072]{1,0:T(8,128)(2,1)S(1)}, bf16[16,3072]{1,0:T(8,128)(2,1)S(1)}, u32[]{:S(2)}, u32[]{:S(2)}) collective-permute-start(bf16[16,3072]{1,0:T(8,128)(2,1)S(1)} %get-tuple-element.52.refs_0_), channel_id=1, source_target_pairs={{0,6},{1,7},{2,4},{3,5},{4,2},{5,3},{6,0},{7,1},{8,14},{9,15},{10,... | collective-permute-start | bytes 294920 | tf_op jit(solution)/shard_map/ppermute | solution.py:33
  36.3 0.5 collective-permute-start.10
  36.8 1.5 %collective-permute-start.9 = (bf16[16,3072]{1,0:T(8,128)(2,1)S(1)}, bf16[16,3072]{1,0:T(8,128)(2,1)S(1)}, u32[]{:S(2)}, u32[]{:S(2)}) collective-permute-start(bf16[16,3072]{1,0:T(8,128)(2,1)S(1)} %get-tuple-element.52.refs_0_), channel_id=1, source_target_pairs={{0,2},{1,3},{2,0},{3,1},{4,6},{5,7},{6,4},{7,5},{8,10},{9,11},{10,... | collective-permute-start | bytes 294920 | tf_op jit(solution)/shard_map/ppermute | solution.py:33
  38.2 1.2 %collective-permute-done.12.refs_0_ = bf16[16,3072]{1,0:T(8,128)(2,1)S(1)} collective-permute-done((bf16[16,3072]{1,0:T(8,128)(2,1)S(1)}, bf16[16,3072]{1,0:T(8,128)(2,1)S(1)}, u32[]{:S(2)}, u32[]{:S(2)}) %collective-permute-start.12) | collective-permute-done | bytes 98336 | tf_op jit(solution)/shard_map/ppermute | solution.py:33
  39.4 1.1 %collective-permute-done.11.refs_3_ = bf16[16,3072]{1,0:T(8,128)(2,1)S(1)} collective-permute-done((bf16[16,3072]{1,0:T(8,128)(2,1)S(1)}, bf16[16,3072]{1,0:T(8,128)(2,1)S(1)}, u32[]{:S(2)}, u32[]{:S(2)}) %collective-permute-start.11) | collective-permute-done | bytes 98336 | tf_op jit(solution)/shard_map/ppermute | solution.py:33
  40.5 1.3 %collective-permute-done.10.refs_2_ = bf16[16,3072]{1,0:T(8,128)(2,1)S(1)} collective-permute-done((bf16[16,3072]{1,0:T(8,128)(2,1)S(1)}, bf16[16,3072]{1,0:T(8,128)(2,1)S(1)}, u32[]{:S(2)}, u32[]{:S(2)}) %collective-permute-start.10) | collective-permute-done | bytes 98336 | tf_op jit(solution)/shard_map/ppermute | solution.py:33
  41.8 0.5 collective-permute-start.14
  42.3 2.0 %collective-permute-start.19 = (bf16[16,3072]{1,0:T(8,128)(2,1)S(1)}, bf16[16,3072]{1,0:T(8,128)(2,1)S(1)}, u32[]{:S(2)}, u32[]{:S(2)}) collective-permute-start(bf16[16,3072]{1,0:T(8,128)(2,1)S(1)} %collective-permute-done.12.refs_0_), channel_id=1, source_target_pairs={{0,6},{1,7},{2,4},{3,5},{4,2},{5,3},{6,0},{7,1},{8,14},{9,15},{10,... | collective-permute-start | bytes 294920 | tf_op jit(solution)/shard_map/ppermute | solution.py:33
  44.3 0.5 collective-permute-start.18
  44.8 1.0 %collective-permute-start.17 = (bf16[16,3072]{1,0:T(8,128)(2,1)S(1)}, bf16[16,3072]{1,0:T(8,128)(2,1)S(1)}, u32[]{:S(2)}, u32[]{:S(2)}) collective-permute-start(bf16[16,3072]{1,0:T(8,128)(2,1)S(1)} %collective-permute-done.12.refs_0_), channel_id=1, source_target_pairs={{0,2},{1,3},{2,0},{3,1},{4,6},{5,7},{6,4},{7,5},{8,10},{9,11},{10,... | collective-permute-start | bytes 294920 | tf_op jit(solution)/shard_map/ppermute | solution.py:33
  45.8 3.7 %near_output.1 = (f32[64,1152]{1,0:T(8,128)S(1)}, bf16[3072,1152]{1,0:T(8,128)(2,1)S(1)}) custom-call(bf16[3072,1152]{1,0:T(8,128)(2,1)S(1)} %get-tuple-element.43.first_ref, bf16[6144,1152]{1,0:T(8,128)(2,1)} %w_hbm.3, bf16[16,3072]{1,0:T(8,128)(2,1)S(1)} %get-tuple-element.52.refs_0_, bf16[16,3072]{1,0:T(8,128)(2,1)S(1)} %collective-permute-done.9.refs_1_, ...), custom_call_target="tpu_custom_call" | custom-call | flops 905969664 | bytes 7077888 | tf_op jit(solution)/shard_map/near_output/pallas_call | solution.py:518
  50.6 0.7 %collective-permute-done.21.refs_5_ = bf16[16,3072]{1,0:T(8,128)(2,1)S(1)} collective-permute-done((bf16[16,3072]{1,0:T(8,128)(2,1)S(1)}, bf16[16,3072]{1,0:T(8,128)(2,1)S(1)}, u32[]{:S(2)}, u32[]{:S(2)}) %collective-permute-start.21) | collective-permute-done | bytes 98336 | tf_op jit(solution)/shard_map/ppermute | solution.py:33
  51.9 3.4 %far_output.1 = f32[128,1152]{1,0:T(8,128)} custom-call(s32[1]{0:T(128)} %bitcast.me_ref, f32[64,1152]{1,0:T(8,128)S(1)} %get-tuple-element.56.near_ref, bf16[128,1152]{1,0:T(8,128)(2,1)S(1)} %copy-done.2, bf16[3072,1152]{1,0:T(8,128)(2,1)S(1)} %get-tuple-element.43.first_ref, bf16[3072,1152]{1,0:T(8,128)(2,1)S(1)} %get-tuple-element.57.second_ref, ...), custom_call_target="tpu_custom_call" | custom-call | tf_op jit(solution)/shard_map/far_output/pallas_call | solution.py:558
  (45 shorter events, 3.7 us)
Async XLA Ops:
  7.4 2.6 %collective-permute-start = (bf16[64,6656]{1,0:T(8,128)(2,1)S(1)}, bf16[64,6656]{1,0:T(8,128)(2,1)S(1)}, u32[]{:S(2)}, u32[]{:S(2)}) collective-permute-start(bf16[64,6656]{1,0:T(8,128)(2,1)S(1)} %get-tuple-element.33), channel_id=1, source_target_pairs={{0,1},{1,0},{2,3},{3,2},{4,5},{5,4},{6,7},{7,6},{8,9},{9,8},{10,11... | collective-permute-start | bytes 2555912 | tf_op jit(solution)/shard_map/ppermute | solution.py:33
  7.9 2.1 %collective-permute-start.1 = (f32[128,128]{1,0:T(8,128)S(1)}, f32[128,128]{1,0:T(8,128)S(1)}, u32[]{:S(2)}, u32[]{:S(2)}) collective-permute-start(f32[128,128]{1,0:T(8,128)S(1)} %get-tuple-element.35.extra_ref), channel_id=1, source_target_pairs={{0,1},{1,0},{2,3},{3,2},{4,5},{5,4},{6,7},{7,6},{8,9},{9,8},{10,11... | collective-permute-start | bytes 196616 | tf_op jit(solution)/shard_map/ppermute | solution.py:33
  10.3 8.1 %collective-permute-start.2 = (bf16[16,3968]{1,0:T(8,128)(2,1)S(1)}, bf16[16,3968]{1,0:T(8,128)(2,1)S(1)}, u32[]{:S(2)}, u32[]{:S(2)}) collective-permute-start(bf16[16,3968]{1,0:T(8,128)(2,1)S(1)} %get-tuple-element.37), channel_id=1, source_target_pairs={{0,6},{1,7},{2,4},{3,5},{4,2},{5,3},{6,0},{7,1},{8,14},{9,15},{10,... | collective-permute-start | bytes 380936 | tf_op jit(solution)/shard_map/ppermute | solution.py:33
  14.3 7.2 %collective-permute-start.3 = (bf16[16,3968]{1,0:T(8,128)(2,1)S(1)}, bf16[16,3968]{1,0:T(8,128)(2,1)S(1)}, u32[]{:S(2)}, u32[]{:S(2)}) collective-permute-start(bf16[16,3968]{1,0:T(8,128)(2,1)S(1)} %get-tuple-element.40), channel_id=1, source_target_pairs={{0,2},{1,3},{2,0},{3,1},{4,6},{5,7},{6,4},{7,5},{8,10},{9,11},{10,... | collective-permute-start | bytes 380936 | tf_op jit(solution)/shard_map/ppermute | solution.py:33
  14.8 6.9 %collective-permute-start.4 = (bf16[16,3968]{1,0:T(8,128)(2,1)S(1)}, bf16[16,3968]{1,0:T(8,128)(2,1)S(1)}, u32[]{:S(2)}, u32[]{:S(2)}) collective-permute-start(bf16[16,3968]{1,0:T(8,128)(2,1)S(1)} %get-tuple-element.41), channel_id=1, source_target_pairs={{0,4},{1,5},{2,6},{3,7},{4,0},{5,1},{6,2},{7,3},{8,12},{9,13},{10,... | collective-permute-start | bytes 380936 | tf_op jit(solution)/shard_map/ppermute | solution.py:33
  15.0 13.1 %collective-permute-start.5 = (bf16[16,3456]{1,0:T(8,128)(2,1)S(1)}, bf16[16,3456]{1,0:T(8,128)(2,1)S(1)}, u32[]{:S(2)}, u32[]{:S(2)}) collective-permute-start(bf16[16,3456]{1,0:T(8,128)(2,1)S(1)} %get-tuple-element.47), channel_id=1, source_target_pairs={{0,2},{1,3},{2,0},{3,1},{4,6},{5,7},{6,4},{7,5},{8,10},{9,11},{10,... | collective-permute-start | bytes 331784 | tf_op jit(solution)/shard_map/ppermute | solution.py:33
  16.8 11.2 %collective-permute-start.6 = (bf16[16,3456]{1,0:T(8,128)(2,1)S(1)}, bf16[16,3456]{1,0:T(8,128)(2,1)S(1)}, u32[]{:S(2)}, u32[]{:S(2)}) collective-permute-start(bf16[16,3456]{1,0:T(8,128)(2,1)S(1)} %get-tuple-element.48), channel_id=1, source_target_pairs={{0,4},{1,5},{2,6},{3,7},{4,0},{5,1},{6,2},{7,3},{8,12},{9,13},{10,... | collective-permute-start | bytes 331784 | tf_op jit(solution)/shard_map/ppermute | solution.py:33
  18.4 9.6 %collective-permute-start.7 = (bf16[16,3456]{1,0:T(8,128)(2,1)S(1)}, bf16[16,3456]{1,0:T(8,128)(2,1)S(1)}, u32[]{:S(2)}, u32[]{:S(2)}) collective-permute-start(bf16[16,3456]{1,0:T(8,128)(2,1)S(1)} %get-tuple-element.49), channel_id=1, source_target_pairs={{0,6},{1,7},{2,4},{3,5},{4,2},{5,3},{6,0},{7,1},{8,14},{9,15},{10,... | collective-permute-start | bytes 331784 | tf_op jit(solution)/shard_map/ppermute | solution.py:33
  22.0 8.6 %collective-permute-start.8 = (bf16[16,3968]{1,0:T(8,128)(2,1)S(1)}, bf16[16,3968]{1,0:T(8,128)(2,1)S(1)}, u32[]{:S(2)}, u32[]{:S(2)}) collective-permute-start(bf16[16,3968]{1,0:T(8,128)(2,1)S(1)} %get-tuple-element.50), channel_id=1, source_target_pairs={{0,8},{1,9},{2,10},{3,11},{4,12},{5,13},{6,14},{7,15},{8,0},{9,1},... | collective-permute-start | bytes 380936 | tf_op jit(solution)/shard_map/ppermute | solution.py:33
  33.1 6.3 %collective-permute-start.12 = (bf16[16,3072]{1,0:T(8,128)(2,1)S(1)}, bf16[16,3072]{1,0:T(8,128)(2,1)S(1)}, u32[]{:S(2)}, u32[]{:S(2)}) collective-permute-start(bf16[16,3072]{1,0:T(8,128)(2,1)S(1)} %get-tuple-element.52.refs_0_), channel_id=1, source_target_pairs={{0,8},{1,9},{2,10},{3,11},{4,12},{5,13},{6,14},{7,15},{8,0},{9,1},... | collective-permute-start | bytes 294920 | tf_op jit(solution)/shard_map/ppermute | solution.py:33
  33.4 7.0 %collective-permute-start.11 = (bf16[16,3072]{1,0:T(8,128)(2,1)S(1)}, bf16[16,3072]{1,0:T(8,128)(2,1)S(1)}, u32[]{:S(2)}, u32[]{:S(2)}) collective-permute-start(bf16[16,3072]{1,0:T(8,128)(2,1)S(1)} %get-tuple-element.52.refs_0_), channel_id=1, source_target_pairs={{0,6},{1,7},{2,4},{3,5},{4,2},{5,3},{6,0},{7,1},{8,14},{9,15},{10,... | collective-permute-start | bytes 294920 | tf_op jit(solution)/shard_map/ppermute | solution.py:33
  36.3 5.5 %collective-permute-start.10 = (bf16[16,3072]{1,0:T(8,128)(2,1)S(1)}, bf16[16,3072]{1,0:T(8,128)(2,1)S(1)}, u32[]{:S(2)}, u32[]{:S(2)}) collective-permute-start(bf16[16,3072]{1,0:T(8,128)(2,1)S(1)} %get-tuple-element.52.refs_0_), channel_id=1, source_target_pairs={{0,4},{1,5},{2,6},{3,7},{4,0},{5,1},{6,2},{7,3},{8,12},{9,13},{10,... | collective-permute-start | bytes 294920 | tf_op jit(solution)/shard_map/ppermute | solution.py:33
  36.8 5.0 %collective-permute-start.9 = (bf16[16,3072]{1,0:T(8,128)(2,1)S(1)}, bf16[16,3072]{1,0:T(8,128)(2,1)S(1)}, u32[]{:S(2)}, u32[]{:S(2)}) collective-permute-start(bf16[16,3072]{1,0:T(8,128)(2,1)S(1)} %get-tuple-element.52.refs_0_), channel_id=1, source_target_pairs={{0,2},{1,3},{2,0},{3,1},{4,6},{5,7},{6,4},{7,5},{8,10},{9,11},{10,... | collective-permute-start | bytes 294920 | tf_op jit(solution)/shard_map/ppermute | solution.py:33
  39.4 4.9 %collective-permute-start.13 = (bf16[16,3072]{1,0:T(8,128)(2,1)S(1)}, bf16[16,3072]{1,0:T(8,128)(2,1)S(1)}, u32[]{:S(2)}, u32[]{:S(2)}) collective-permute-start(bf16[16,3072]{1,0:T(8,128)(2,1)S(1)} %get-tuple-element.52.refs_0_), channel_id=1, source_target_pairs={{0,1},{1,0},{2,3},{3,2},{4,5},{5,4},{6,7},{7,6},{8,9},{9,8},{10,11... | collective-permute-start | bytes 294920 | tf_op jit(solution)/shard_map/ppermute | solution.py:33
  40.5 4.3 %collective-permute-start.16 = (bf16[16,3072]{1,0:T(8,128)(2,1)S(1)}, bf16[16,3072]{1,0:T(8,128)(2,1)S(1)}, u32[]{:S(2)}, u32[]{:S(2)}) collective-permute-start(bf16[16,3072]{1,0:T(8,128)(2,1)S(1)} %collective-permute-done.11.refs_3_), channel_id=1, source_target_pairs={{0,1},{1,0},{2,3},{3,2},{4,5},{5,4},{6,7},{7,6},{8,9},{9,8},{10,11... | collective-permute-start | bytes 294920 | tf_op jit(solution)/shard_map/ppermute | solution.py:33
  41.8 4.0 %collective-permute-start.15 = (bf16[16,3072]{1,0:T(8,128)(2,1)S(1)}, bf16[16,3072]{1,0:T(8,128)(2,1)S(1)}, u32[]{:S(2)}, u32[]{:S(2)}) collective-permute-start(bf16[16,3072]{1,0:T(8,128)(2,1)S(1)} %collective-permute-done.10.refs_2_), channel_id=1, source_target_pairs={{0,1},{1,0},{2,3},{3,2},{4,5},{5,4},{6,7},{7,6},{8,9},{9,8},{10,11... | collective-permute-start | bytes 294920 | tf_op jit(solution)/shard_map/ppermute | solution.py:33
  41.8 4.0 %collective-permute-start.14 = (bf16[16,3072]{1,0:T(8,128)(2,1)S(1)}, bf16[16,3072]{1,0:T(8,128)(2,1)S(1)}, u32[]{:S(2)}, u32[]{:S(2)}) collective-permute-start(bf16[16,3072]{1,0:T(8,128)(2,1)S(1)} %collective-permute-done.9.refs_1_), channel_id=1, source_target_pairs={{0,1},{1,0},{2,3},{3,2},{4,5},{5,4},{6,7},{7,6},{8,9},{9,8},{10,11... | collective-permute-start | bytes 294920 | tf_op jit(solution)/shard_map/ppermute | solution.py:33
  42.3 7.3 %collective-permute-start.19 = (bf16[16,3072]{1,0:T(8,128)(2,1)S(1)}, bf16[16,3072]{1,0:T(8,128)(2,1)S(1)}, u32[]{:S(2)}, u32[]{:S(2)}) collective-permute-start(bf16[16,3072]{1,0:T(8,128)(2,1)S(1)} %collective-permute-done.12.refs_0_), channel_id=1, source_target_pairs={{0,6},{1,7},{2,4},{3,5},{4,2},{5,3},{6,0},{7,1},{8,14},{9,15},{10,... | collective-permute-start | bytes 294920 | tf_op jit(solution)/shard_map/ppermute | solution.py:33
  44.3 5.6 %collective-permute-start.18 = (bf16[16,3072]{1,0:T(8,128)(2,1)S(1)}, bf16[16,3072]{1,0:T(8,128)(2,1)S(1)}, u32[]{:S(2)}, u32[]{:S(2)}) collective-permute-start(bf16[16,3072]{1,0:T(8,128)(2,1)S(1)} %collective-permute-done.12.refs_0_), channel_id=1, source_target_pairs={{0,4},{1,5},{2,6},{3,7},{4,0},{5,1},{6,2},{7,3},{8,12},{9,13},{10,... | collective-permute-start | bytes 294920 | tf_op jit(solution)/shard_map/ppermute | solution.py:33
  44.8 5.2 %collective-permute-start.17 = (bf16[16,3072]{1,0:T(8,128)(2,1)S(1)}, bf16[16,3072]{1,0:T(8,128)(2,1)S(1)}, u32[]{:S(2)}, u32[]{:S(2)}) collective-permute-start(bf16[16,3072]{1,0:T(8,128)(2,1)S(1)} %collective-permute-done.12.refs_0_), channel_id=1, source_target_pairs={{0,2},{1,3},{2,0},{3,1},{4,6},{5,7},{6,4},{7,5},{8,10},{9,11},{10,... | collective-permute-start | bytes 294920 | tf_op jit(solution)/shard_map/ppermute | solution.py:33
  45.8 4.9 %collective-permute-start.20 = (bf16[16,3072]{1,0:T(8,128)(2,1)S(1)}, bf16[16,3072]{1,0:T(8,128)(2,1)S(1)}, u32[]{:S(2)}, u32[]{:S(2)}) collective-permute-start(bf16[16,3072]{1,0:T(8,128)(2,1)S(1)} %collective-permute-done.12.refs_0_), channel_id=1, source_target_pairs={{0,1},{1,0},{2,3},{3,2},{4,5},{5,4},{6,7},{7,6},{8,9},{9,8},{10,11... | collective-permute-start | bytes 294920 | tf_op jit(solution)/shard_map/ppermute | solution.py:33
  50.0 1.3 %collective-permute-start.21 = (bf16[16,3072]{1,0:T(8,128)(2,1)S(1)}, bf16[16,3072]{1,0:T(8,128)(2,1)S(1)}, u32[]{:S(2)}, u32[]{:S(2)}) collective-permute-start(bf16[16,3072]{1,0:T(8,128)(2,1)S(1)} %collective-permute-done.17.refs_1_), channel_id=1, source_target_pairs={{0,1},{1,0},{2,3},{3,2},{4,5},{5,4},{6,7},{7,6},{8,9},{9,8},{10,11... | collective-permute-start | bytes 294920 | tf_op jit(solution)/shard_map/ppermute | solution.py:33
  50.1 1.4 %collective-permute-start.22 = (bf16[16,3072]{1,0:T(8,128)(2,1)S(1)}, bf16[16,3072]{1,0:T(8,128)(2,1)S(1)}, u32[]{:S(2)}, u32[]{:S(2)}) collective-permute-start(bf16[16,3072]{1,0:T(8,128)(2,1)S(1)} %collective-permute-done.18.refs_2_), channel_id=1, source_target_pairs={{0,1},{1,0},{2,3},{3,2},{4,5},{5,4},{6,7},{7,6},{8,9},{9,8},{10,11... | collective-permute-start | bytes 294920 | tf_op jit(solution)/shard_map/ppermute | solution.py:33
  50.6 1.3 %collective-permute-start.23 = (bf16[16,3072]{1,0:T(8,128)(2,1)S(1)}, bf16[16,3072]{1,0:T(8,128)(2,1)S(1)}, u32[]{:S(2)}, u32[]{:S(2)}) collective-permute-start(bf16[16,3072]{1,0:T(8,128)(2,1)S(1)} %collective-permute-done.19.refs_3_), channel_id=1, source_target_pairs={{0,1},{1,0},{2,3},{3,2},{4,5},{5,4},{6,7},{7,6},{8,9},{9,8},{10,11... | collective-permute-start | bytes 294920 | tf_op jit(solution)/shard_map/ppermute | solution.py:33
  (5 other events, 37.9 us)

commit v4 on v3

--- a/solution.py
+++ b/solution.py
@@ -12,11 +12,13 @@
 LANES = 128
 BLOCK = 8
 TILE = 512
+WIDE = 1024
 SIDE = 32
 AHEAD = 3
 PACE = 1
 QUAD = 4
 PARTS = 4
+LOADS = (11, 16)
 EPSILON = 1e-05
 VMEM = pl.BlockSpec(memory_space=pltpu.VMEM)
 SMEM = pl.BlockSpec(memory_space=pltpu.SMEM)
@@ -88,19 +90,23 @@
 
 
 def project_kernel(order, me_ref, x_hbm, gain_hbm, wq_hbm, wkv_hbm, keep_ref, send_ref, stats_ref,
-                   extra_ref, x_ref, gain_ref, rows_ref, lhs_ref, w_ref, in_sem, w_sem):
+                   extra_ref, x_ref, gain_ref, rows_ref, lhs_ref, wkv_ref, w_ref, in_sem,
+                   w_sem):
     total = x_ref.shape[0]
     half = total // 2
     me = me_ref[0]
-    tiles = w_ref.shape[0]
+    tiles = w_sem.shape[0]
     x_copy = pltpu.make_async_copy(x_hbm, x_ref, in_sem.at[0])
     gain_copy = pltpu.make_async_copy(gain_hbm, gain_ref, in_sem.at[1])
     x_copy.start()
     gain_copy.start()
     copies = []
     for t in range(tiles):
-        source = wkv_hbm if t == 0 else wq_hbm.at[:, (t - 1) * TILE : t * TILE]
-        copies.append(pltpu.make_async_copy(source, w_ref.at[t], w_sem.at[t]))
+        if t == 0:
+            source, target = wkv_hbm, wkv_ref
+        else:
+            source, target = wq_hbm.at[:, (t - 1) * WIDE : t * WIDE], w_ref.at[t - 1]
+        copies.append(pltpu.make_async_copy(source, target, w_sem.at[t]))
     started = min(AHEAD, tiles)
     for t in range(started):
         copies[t].start()
@@ -135,28 +141,33 @@
         else:
             extra_ref[at - half : at - half + 2 * BLOCK, :] = stats
 
-    chunks = tiles * (TILE // LANES) // 2
+    chunks = keep_ref.shape[1] // LANES // 2
+    at_column = 0
     for t in range(tiles):
         while started < min(tiles, t + AHEAD + 4):
             copies[started].start()
             started += 1
         copies[t].wait()
-        out = jnp.dot(lhs_ref[...], w_ref[t], preferred_element_type=jnp.float32)
-        columns = slice(t * TILE, (t + 1) * TILE)
-        keep_ref[:, columns] = out[:half]
-        send_ref[:, columns] = out[half:total].astype(jnp.bfloat16)
-        gained = out[total : total + 1] + out[total + 1 : total + 2]
-        for k in range(TILE // LANES):
-            c = t * (TILE // LANES) + k
-            at = half + c if c < chunks else half + SIDE + c - chunks
-            extra_ref[at : at + 1, :] = gained[:, k * LANES : (k + 1) * LANES]
+        weights = wkv_ref if t == 0 else w_ref.at[t - 1]
+        for start in range(0, weights.shape[1], TILE):
+            out = jnp.dot(
+                lhs_ref[...], weights[:, start : start + TILE], preferred_element_type=jnp.float32
+            )
+            columns = slice(at_column, at_column + TILE)
+            keep_ref[:, columns] = out[:half]
+            send_ref[:, columns] = out[half:total].astype(jnp.bfloat16)
+            gained = out[total : total + 1] + out[total + 1 : total + 2]
+            for k in range(TILE // LANES):
+                c = at_column // LANES + k
+                at = half + c if c < chunks else half + SIDE + c - chunks
+                extra_ref[at : at + 1, :] = gained[:, k * LANES : (k + 1) * LANES]
+            at_column += TILE
 
 
 def project(me, order, residual, gain, w_query, w_keyval):
     total, depth = residual.shape
     width = w_query.shape[1] + w_keyval.shape[1]
     half = total // 2
-    tiles = width // TILE
     return pl.pallas_call(
         functools.partial(project_kernel, order),
         in_specs=[SMEM] + [pl.BlockSpec(memory_space=pltpu.HBM)] * 4,
@@ -172,9 +183,10 @@
             pltpu.VMEM((depth,), jnp.float32),
             pltpu.VMEM((total, depth), jnp.float32),
             pltpu.VMEM((total + 16, depth), jnp.bfloat16),
-            pltpu.VMEM((tiles, depth, TILE), jnp.bfloat16),
+            pltpu.VMEM((depth, w_keyval.shape[1]), jnp.bfloat16),
+            pltpu.VMEM((w_query.shape[1] // WIDE, depth, WIDE), jnp.bfloat16),
             pltpu.SemaphoreType.DMA((2,)),
-            pltpu.SemaphoreType.DMA((tiles,)),
+            pltpu.SemaphoreType.DMA((1 + w_query.shape[1] // WIDE,)),
         ],
         compiler_params=pltpu.CompilerParams(vmem_limit_bytes=24 * 2**20),
         name="project",
@@ -442,12 +454,14 @@
     )
 
 
-def load_kernel(w_hbm, after_ref, out_ref, token_ref, sems):
+def load_kernel(base, w_hbm, after_ref, out_ref, token_ref, sems):
     parts = sems.shape[0]
     rows = out_ref.shape[0] // parts
     copies = [
         pltpu.make_async_copy(
-            w_hbm.at[k * rows : (k + 1) * rows, :], out_ref.at[k * rows : (k + 1) * rows, :], sems.at[k]
+            w_hbm.at[base + k * rows : base + (k + 1) * rows, :],
+            out_ref.at[k * rows : (k + 1) * rows, :],
+            sems.at[k],
         )
         for k in range(parts)
     ]
@@ -458,19 +472,19 @@
     token_ref[...] = jnp.zeros_like(token_ref)
 
 
-def load(w_output, after):
-    return pl.pallas_call(
-        load_kernel,
+def load(begin, end, w_output, after):
+    return pl.pallas_call(
+        functools.partial(load_kernel, begin),
         in_specs=[pl.BlockSpec(memory_space=pltpu.HBM), pl.BlockSpec(memory_space=pl.ANY)],
         out_specs=[VMEM] * 2,
         out_shape=[
-            struct((w_output.shape[0] // 2, w_output.shape[1]), w_output.dtype),
+            struct((end - begin, w_output.shape[1]), w_output.dtype),
             struct((BLOCK, LANES), jnp.float32),
         ],
         scratch_shapes=[pltpu.SemaphoreType.DMA((PARTS,))],
         compiler_params=pltpu.CompilerParams(vmem_limit_bytes=16 * 2**20),
         cost_estimate=pl.CostEstimate(
-            flops=0, bytes_accessed=w_output.size, transcendentals=0
+            flops=0, bytes_accessed=2 * (end - begin) * w_output.shape[1], transcendentals=0
         ),
         name="load",
     )(in_hbm(w_output), after)
@@ -479,95 +493,99 @@
 def unfold(lhs_ref, pieces):
     cut = pieces[0].shape[1]
     for k in range(0, len(pieces), 2):
-        pair = [p[...].astype(jnp.float32) for p in pieces[k : k + 2]]
+        pair = [p.astype(jnp.float32) for p in pieces[k : k + 2]]
         at = slice(k * BLOCK, (k + 2) * BLOCK)
         lhs_ref[at, :cut] = jnp.concatenate([p[:BLOCK] for p in pair], axis=0).astype(jnp.bfloat16)
         lhs_ref[at, cut:] = jnp.concatenate([p[BLOCK:] for p in pair], axis=0).astype(jnp.bfloat16)
 
 
-def near_output_kernel(first_ref, w_hbm, *refs):
-    pieces, (out_ref, second_ref, lhs_ref, sems) = refs[:-4], refs[-4:]
-    depth = second_ref.shape[0]
-    rows = depth // PARTS
-    copies = [
-        pltpu.make_async_copy(
-            w_hbm.at[depth + k * rows : depth + (k + 1) * rows, :],
-            second_ref.at[k * rows : (k + 1) * rows, :],
-            sems.at[k],
+def unfold_kernel(*refs):
+    fold = 2 * BLOCK
+    unfold(
+        refs[-1],
+        [r[k : k + fold, :] for r in refs[:-1] for k in range(0, r.shape[0], fold)],
+    )
+
+
+def stack_kernel(*refs):
+    at = 0
+    for r in refs[:-1]:
+        refs[-1][at : at + r.shape[0], :] = r[...]
+        at += r.shape[0]
+
+
+def stack(pieces):
+    return pl.pallas_call(
+        stack_kernel,
+        in_specs=[VMEM] * len(pieces),
+        out_specs=VMEM,
+        out_shape=struct((sum(p.shape[0] for p in pieces), pieces[0].shape[1]), jnp.bfloat16),
+        compiler_params=pltpu.CompilerParams(vmem_limit_bytes=16 * 2**20),
+        name="stack",
+    )(*pieces)
+
+
+def unfold_rows(pieces):
+    return pl.pallas_call(
+        unfold_kernel,
+        in_specs=[VMEM] * len(pieces),
+        out_specs=VMEM,
+        out_shape=struct(
+            (sum(p.shape[0] for p in pieces) // 2, 2 * pieces[0].shape[1]), jnp.bfloat16
+        ),
+        compiler_params=pltpu.CompilerParams(vmem_limit_bytes=16 * 2**20),
+        name="unfold_rows",
+    )(*pieces)
+
+
+def output_kernel(order, parts, me_ref, x_ref, *refs):
+    weights, refs = refs[:parts], refs[parts:]
+    pieces, (out_hbm, rows_ref, sum_ref, sems) = refs[:-4], refs[-4:]
+    me = me_ref[0]
+    width = x_ref.shape[1]
+    rows_ref[...] = x_ref[...].astype(jnp.float32)
+    copies = []
+    for k, left in enumerate(range(0, width, TILE)):
+        columns = slice(left, min(left + TILE, width))
+        total = 0.0
+        begin = 0
+        for w in weights:
+            end = begin + w.shape[0]
+            total = total + jnp.dot(
+                jnp.concatenate([p[:, begin:end] for p in pieces], axis=0),
+                w[:, columns],
+                preferred_element_type=jnp.float32,
+            )
+            begin = end
+        sum_ref[:, columns] = total
+        for p, b in enumerate(order):
+            at = pl.ds(pl.multiple_of((me ^ b) * BLOCK, BLOCK), BLOCK)
+            rows_ref[at, columns] = (
+                rows_ref[at, columns] + sum_ref[p * BLOCK : (p + 1) * BLOCK, columns]
+            )
+        copies.append(
+            pltpu.make_async_copy(rows_ref.at[:, columns], out_hbm.at[:, columns], sems.at[k])
         )
-        for k in range(PARTS)
-    ]
+        copies[-1].start()
     for copy in copies:
-        copy.start()
-    unfold(lhs_ref, pieces)
-    out_ref[...] = jnp.dot(
-        lhs_ref[:, :depth], first_ref[...], preferred_element_type=jnp.float32
-    )
-    for k in range(PARTS):
-        copies[k].wait()
-        out_ref[...] += jnp.dot(
-            lhs_ref[:, depth + k * rows : depth + (k + 1) * rows],
-            second_ref[k * rows : (k + 1) * rows, :],
-            preferred_element_type=jnp.float32,
-        )
-
-
-def near_output(pieces, first, w_output):
-    rows = len(pieces) * BLOCK
-    depth, width = w_output.shape
-    return pl.pallas_call(
-        near_output_kernel,
-        in_specs=[VMEM, pl.BlockSpec(memory_space=pltpu.HBM)] + [VMEM] * len(pieces),
-        out_specs=[VMEM] * 2,
-        out_shape=[
-            struct((rows, width), jnp.float32),
-            struct((depth // 2, width), w_output.dtype),
-        ],
+        copy.wait()
+
+
+def output(me, order, pieces, residual, weights):
+    total, width = residual.shape
+    return pl.pallas_call(
+        functools.partial(output_kernel, order, len(weights)),
+        in_specs=[SMEM] + [VMEM] * (1 + len(weights) + len(pieces)),
+        out_specs=pl.BlockSpec(memory_space=pltpu.HBM),
+        out_shape=struct((total, width), jnp.float32),
         scratch_shapes=[
-            pltpu.VMEM((rows, depth), jnp.bfloat16),
-            pltpu.SemaphoreType.DMA((PARTS,)),
+            pltpu.VMEM((total, width), jnp.float32),
+            pltpu.VMEM((total, width), jnp.float32),
+            pltpu.SemaphoreType.DMA((-(-width // TILE),)),
         ],
         compiler_params=pltpu.CompilerParams(vmem_limit_bytes=24 * 2**20),
-        cost_estimate=pl.CostEstimate(
-            flops=2 * rows * depth * width, bytes_accessed=w_output.size, transcendentals=0
-        ),
-        name="near_output",
-    )(first, in_hbm(w_output), *pieces)
-
-
-def far_output_kernel(near_order, far_order, me_ref, near_ref, x_ref, first_ref, second_ref, *refs):
-    pieces, (out_ref, lhs_ref, rows_ref, sum_ref) = refs[:-4], refs[-4:]
-    me = me_ref[0]
-    rows_ref[...] = x_ref[...].astype(jnp.float32)
-    for p, b in enumerate(near_order):
-        at = pl.ds(pl.multiple_of((me ^ b) * BLOCK, BLOCK), BLOCK)
-        out_ref[at, :] = rows_ref[at, :] + near_ref[p * BLOCK : (p + 1) * BLOCK, :]
-    unfold(lhs_ref, pieces)
-    depth = first_ref.shape[0]
-    sum_ref[...] = jnp.dot(
-        lhs_ref[:, :depth], first_ref[...], preferred_element_type=jnp.float32
-    ) + jnp.dot(lhs_ref[:, depth:], second_ref[...], preferred_element_type=jnp.float32)
-    for p, b in enumerate(far_order):
-        at = pl.ds(pl.multiple_of((me ^ b) * BLOCK, BLOCK), BLOCK)
-        out_ref[at, :] = rows_ref[at, :] + sum_ref[p * BLOCK : (p + 1) * BLOCK, :]
-
-
-def far_output(me, orders, near, pieces, residual, weights):
-    total, width = residual.shape
-    rows = len(pieces) * BLOCK
-    return pl.pallas_call(
-        functools.partial(far_output_kernel, *orders),
-        in_specs=[SMEM] + [VMEM] * (4 + len(pieces)),
-        out_specs=VMEM,
-        out_shape=struct((total, width), jnp.float32),
-        scratch_shapes=[
-            pltpu.VMEM((rows, 2 * weights[0].shape[0]), jnp.bfloat16),
-            pltpu.VMEM((total, width), jnp.float32),
-            pltpu.VMEM((rows, width), jnp.float32),
-        ],
-        compiler_params=pltpu.CompilerParams(vmem_limit_bytes=24 * 2**20),
-        name="far_output",
-    )(me, near, residual, *weights, *pieces)
+        name="output",
+    )(me, residual, *weights, *pieces)
 
 
 def local(
@@ -592,36 +610,35 @@
     far = far_add(far, early[-1])
     summed, *far_sends = far_combine(far, far_stats, side, early)
     late = [exchange(v, m, count) for v, m in zip(sends[QUAD - 1 :], quad_masks)]
-    first, token = load(w_output, summed)
+    depth = w_output.shape[0]
+    cuts = [0] + [depth * part // 16 for part in LOADS]
+    first, token = load(cuts[0], cuts[1], w_output, summed)
     far_sums = [exchange(v, m, count) for v, m in zip(far_sends, far_masks)]
     attended, new_keyval = attend(
         lengths, token, own, own_stats, side, summed, tables, key_cache, value_cache, early, late,
         far_sums, heads,
     )
 
-    far_pieces = [exchange(attended, m, count) for m in far_masks]
-    copied = attended
-    near_pieces = [attended] + [exchange(copied, m, count) for m in quad_masks]
-    far_pieces = [
-        piece if mask == 0 else exchange(piece, mask, count)
-        for piece in far_pieces
-        for mask in [0] + quad_masks
-    ]
-    near_order = [core + 2 * q for core in range(2) for q in range(QUAD)]
+    near_masks, diagonal_mask = quad_masks[:-1], quad_masks[-1]
+    far_own = [exchange(attended, m, count) for m in far_masks]
+    near_pieces = [attended] + [exchange(attended, m, count) for m in near_masks] + far_own
+    far_pieces = [exchange(piece, mask, count) for piece in far_own for mask in near_masks]
+    far_pieces += [exchange(p, diagonal_mask, count) for p in [attended] + far_own]
+    near_order = [[core + b for b in [0] + near_masks + far_masks] for core in range(2)]
     far_order = [
-        core + 2 * q + 2 * QUAD * g
+        [core + b for b in [far + near for far in far_masks for near in near_masks]
+         + [far + diagonal_mask for far in [0] + far_masks]]
         for core in range(2)
-        for g in range(1, groups)
-        for q in range(QUAD)
-    ]
-    near_pieces += [exchange(behind(p, far_pieces[0]), 1, count) for p in near_pieces]
-    near, second = near_output(near_pieces, first, w_output)
-    far_pieces += [
-        exchange(p if k % QUAD == 0 else behind(p, near), 1, count)
-        for k, p in enumerate(far_pieces)
-    ]
-    updated = far_output(
-        me, (near_order, far_order), near, far_pieces, residual, (first, second)
+    ]
+    second, token = load(cuts[1], cuts[2], w_output, far_own[0])
+    near_rows = unfold_rows([behind(p, token) for p in near_pieces])
+    far_rows = unfold_rows([behind(p, token) for p in far_pieces])
+    updated = output(
+        me,
+        near_order[0] + near_order[1] + far_order[0] + far_order[1],
+        [near_rows, exchange(near_rows, 1, count), far_rows, exchange(far_rows, 1, count)],
+        residual,
+        (first, second),
     )
     return (updated, new_keyval)
 

time: 55.4 us -> 51.5 us (0.930)
  waiting for transfers between devices: 9.98 us -> 7.76 us
  starting transfers between devices: 24.1 us -> 23.2 us
  Pallas kernels: 20.2 us -> 19.5 us
    ppermute x24 -> x18, waiting for transfers between devices: 9.98 us -> 7.76 us  [exchange(): return lax.ppermute(value, 'gx', [(i, i ^ mask) for i in range(count)])]
    ppermute x24 -> x18, starting transfers between devices: 24.1 us -> 23.2 us  [exchange(): return lax.ppermute(value, 'gx', [(i, i ^ mask) for i in range(count)])]
    pallas_call x3 -> x5, Pallas kernels: 10.4 us -> 9.92 us  [the longest x2 6.9 us: load(): pl.pallas_call(functools.partial(load_kernel, begin), in_specs=[pl.BlockS...]
  transfers between devices with their start and end apart: 24 -> 18, of which waited for: 11 -> 8; matrix products, arithmetic and copies ran while one was open for 0% -> 0% of each run, Pallas kernels for 13% -> 14%
where the time goes in v4:
time: 51.5 us; the launch traced here: 51.4 us
  starting transfers between devices  23.2 us (45%)
  Pallas kernels  19.5 us (38%)
  waiting for transfers between devices  7.76 us (15%)
  between operations  0.81 us (2%)
    ppermute x18, starting transfers between devices, exchange(): return lax.ppermute(value, 'gx', [(i, i ^ mask) for i in range(count)])  23.2 us
    ppermute x18, waiting for transfers between devices, exchange(): return lax.ppermute(value, 'gx', [(i, i ^ mask) for i in range(count)])  7.76 us
    pallas_call x2, Pallas kernels, load(): pl.pallas_call(functools.partial(load_kernel, begin), in_specs=[pl.BlockS...  6.9 us
    pallas_call x1, Pallas kernels, project(): pl.pallas_call(functools.partial(project_kernel, order), in_specs=[SMEM]...  6.46 us
    pallas_call x1, Pallas kernels, output(): pl.pallas_call(functools.partial(output_kernel, order, len(weights)), in_...  2.97 us
    pallas_call x1, Pallas kernels, attend(): pl.pallas_call(functools.partial(attend_kernel, heads), in_specs=[SMEM, p...  2.45 us
  transfers between devices with their start and end apart: 18, of which 8 were waited for; matrix products, arithmetic and copies ran while one was open for 0% of the time, Pallas kernels for 14%

profile of v4, /device:TPU:0, one launch (start us, length us, event | category | flops | bytes accessed | tf_op | source)
XLA Modules:
  0.0 51.4 jit_solution(16940726415418307447)
XLA Ops:
  0.6 6.5 %project.1 = (f32[64,6656]{1,0:T(8,128)S(1)}, bf16[64,6656]{1,0:T(8,128)(2,1)S(1)}, f32[64,128]{1,0:T(8,128)S(1)}, f32[128,128]{1,0:T(8,128)S(1)}) custom-call(s32[1]{0:T(128)} %bitcast.me_ref, bf16[128,1152]{1,0:T(8,128)(2,1)} %x_ref.1, f32[1152]{0:T(1024)} %gain_hbm.1, bf16[1152,6144]{1,0:T(8,128)(2,1)} %wq_hbm.1, bf16[1152,512]{1,0:T(8,128)(2,1)} %wkv_hbm.1), custom_call_target="tpu_custom_call" | custom-call | tf_op jit(solution)/shard_map/project/pallas_call | solution.py:171
  7.1 0.5 %collective-permute-start = (bf16[64,6656]{1,0:T(8,128)(2,1)S(1)}, bf16[64,6656]{1,0:T(8,128)(2,1)S(1)}, u32[]{:S(2)}, u32[]{:S(2)}) collective-permute-start(bf16[64,6656]{1,0:T(8,128)(2,1)S(1)} %get-tuple-element.34), channel_id=1, source_target_pairs={{0,1},{1,0},{2,3},{3,2},{4,5},{5,4},{6,7},{7,6},{8,9},{9,8},{10,11... | collective-permute-start | bytes 2555912 | tf_op jit(solution)/shard_map/ppermute | solution.py:35
  7.7 2.0 %collective-permute-done.1.other_ref = f32[128,128]{1,0:T(8,128)S(1)} collective-permute-done((f32[128,128]{1,0:T(8,128)S(1)}, f32[128,128]{1,0:T(8,128)S(1)}, u32[]{:S(2)}, u32[]{:S(2)}) %collective-permute-start.1) | collective-permute-done | bytes 65568 | tf_op jit(solution)/shard_map/ppermute | solution.py:35
  10.1 4.0 %collective-permute-start.2 = (bf16[16,3968]{1,0:T(8,128)(2,1)S(1)}, bf16[16,3968]{1,0:T(8,128)(2,1)S(1)}, u32[]{:S(2)}, u32[]{:S(2)}) collective-permute-start(bf16[16,3968]{1,0:T(8,128)(2,1)S(1)} %get-tuple-element.38), channel_id=1, source_target_pairs={{0,6},{1,7},{2,4},{3,5},{4,2},{5,3},{6,0},{7,1},{8,14},{9,15},{10,... | collective-permute-start | bytes 380936 | tf_op jit(solution)/shard_map/ppermute | solution.py:35
  14.0 0.5 collective-permute-start.3
  14.7 1.9 %collective-permute-start.5 = (bf16[16,3456]{1,0:T(8,128)(2,1)S(1)}, bf16[16,3456]{1,0:T(8,128)(2,1)S(1)}, u32[]{:S(2)}, u32[]{:S(2)}) collective-permute-start(bf16[16,3456]{1,0:T(8,128)(2,1)S(1)} %get-tuple-element.48), channel_id=1, source_target_pairs={{0,2},{1,3},{2,0},{3,1},{4,6},{5,7},{6,4},{7,5},{8,10},{9,11},{10,... | collective-permute-start | bytes 331784 | tf_op jit(solution)/shard_map/ppermute | solution.py:35
  16.6 1.6 %collective-permute-start.6 = (bf16[16,3456]{1,0:T(8,128)(2,1)S(1)}, bf16[16,3456]{1,0:T(8,128)(2,1)S(1)}, u32[]{:S(2)}, u32[]{:S(2)}) collective-permute-start(bf16[16,3456]{1,0:T(8,128)(2,1)S(1)} %get-tuple-element.49), channel_id=1, source_target_pairs={{0,4},{1,5},{2,6},{3,7},{4,0},{5,1},{6,2},{7,3},{8,12},{9,13},{10,... | collective-permute-start | bytes 331784 | tf_op jit(solution)/shard_map/ppermute | solution.py:35
  18.2 3.1 %collective-permute-start.7 = (bf16[16,3456]{1,0:T(8,128)(2,1)S(1)}, bf16[16,3456]{1,0:T(8,128)(2,1)S(1)}, u32[]{:S(2)}, u32[]{:S(2)}) collective-permute-start(bf16[16,3456]{1,0:T(8,128)(2,1)S(1)} %get-tuple-element.50), channel_id=1, source_target_pairs={{0,6},{1,7},{2,4},{3,5},{4,2},{5,3},{6,0},{7,1},{8,14},{9,15},{10,... | collective-permute-start | bytes 331784 | tf_op jit(solution)/shard_map/ppermute | solution.py:35
  21.8 2.7 %collective-permute-start.8 = (bf16[16,3968]{1,0:T(8,128)(2,1)S(1)}, bf16[16,3968]{1,0:T(8,128)(2,1)S(1)}, u32[]{:S(2)}, u32[]{:S(2)}) collective-permute-start(bf16[16,3968]{1,0:T(8,128)(2,1)S(1)} %get-tuple-element.51), channel_id=1, source_target_pairs={{0,8},{1,9},{2,10},{3,11},{4,12},{5,13},{6,14},{7,15},{8,0},{9,1},... | collective-permute-start | bytes 380936 | tf_op jit(solution)/shard_map/ppermute | solution.py:35
  24.6 4.0 %load.2 = (bf16[4224,1152]{1,0:T(8,128)(2,1)S(1)}, f32[8,128]{1,0:T(8,128)S(1)}) custom-call(bf16[6144,1152]{1,0:T(8,128)(2,1)} %w_hbm.3, f32[16,512]{1,0:T(8,128)S(1)} %get-tuple-element.43.after_ref.summed_ref), custom_call_target="tpu_custom_call" | custom-call | bytes 9732096 | tf_op jit(solution)/shard_map/load/pallas_call | solution.py:476
  28.6 1.7 %collective-permute-done.8.refs_6_ = bf16[16,3968]{1,0:T(8,128)(2,1)S(1)} collective-permute-done((bf16[16,3968]{1,0:T(8,128)(2,1)S(1)}, bf16[16,3968]{1,0:T(8,128)(2,1)S(1)}, u32[]{:S(2)}, u32[]{:S(2)}) %collective-permute-start.8) | collective-permute-done | bytes 127008 | tf_op jit(solution)/shard_map/ppermute | solution.py:35
  30.4 2.4 %attend.1 = (bf16[16,3072]{1,0:T(8,128)(2,1)S(1)}, f32[8,512]{1,0:T(8,128)}) custom-call(s32[8]{0:T(128)S(1)} %copy-done.3, f32[8,128]{1,0:T(8,128)S(1)} %get-tuple-element.45.after_ref, f32[16,3328]{1,0:T(8,128)S(1)} %get-tuple-element.46.own_ref, f32[16,128]{1,0:T(8,128)S(1)} %get-tuple-element.47.stats_ref, f32[64,128]{1,0:T(8,128)S(1)} %get-tuple-element.40.side_ref, ...), custom_call_target="tpu_custom_call" | custom-call | tf_op jit(solution)/shard_map/attend/pallas_call | solution.py:437
  33.2 2.9 %collective-permute-start.15 = (bf16[16,3072]{1,0:T(8,128)(2,1)S(1)}, bf16[16,3072]{1,0:T(8,128)(2,1)S(1)}, u32[]{:S(2)}, u32[]{:S(2)}) collective-permute-start(bf16[16,3072]{1,0:T(8,128)(2,1)S(1)} %get-tuple-element.55.refs_0_), channel_id=1, source_target_pairs={{0,6},{1,7},{2,4},{3,5},{4,2},{5,3},{6,0},{7,1},{8,14},{9,15},{10,... | collective-permute-start | bytes 294920 | tf_op jit(solution)/shard_map/ppermute | solution.py:35
  36.0 0.5 collective-permute-start.11
  36.5 1.5 %collective-permute-start.10 = (bf16[16,3072]{1,0:T(8,128)(2,1)S(1)}, bf16[16,3072]{1,0:T(8,128)(2,1)S(1)}, u32[]{:S(2)}, u32[]{:S(2)}) collective-permute-start(bf16[16,3072]{1,0:T(8,128)(2,1)S(1)} %get-tuple-element.55.refs_0_), channel_id=1, source_target_pairs={{0,2},{1,3},{2,0},{3,1},{4,6},{5,7},{6,4},{7,5},{8,10},{9,11},{10,... | collective-permute-start | bytes 294920 | tf_op jit(solution)/shard_map/ppermute | solution.py:35
  38.0 1.1 %collective-permute-done.9.after_ref.refs_3_ = bf16[16,3072]{1,0:T(8,128)(2,1)S(1)} collective-permute-done((bf16[16,3072]{1,0:T(8,128)(2,1)S(1)}, bf16[16,3072]{1,0:T(8,128)(2,1)S(1)}, u32[]{:S(2)}, u32[]{:S(2)}) %collective-permute-start.9) | collective-permute-done | bytes 98336 | tf_op jit(solution)/shard_map/ppermute | solution.py:35
  39.1 0.7 %collective-permute-start.16 = (bf16[16,3072]{1,0:T(8,128)(2,1)S(1)}, bf16[16,3072]{1,0:T(8,128)(2,1)S(1)}, u32[]{:S(2)}, u32[]{:S(2)}) collective-permute-start(bf16[16,3072]{1,0:T(8,128)(2,1)S(1)} %collective-permute-done.9.after_ref.refs_3_), channel_id=1, source_target_pairs={{0,6},{1,7},{2,4},{3,5},{4,2},{5,3},{6,0},{7,1},{8,14},{9,15},{10,... | collective-permute-start | bytes 294920 | tf_op jit(solution)/shard_map/ppermute | solution.py:35
  39.8 2.1 %collective-permute-start.14 = (bf16[16,3072]{1,0:T(8,128)(2,1)S(1)}, bf16[16,3072]{1,0:T(8,128)(2,1)S(1)}, u32[]{:S(2)}, u32[]{:S(2)}) collective-permute-start(bf16[16,3072]{1,0:T(8,128)(2,1)S(1)} %collective-permute-done.9.after_ref.refs_3_), channel_id=1, source_target_pairs={{0,4},{1,5},{2,6},{3,7},{4,0},{5,1},{6,2},{7,3},{8,12},{9,13},{10,... | collective-permute-start | bytes 294920 | tf_op jit(solution)/shard_map/ppermute | solution.py:35
  42.0 0.6 %collective-permute-start.13 = (bf16[16,3072]{1,0:T(8,128)(2,1)S(1)}, bf16[16,3072]{1,0:T(8,128)(2,1)S(1)}, u32[]{:S(2)}, u32[]{:S(2)}) collective-permute-start(bf16[16,3072]{1,0:T(8,128)(2,1)S(1)} %collective-permute-done.9.after_ref.refs_3_), channel_id=1, source_target_pairs={{0,2},{1,3},{2,0},{3,1},{4,6},{5,7},{6,4},{7,5},{8,10},{9,11},{10,... | collective-permute-start | bytes 294920 | tf_op jit(solution)/shard_map/ppermute | solution.py:35
  42.6 2.9 %load.3 = (bf16[1920,1152]{1,0:T(8,128)(2,1)S(1)}, f32[8,128]{1,0:T(8,128)}) custom-call(bf16[6144,1152]{1,0:T(8,128)(2,1)} %w_hbm.3, bf16[16,3072]{1,0:T(8,128)(2,1)S(1)} %collective-permute-done.9.after_ref.refs_3_), custom_call_target="tpu_custom_call" | custom-call | bytes 4423680 | tf_op jit(solution)/shard_map/load/pallas_call | solution.py:476
  45.7 0.8 %collective-permute-done.13.refs_0_ = bf16[16,3072]{1,0:T(8,128)(2,1)S(1)} collective-permute-done((bf16[16,3072]{1,0:T(8,128)(2,1)S(1)}, bf16[16,3072]{1,0:T(8,128)(2,1)S(1)}, u32[]{:S(2)}, u32[]{:S(2)}) %collective-permute-start.13) | collective-permute-done | bytes 98336 | tf_op jit(solution)/shard_map/ppermute | solution.py:35
  46.7 0.6 %collective-permute-done.12.refs_3_ = bf16[32,6144]{1,0:T(8,128)(2,1)S(1)} collective-permute-done((bf16[32,6144]{1,0:T(8,128)(2,1)S(1)}, bf16[32,6144]{1,0:T(8,128)(2,1)S(1)}, u32[]{:S(2)}, u32[]{:S(2)}) %collective-permute-start.12) | collective-permute-done | bytes 393248 | tf_op jit(solution)/shard_map/ppermute | solution.py:35
  47.3 1.1 %collective-permute-done.17.refs_5_ = bf16[32,6144]{1,0:T(8,128)(2,1)S(1)} collective-permute-done((bf16[32,6144]{1,0:T(8,128)(2,1)S(1)}, bf16[32,6144]{1,0:T(8,128)(2,1)S(1)}, u32[]{:S(2)}, u32[]{:S(2)}) %collective-permute-start.17) | collective-permute-done | bytes 393248 | tf_op jit(solution)/shard_map/ppermute | solution.py:35
  48.4 3.0 %output.1 = f32[128,1152]{1,0:T(8,128)} custom-call(s32[1]{0:T(128)} %bitcast.me_ref, bf16[128,1152]{1,0:T(8,128)(2,1)S(1)} %copy-done.2, bf16[4224,1152]{1,0:T(8,128)(2,1)S(1)} %get-tuple-element.44.refs_0_, bf16[1920,1152]{1,0:T(8,128)(2,1)S(1)} %get-tuple-element.53.refs_1_, bf16[32,6144]{1,0:T(8,128)(2,1)S(1)} %unfold_rows.2.refs_2_, ...), custom_call_target="tpu_custom_call" | custom-call | tf_op jit(solution)/shard_map/output/pallas_call | solution.py:576
  (35 shorter events, 1.9 us)
Async XLA Ops:
  0.6 14.1 %copy-start.4 = (s32[8]{0:T(128)S(1)}, s32[8]{0:T(128)}, u32[]{:S(2)}) copy-start(s32[8]{0:T(128)} %param.17) | copy-start | bytes 100
  7.1 2.6 %collective-permute-start = (bf16[64,6656]{1,0:T(8,128)(2,1)S(1)}, bf16[64,6656]{1,0:T(8,128)(2,1)S(1)}, u32[]{:S(2)}, u32[]{:S(2)}) collective-permute-start(bf16[64,6656]{1,0:T(8,128)(2,1)S(1)} %get-tuple-element.34), channel_id=1, source_target_pairs={{0,1},{1,0},{2,3},{3,2},{4,5},{5,4},{6,7},{7,6},{8,9},{9,8},{10,11... | collective-permute-start | bytes 2555912 | tf_op jit(solution)/shard_map/ppermute | solution.py:35
  7.6 2.1 %collective-permute-start.1 = (f32[128,128]{1,0:T(8,128)S(1)}, f32[128,128]{1,0:T(8,128)S(1)}, u32[]{:S(2)}, u32[]{:S(2)}) collective-permute-start(f32[128,128]{1,0:T(8,128)S(1)} %get-tuple-element.36.extra_ref), channel_id=1, source_target_pairs={{0,1},{1,0},{2,3},{3,2},{4,5},{5,4},{6,7},{7,6},{8,9},{9,8},{10,11... | collective-permute-start | bytes 196616 | tf_op jit(solution)/shard_map/ppermute | solution.py:35
  10.1 8.1 %collective-permute-start.2 = (bf16[16,3968]{1,0:T(8,128)(2,1)S(1)}, bf16[16,3968]{1,0:T(8,128)(2,1)S(1)}, u32[]{:S(2)}, u32[]{:S(2)}) collective-permute-start(bf16[16,3968]{1,0:T(8,128)(2,1)S(1)} %get-tuple-element.38), channel_id=1, source_target_pairs={{0,6},{1,7},{2,4},{3,5},{4,2},{5,3},{6,0},{7,1},{8,14},{9,15},{10,... | collective-permute-start | bytes 380936 | tf_op jit(solution)/shard_map/ppermute | solution.py:35
  14.0 7.2 %collective-permute-start.3 = (bf16[16,3968]{1,0:T(8,128)(2,1)S(1)}, bf16[16,3968]{1,0:T(8,128)(2,1)S(1)}, u32[]{:S(2)}, u32[]{:S(2)}) collective-permute-start(bf16[16,3968]{1,0:T(8,128)(2,1)S(1)} %get-tuple-element.41), channel_id=1, source_target_pairs={{0,2},{1,3},{2,0},{3,1},{4,6},{5,7},{6,4},{7,5},{8,10},{9,11},{10,... | collective-permute-start | bytes 380936 | tf_op jit(solution)/shard_map/ppermute | solution.py:35
  14.5 6.9 %collective-permute-start.4 = (bf16[16,3968]{1,0:T(8,128)(2,1)S(1)}, bf16[16,3968]{1,0:T(8,128)(2,1)S(1)}, u32[]{:S(2)}, u32[]{:S(2)}) collective-permute-start(bf16[16,3968]{1,0:T(8,128)(2,1)S(1)} %get-tuple-element.42), channel_id=1, source_target_pairs={{0,4},{1,5},{2,6},{3,7},{4,0},{5,1},{6,2},{7,3},{8,12},{9,13},{10,... | collective-permute-start | bytes 380936 | tf_op jit(solution)/shard_map/ppermute | solution.py:35
  14.7 13.9 %collective-permute-start.5 = (bf16[16,3456]{1,0:T(8,128)(2,1)S(1)}, bf16[16,3456]{1,0:T(8,128)(2,1)S(1)}, u32[]{:S(2)}, u32[]{:S(2)}) collective-permute-start(bf16[16,3456]{1,0:T(8,128)(2,1)S(1)} %get-tuple-element.48), channel_id=1, source_target_pairs={{0,2},{1,3},{2,0},{3,1},{4,6},{5,7},{6,4},{7,5},{8,10},{9,11},{10,... | collective-permute-start | bytes 331784 | tf_op jit(solution)/shard_map/ppermute | solution.py:35
  16.6 12.0 %collective-permute-start.6 = (bf16[16,3456]{1,0:T(8,128)(2,1)S(1)}, bf16[16,3456]{1,0:T(8,128)(2,1)S(1)}, u32[]{:S(2)}, u32[]{:S(2)}) collective-permute-start(bf16[16,3456]{1,0:T(8,128)(2,1)S(1)} %get-tuple-element.49), channel_id=1, source_target_pairs={{0,4},{1,5},{2,6},{3,7},{4,0},{5,1},{6,2},{7,3},{8,12},{9,13},{10,... | collective-permute-start | bytes 331784 | tf_op jit(solution)/shard_map/ppermute | solution.py:35
  18.2 10.4 %collective-permute-start.7 = (bf16[16,3456]{1,0:T(8,128)(2,1)S(1)}, bf16[16,3456]{1,0:T(8,128)(2,1)S(1)}, u32[]{:S(2)}, u32[]{:S(2)}) collective-permute-start(bf16[16,3456]{1,0:T(8,128)(2,1)S(1)} %get-tuple-element.50), channel_id=1, source_target_pairs={{0,6},{1,7},{2,4},{3,5},{4,2},{5,3},{6,0},{7,1},{8,14},{9,15},{10,... | collective-permute-start | bytes 331784 | tf_op jit(solution)/shard_map/ppermute | solution.py:35
  21.8 8.6 %collective-permute-start.8 = (bf16[16,3968]{1,0:T(8,128)(2,1)S(1)}, bf16[16,3968]{1,0:T(8,128)(2,1)S(1)}, u32[]{:S(2)}, u32[]{:S(2)}) collective-permute-start(bf16[16,3968]{1,0:T(8,128)(2,1)S(1)} %get-tuple-element.51), channel_id=1, source_target_pairs={{0,8},{1,9},{2,10},{3,11},{4,12},{5,13},{6,14},{7,15},{8,0},{9,1},... | collective-permute-start | bytes 380936 | tf_op jit(solution)/shard_map/ppermute | solution.py:35
  24.5 5.8 %copy-start = (bf16[8,512,256]{2,1,0:T(8,128)(2,1)S(1)}, bf16[8,512,256]{2,1,0:T(8,128)(2,1)}, u32[]{:S(2)}) copy-start(bf16[8,512,256]{2,1,0:T(8,128)(2,1)} %key_ref.1) | copy-start | bytes 6291460
  24.5 5.8 %copy-start.1 = (bf16[8,512,256]{2,1,0:T(8,128)(2,1)S(1)}, bf16[8,512,256]{2,1,0:T(8,128)(2,1)}, u32[]{:S(2)}) copy-start(bf16[8,512,256]{2,1,0:T(8,128)(2,1)} %value_ref.1) | copy-start | bytes 6291460
  24.6 5.8 %copy-start.3 = (s32[8]{0:T(128)S(1)}, s32[8]{0:T(128)}, u32[]{:S(2)}) copy-start(s32[8]{0:T(128)} %length_ref.1) | copy-start | bytes 100
  32.8 15.6 %copy-start.2 = (bf16[128,1152]{1,0:T(8,128)(2,1)S(1)}, bf16[128,1152]{1,0:T(8,128)(2,1)}, u32[]{:S(2)}) copy-start(bf16[128,1152]{1,0:T(8,128)(2,1)} %x_ref.1) | copy-start | bytes 884740
  32.8 6.2 %collective-permute-start.9 = (bf16[16,3072]{1,0:T(8,128)(2,1)S(1)}, bf16[16,3072]{1,0:T(8,128)(2,1)S(1)}, u32[]{:S(2)}, u32[]{:S(2)}) collective-permute-start(bf16[16,3072]{1,0:T(8,128)(2,1)S(1)} %get-tuple-element.55.refs_0_), channel_id=1, source_target_pairs={{0,8},{1,9},{2,10},{3,11},{4,12},{5,13},{6,14},{7,15},{8,0},{9,1},... | collective-permute-start | bytes 294920 | tf_op jit(solution)/shard_map/ppermute | solution.py:35
  33.2 8.8 %collective-permute-start.15 = (bf16[16,3072]{1,0:T(8,128)(2,1)S(1)}, bf16[16,3072]{1,0:T(8,128)(2,1)S(1)}, u32[]{:S(2)}, u32[]{:S(2)}) collective-permute-start(bf16[16,3072]{1,0:T(8,128)(2,1)S(1)} %get-tuple-element.55.refs_0_), channel_id=1, source_target_pairs={{0,6},{1,7},{2,4},{3,5},{4,2},{5,3},{6,0},{7,1},{8,14},{9,15},{10,... | collective-permute-start | bytes 294920 | tf_op jit(solution)/shard_map/ppermute | solution.py:35
  36.0 9.4 %collective-permute-start.11 = (bf16[16,3072]{1,0:T(8,128)(2,1)S(1)}, bf16[16,3072]{1,0:T(8,128)(2,1)S(1)}, u32[]{:S(2)}, u32[]{:S(2)}) collective-permute-start(bf16[16,3072]{1,0:T(8,128)(2,1)S(1)} %get-tuple-element.55.refs_0_), channel_id=1, source_target_pairs={{0,4},{1,5},{2,6},{3,7},{4,0},{5,1},{6,2},{7,3},{8,12},{9,13},{10,... | collective-permute-start | bytes 294920 | tf_op jit(solution)/shard_map/ppermute | solution.py:35
  36.5 9.0 %collective-permute-start.10 = (bf16[16,3072]{1,0:T(8,128)(2,1)S(1)}, bf16[16,3072]{1,0:T(8,128)(2,1)S(1)}, u32[]{:S(2)}, u32[]{:S(2)}) collective-permute-start(bf16[16,3072]{1,0:T(8,128)(2,1)S(1)} %get-tuple-element.55.refs_0_), channel_id=1, source_target_pairs={{0,2},{1,3},{2,0},{3,1},{4,6},{5,7},{6,4},{7,5},{8,10},{9,11},{10,... | collective-permute-start | bytes 294920 | tf_op jit(solution)/shard_map/ppermute | solution.py:35
  39.1 6.5 %collective-permute-start.16 = (bf16[16,3072]{1,0:T(8,128)(2,1)S(1)}, bf16[16,3072]{1,0:T(8,128)(2,1)S(1)}, u32[]{:S(2)}, u32[]{:S(2)}) collective-permute-start(bf16[16,3072]{1,0:T(8,128)(2,1)S(1)} %collective-permute-done.9.after_ref.refs_3_), channel_id=1, source_target_pairs={{0,6},{1,7},{2,4},{3,5},{4,2},{5,3},{6,0},{7,1},{8,14},{9,15},{10,... | collective-permute-start | bytes 294920 | tf_op jit(solution)/shard_map/ppermute | solution.py:35
  39.8 5.9 %collective-permute-start.14 = (bf16[16,3072]{1,0:T(8,128)(2,1)S(1)}, bf16[16,3072]{1,0:T(8,128)(2,1)S(1)}, u32[]{:S(2)}, u32[]{:S(2)}) collective-permute-start(bf16[16,3072]{1,0:T(8,128)(2,1)S(1)} %collective-permute-done.9.after_ref.refs_3_), channel_id=1, source_target_pairs={{0,4},{1,5},{2,6},{3,7},{4,0},{5,1},{6,2},{7,3},{8,12},{9,13},{10,... | collective-permute-start | bytes 294920 | tf_op jit(solution)/shard_map/ppermute | solution.py:35
  42.0 4.6 %collective-permute-start.13 = (bf16[16,3072]{1,0:T(8,128)(2,1)S(1)}, bf16[16,3072]{1,0:T(8,128)(2,1)S(1)}, u32[]{:S(2)}, u32[]{:S(2)}) collective-permute-start(bf16[16,3072]{1,0:T(8,128)(2,1)S(1)} %collective-permute-done.9.after_ref.refs_3_), channel_id=1, source_target_pairs={{0,2},{1,3},{2,0},{3,1},{4,6},{5,7},{6,4},{7,5},{8,10},{9,11},{10,... | collective-permute-start | bytes 294920 | tf_op jit(solution)/shard_map/ppermute | solution.py:35
  45.5 1.8 %collective-permute-start.12 = (bf16[32,6144]{1,0:T(8,128)(2,1)S(1)}, bf16[32,6144]{1,0:T(8,128)(2,1)S(1)}, u32[]{:S(2)}, u32[]{:S(2)}) collective-permute-start(bf16[32,6144]{1,0:T(8,128)(2,1)S(1)} %unfold_rows.2.refs_2_), channel_id=1, source_target_pairs={{0,1},{1,0},{2,3},{3,2},{4,5},{5,4},{6,7},{7,6},{8,9},{9,8},{10,11... | collective-permute-start | bytes 1179656 | tf_op jit(solution)/shard_map/ppermute | solution.py:35
  46.6 1.8 %collective-permute-start.17 = (bf16[32,6144]{1,0:T(8,128)(2,1)S(1)}, bf16[32,6144]{1,0:T(8,128)(2,1)S(1)}, u32[]{:S(2)}, u32[]{:S(2)}) collective-permute-start(bf16[32,6144]{1,0:T(8,128)(2,1)S(1)} %unfold_rows.3.refs_4_), channel_id=1, source_target_pairs={{0,1},{1,0},{2,3},{3,2},{4,5},{5,4},{6,7},{7,6},{8,9},{9,8},{10,11... | collective-permute-start | bytes 1179656 | tf_op jit(solution)/shard_map/ppermute | solution.py:35

commit v5 on v4

--- a/solution.py
+++ b/solution.py
@@ -406,7 +406,7 @@
         * factor
         for r in requests
     ]
-    masked = [jnp.where(slot < length_ref[r], scores[r] * factor, -jnp.inf) for r in requests]
+    masked = [jnp.where(slot < length_ref[r : r + 1, 0:1], scores[r] * factor, -jnp.inf) for r in requests]
     highest = [
         jnp.maximum(jnp.max(masked[r], axis=1, keepdims=True), own_scores[r]) for r in requests
     ]
@@ -436,12 +436,12 @@
            heads):
     return pl.pallas_call(
         functools.partial(attend_kernel, heads),
-        in_specs=[SMEM, pl.BlockSpec(memory_space=pl.ANY)]
+        in_specs=[VMEM, pl.BlockSpec(memory_space=pl.ANY)]
         + [VMEM] * (8 + len(early) + len(late) + len(far)),
         out_specs=[VMEM] * 2,
         out_shape=[
             struct((2 * BLOCK, heads * HD // 2), jnp.bfloat16),
-            struct((BLOCK, 2 * HD), jnp.float32),
+            pltpu.VMEM((BLOCK, 2 * HD), jnp.float32),
         ],
         scratch_shapes=[
             pltpu.VMEM((2, heads * BLOCK, LANES), jnp.float32),
@@ -452,6 +452,37 @@
     )(
         lengths, after, own, stats, side, summed, *tables, key_cache, value_cache, *early, *late, *far
     )
+
+
+def load_and_write_kernel(base, w_hbm, after_ref, value_ref, out_ref, token_ref, value_hbm, sems,
+                          value_sem):
+    write = pltpu.make_async_copy(value_ref, value_hbm, value_sem)
+    write.start()
+    load_kernel(base, w_hbm, after_ref, out_ref, token_ref, sems)
+    write.wait()
+
+
+def load_and_write(begin, end, w_output, after, value):
+    return pl.pallas_call(
+        functools.partial(load_and_write_kernel, begin),
+        in_specs=[
+            pl.BlockSpec(memory_space=pltpu.HBM),
+            pl.BlockSpec(memory_space=pl.ANY),
+            VMEM,
+        ],
+        out_specs=[VMEM] * 2 + [pl.BlockSpec(memory_space=pltpu.HBM)],
+        out_shape=[
+            struct((end - begin, w_output.shape[1]), w_output.dtype),
+            struct((BLOCK, LANES), jnp.float32),
+            struct(value.shape, value.dtype),
+        ],
+        scratch_shapes=[pltpu.SemaphoreType.DMA((PARTS,)), pltpu.SemaphoreType.DMA],
+        compiler_params=pltpu.CompilerParams(vmem_limit_bytes=16 * 2**20),
+        cost_estimate=pl.CostEstimate(
+            flops=0, bytes_accessed=2 * (end - begin) * w_output.shape[1], transcendentals=0
+        ),
+        name="load_and_write",
+    )(in_hbm(w_output), after, value)
 
 
 def load_kernel(base, w_hbm, after_ref, out_ref, token_ref, sems):
@@ -601,6 +632,7 @@
         core + 2 * q + 2 * QUAD * g for core in range(2) for g in range(groups) for q in range(QUAD)
     ]
     tables = rope_tables(positions)
+    limits = jnp.broadcast_to(lengths[:, None], (lengths.shape[0], LANES))
 
     keep, send, stats, extra = project(me, order, residual, norm_gain, w_query, w_keyval)
     recv = exchange(send, 1, count)
@@ -615,7 +647,7 @@
     first, token = load(cuts[0], cuts[1], w_output, summed)
     far_sums = [exchange(v, m, count) for v, m in zip(far_sends, far_masks)]
     attended, new_keyval = attend(
-        lengths, token, own, own_stats, side, summed, tables, key_cache, value_cache, early, late,
+        limits, token, own, own_stats, side, summed, tables, key_cache, value_cache, early, late,
         far_sums, heads,
     )
 
@@ -630,7 +662,9 @@
          + [far + diagonal_mask for far in [0] + far_masks]]
         for core in range(2)
     ]
-    second, token = load(cuts[1], cuts[2], w_output, far_own[0])
+    second, token, new_keyval = load_and_write(
+        cuts[1], cuts[2], w_output, far_own[0], new_keyval
+    )
     near_rows = unfold_rows([behind(p, token) for p in near_pieces])
     far_rows = unfold_rows([behind(p, token) for p in far_pieces])
     updated = output(

time: 51.5 us -> 50.6 us (0.983)
  Pallas kernels: 19.5 us -> 18.6 us
    pallas_call x2 -> x1, Pallas kernels: 6.9 us -> 4.03 us  [load(): pl.pallas_call(functools.partial(load_kernel, begin), in_specs=[pl.BlockS...]
    pallas_call x1 -> x2, Pallas kernels: 2.45 us -> 4.38 us  [the longest x1 2.92 us: load_and_write(): pl.pallas_call(functools.partial(load_and_write_kernel, begin), in_specs=...]
  transfers between devices with their start and end apart: 18 -> 18, of which waited for: 8 -> 7; matrix products, arithmetic and copies ran while one was open for 0% -> 0% of each run, Pallas kernels for 14% -> 15%
where the time goes in v5:
time: 50.6 us; the launch traced here: 50.5 us
  starting transfers between devices  23.2 us (46%)
  Pallas kernels  18.6 us (37%)
  waiting for transfers between devices  7.65 us (15%)
  between operations  0.81 us (2%)
    ppermute x18, starting transfers between devices, exchange(): return lax.ppermute(value, 'gx', [(i, i ^ mask) for i in range(count)])  23.2 us
    ppermute x18, waiting for transfers between devices, exchange(): return lax.ppermute(value, 'gx', [(i, i ^ mask) for i in range(count)])  7.65 us
    pallas_call x1, Pallas kernels, project(): pl.pallas_call(functools.partial(project_kernel, order), in_specs=[SMEM]...  6.46 us
    pallas_call x1, Pallas kernels, load(): pl.pallas_call(functools.partial(load_kernel, begin), in_specs=[pl.BlockS...  4.03 us
    pallas_call x1, Pallas kernels, output(): pl.pallas_call(functools.partial(output_kernel, order, len(weights)), in_...  2.97 us
    pallas_call x1, Pallas kernels, load_and_write(): pl.pallas_call(functools.partial(load_and_write_kernel, begin), in_specs=...  2.92 us
    pallas_call x1, Pallas kernels, attend(): pl.pallas_call(functools.partial(attend_kernel, heads), in_specs=[VMEM, p...  1.46 us
  transfers between devices with their start and end apart: 18, of which 7 were waited for; matrix products, arithmetic and copies ran while one was open for 0% of the time, Pallas kernels for 15%

profile of v5, /device:TPU:0, one launch (start us, length us, event | category | flops | bytes accessed | tf_op | source)
XLA Modules:
  0.0 50.5 jit_solution(13031887724368961303)
XLA Ops:
  0.6 6.5 %project.1 = (f32[64,6656]{1,0:T(8,128)S(1)}, bf16[64,6656]{1,0:T(8,128)(2,1)S(1)}, f32[64,128]{1,0:T(8,128)S(1)}, f32[128,128]{1,0:T(8,128)S(1)}) custom-call(s32[1]{0:T(128)} %bitcast.me_ref, bf16[128,1152]{1,0:T(8,128)(2,1)} %x_ref.1, f32[1152]{0:T(1024)} %gain_hbm.1, bf16[1152,6144]{1,0:T(8,128)(2,1)} %wq_hbm.1, bf16[1152,512]{1,0:T(8,128)(2,1)} %wkv_hbm.1), custom_call_target="tpu_custom_call" | custom-call | tf_op jit(solution)/shard_map/project/pallas_call | solution.py:171
  7.1 0.5 %collective-permute-start = (bf16[64,6656]{1,0:T(8,128)(2,1)S(1)}, bf16[64,6656]{1,0:T(8,128)(2,1)S(1)}, u32[]{:S(2)}, u32[]{:S(2)}) collective-permute-start(bf16[64,6656]{1,0:T(8,128)(2,1)S(1)} %get-tuple-element.35), channel_id=1, source_target_pairs={{0,1},{1,0},{2,3},{3,2},{4,5},{5,4},{6,7},{7,6},{8,9},{9,8},{10,11... | collective-permute-start | bytes 2555912 | tf_op jit(solution)/shard_map/ppermute | solution.py:35
  7.7 2.0 %collective-permute-done.1.other_ref = f32[128,128]{1,0:T(8,128)S(1)} collective-permute-done((f32[128,128]{1,0:T(8,128)S(1)}, f32[128,128]{1,0:T(8,128)S(1)}, u32[]{:S(2)}, u32[]{:S(2)}) %collective-permute-start.1) | collective-permute-done | bytes 65568 | tf_op jit(solution)/shard_map/ppermute | solution.py:35
  10.1 4.0 %collective-permute-start.2 = (bf16[16,3968]{1,0:T(8,128)(2,1)S(1)}, bf16[16,3968]{1,0:T(8,128)(2,1)S(1)}, u32[]{:S(2)}, u32[]{:S(2)}) collective-permute-start(bf16[16,3968]{1,0:T(8,128)(2,1)S(1)} %get-tuple-element.39), channel_id=1, source_target_pairs={{0,6},{1,7},{2,4},{3,5},{4,2},{5,3},{6,0},{7,1},{8,14},{9,15},{10,... | collective-permute-start | bytes 380936 | tf_op jit(solution)/shard_map/ppermute | solution.py:35
  14.0 0.5 collective-permute-start.3
  14.7 1.9 %collective-permute-start.5 = (bf16[16,3456]{1,0:T(8,128)(2,1)S(1)}, bf16[16,3456]{1,0:T(8,128)(2,1)S(1)}, u32[]{:S(2)}, u32[]{:S(2)}) collective-permute-start(bf16[16,3456]{1,0:T(8,128)(2,1)S(1)} %get-tuple-element.49), channel_id=1, source_target_pairs={{0,2},{1,3},{2,0},{3,1},{4,6},{5,7},{6,4},{7,5},{8,10},{9,11},{10,... | collective-permute-start | bytes 331784 | tf_op jit(solution)/shard_map/ppermute | solution.py:35
  16.6 1.6 %collective-permute-start.6 = (bf16[16,3456]{1,0:T(8,128)(2,1)S(1)}, bf16[16,3456]{1,0:T(8,128)(2,1)S(1)}, u32[]{:S(2)}, u32[]{:S(2)}) collective-permute-start(bf16[16,3456]{1,0:T(8,128)(2,1)S(1)} %get-tuple-element.50), channel_id=1, source_target_pairs={{0,4},{1,5},{2,6},{3,7},{4,0},{5,1},{6,2},{7,3},{8,12},{9,13},{10,... | collective-permute-start | bytes 331784 | tf_op jit(solution)/shard_map/ppermute | solution.py:35
  18.2 3.1 %collective-permute-start.7 = (bf16[16,3456]{1,0:T(8,128)(2,1)S(1)}, bf16[16,3456]{1,0:T(8,128)(2,1)S(1)}, u32[]{:S(2)}, u32[]{:S(2)}) collective-permute-start(bf16[16,3456]{1,0:T(8,128)(2,1)S(1)} %get-tuple-element.51), channel_id=1, source_target_pairs={{0,6},{1,7},{2,4},{3,5},{4,2},{5,3},{6,0},{7,1},{8,14},{9,15},{10,... | collective-permute-start | bytes 331784 | tf_op jit(solution)/shard_map/ppermute | solution.py:35
  21.8 2.7 %collective-permute-start.8 = (bf16[16,3968]{1,0:T(8,128)(2,1)S(1)}, bf16[16,3968]{1,0:T(8,128)(2,1)S(1)}, u32[]{:S(2)}, u32[]{:S(2)}) collective-permute-start(bf16[16,3968]{1,0:T(8,128)(2,1)S(1)} %get-tuple-element.52), channel_id=1, source_target_pairs={{0,8},{1,9},{2,10},{3,11},{4,12},{5,13},{6,14},{7,15},{8,0},{9,1},... | collective-permute-start | bytes 380936 | tf_op jit(solution)/shard_map/ppermute | solution.py:35
  24.6 4.0 %load.1 = (bf16[4224,1152]{1,0:T(8,128)(2,1)S(1)}, f32[8,128]{1,0:T(8,128)S(1)}) custom-call(bf16[6144,1152]{1,0:T(8,128)(2,1)} %w_hbm.3, f32[16,512]{1,0:T(8,128)S(1)} %get-tuple-element.44.after_ref.summed_ref), custom_call_target="tpu_custom_call" | custom-call | bytes 9732096 | tf_op jit(solution)/shard_map/load/pallas_call | solution.py:507
  28.6 1.7 %collective-permute-done.8.refs_6_ = bf16[16,3968]{1,0:T(8,128)(2,1)S(1)} collective-permute-done((bf16[16,3968]{1,0:T(8,128)(2,1)S(1)}, bf16[16,3968]{1,0:T(8,128)(2,1)S(1)}, u32[]{:S(2)}, u32[]{:S(2)}) %collective-permute-start.8) | collective-permute-done | bytes 127008 | tf_op jit(solution)/shard_map/ppermute | solution.py:35
  30.5 1.5 %attend.1 = (bf16[16,3072]{1,0:T(8,128)(2,1)S(1)}, f32[8,512]{1,0:T(8,128)S(1)}) custom-call(s32[8,128]{1,0:T(8,128)S(1)} %broadcast_in_dim.2.length_ref, f32[8,128]{1,0:T(8,128)S(1)} %get-tuple-element.46.after_ref, f32[16,3328]{1,0:T(8,128)S(1)} %get-tuple-element.47.own_ref, f32[16,128]{1,0:T(8,128)S(1)} %get-tuple-element.48.stats_ref, ...), custom_call_target="tpu_custom_call" | custom-call | tf_op jit(solution)/shard_map/attend/pallas_call | solution.py:437
  32.3 2.9 %collective-permute-start.15 = (bf16[16,3072]{1,0:T(8,128)(2,1)S(1)}, bf16[16,3072]{1,0:T(8,128)(2,1)S(1)}, u32[]{:S(2)}, u32[]{:S(2)}) collective-permute-start(bf16[16,3072]{1,0:T(8,128)(2,1)S(1)} %get-tuple-element.57.refs_0_), channel_id=1, source_target_pairs={{0,6},{1,7},{2,4},{3,5},{4,2},{5,3},{6,0},{7,1},{8,14},{9,15},{10,... | collective-permute-start | bytes 294920 | tf_op jit(solution)/shard_map/ppermute | solution.py:35
  35.2 0.5 collective-permute-start.11
  35.7 1.5 %collective-permute-start.10 = (bf16[16,3072]{1,0:T(8,128)(2,1)S(1)}, bf16[16,3072]{1,0:T(8,128)(2,1)S(1)}, u32[]{:S(2)}, u32[]{:S(2)}) collective-permute-start(bf16[16,3072]{1,0:T(8,128)(2,1)S(1)} %get-tuple-element.57.refs_0_), channel_id=1, source_target_pairs={{0,2},{1,3},{2,0},{3,1},{4,6},{5,7},{6,4},{7,5},{8,10},{9,11},{10,... | collective-permute-start | bytes 294920 | tf_op jit(solution)/shard_map/ppermute | solution.py:35
  37.1 1.2 %collective-permute-done.9.after_ref.refs_3_ = bf16[16,3072]{1,0:T(8,128)(2,1)S(1)} collective-permute-done((bf16[16,3072]{1,0:T(8,128)(2,1)S(1)}, bf16[16,3072]{1,0:T(8,128)(2,1)S(1)}, u32[]{:S(2)}, u32[]{:S(2)}) %collective-permute-start.9) | collective-permute-done | bytes 98336 | tf_op jit(solution)/shard_map/ppermute | solution.py:35
  38.3 0.5 %collective-permute-start.16 = (bf16[16,3072]{1,0:T(8,128)(2,1)S(1)}, bf16[16,3072]{1,0:T(8,128)(2,1)S(1)}, u32[]{:S(2)}, u32[]{:S(2)}) collective-permute-start(bf16[16,3072]{1,0:T(8,128)(2,1)S(1)} %collective-permute-done.9.after_ref.refs_3_), channel_id=1, source_target_pairs={{0,6},{1,7},{2,4},{3,5},{4,2},{5,3},{6,0},{7,1},{8,14},{9,15},{10,... | collective-permute-start | bytes 294920 | tf_op jit(solution)/shard_map/ppermute | solution.py:35
  38.8 2.3 %collective-permute-start.14 = (bf16[16,3072]{1,0:T(8,128)(2,1)S(1)}, bf16[16,3072]{1,0:T(8,128)(2,1)S(1)}, u32[]{:S(2)}, u32[]{:S(2)}) collective-permute-start(bf16[16,3072]{1,0:T(8,128)(2,1)S(1)} %collective-permute-done.9.after_ref.refs_3_), channel_id=1, source_target_pairs={{0,4},{1,5},{2,6},{3,7},{4,0},{5,1},{6,2},{7,3},{8,12},{9,13},{10,... | collective-permute-start | bytes 294920 | tf_op jit(solution)/shard_map/ppermute | solution.py:35
  41.1 0.7 %collective-permute-start.13 = (bf16[16,3072]{1,0:T(8,128)(2,1)S(1)}, bf16[16,3072]{1,0:T(8,128)(2,1)S(1)}, u32[]{:S(2)}, u32[]{:S(2)}) collective-permute-start(bf16[16,3072]{1,0:T(8,128)(2,1)S(1)} %collective-permute-done.9.after_ref.refs_3_), channel_id=1, source_target_pairs={{0,2},{1,3},{2,0},{3,1},{4,6},{5,7},{6,4},{7,5},{8,10},{9,11},{10,... | collective-permute-start | bytes 294920 | tf_op jit(solution)/shard_map/ppermute | solution.py:35
  41.8 2.9 %load_and_write.1 = (bf16[1920,1152]{1,0:T(8,128)(2,1)S(1)}, f32[8,128]{1,0:T(8,128)}, f32[8,512]{1,0:T(8,128)}) custom-call(bf16[6144,1152]{1,0:T(8,128)(2,1)} %w_hbm.3, bf16[16,3072]{1,0:T(8,128)(2,1)S(1)} %collective-permute-done.9.after_ref.refs_3_, f32[8,512]{1,0:T(8,128)S(1)} %get-tuple-element.54.value_ref), custom_call_target="tpu_custom_call" | custom-call | bytes 4423680 | tf_op jit(solution)/shard_map/load_and_write/pallas_call | solution.py:466
  44.9 0.8 %collective-permute-done.13.refs_0_ = bf16[16,3072]{1,0:T(8,128)(2,1)S(1)} collective-permute-done((bf16[16,3072]{1,0:T(8,128)(2,1)S(1)}, bf16[16,3072]{1,0:T(8,128)(2,1)S(1)}, u32[]{:S(2)}, u32[]{:S(2)}) %collective-permute-start.13) | collective-permute-done | bytes 98336 | tf_op jit(solution)/shard_map/ppermute | solution.py:35
  45.8 0.8 %collective-permute-done.12.refs_3_ = bf16[32,6144]{1,0:T(8,128)(2,1)S(1)} collective-permute-done((bf16[32,6144]{1,0:T(8,128)(2,1)S(1)}, bf16[32,6144]{1,0:T(8,128)(2,1)S(1)}, u32[]{:S(2)}, u32[]{:S(2)}) %collective-permute-start.12) | collective-permute-done | bytes 393248 | tf_op jit(solution)/shard_map/ppermute | solution.py:35
  46.6 0.9 %collective-permute-done.17.refs_5_ = bf16[32,6144]{1,0:T(8,128)(2,1)S(1)} collective-permute-done((bf16[32,6144]{1,0:T(8,128)(2,1)S(1)}, bf16[32,6144]{1,0:T(8,128)(2,1)S(1)}, u32[]{:S(2)}, u32[]{:S(2)}) %collective-permute-start.17) | collective-permute-done | bytes 393248 | tf_op jit(solution)/shard_map/ppermute | solution.py:35
  47.5 3.0 %output.1 = f32[128,1152]{1,0:T(8,128)} custom-call(s32[1]{0:T(128)} %bitcast.me_ref, bf16[128,1152]{1,0:T(8,128)(2,1)S(1)} %copy-done.2, bf16[4224,1152]{1,0:T(8,128)(2,1)S(1)} %get-tuple-element.45.refs_0_, bf16[1920,1152]{1,0:T(8,128)(2,1)S(1)} %get-tuple-element.55.refs_1_, bf16[32,6144]{1,0:T(8,128)(2,1)S(1)} %unfold_rows.2.refs_2_, ...), custom_call_target="tpu_custom_call" | custom-call | tf_op jit(solution)/shard_map/output/pallas_call | solution.py:607
  (36 shorter events, 1.9 us)
Async XLA Ops:
  0.6 14.1 %copy-start.4 = (s32[8]{0:T(128)S(1)}, s32[8]{0:T(128)}, u32[]{:S(2)}) copy-start(s32[8]{0:T(128)} %param.17) | copy-start | bytes 100
  7.1 2.6 %collective-permute-start = (bf16[64,6656]{1,0:T(8,128)(2,1)S(1)}, bf16[64,6656]{1,0:T(8,128)(2,1)S(1)}, u32[]{:S(2)}, u32[]{:S(2)}) collective-permute-start(bf16[64,6656]{1,0:T(8,128)(2,1)S(1)} %get-tuple-element.35), channel_id=1, source_target_pairs={{0,1},{1,0},{2,3},{3,2},{4,5},{5,4},{6,7},{7,6},{8,9},{9,8},{10,11... | collective-permute-start | bytes 2555912 | tf_op jit(solution)/shard_map/ppermute | solution.py:35
  7.6 2.1 %collective-permute-start.1 = (f32[128,128]{1,0:T(8,128)S(1)}, f32[128,128]{1,0:T(8,128)S(1)}, u32[]{:S(2)}, u32[]{:S(2)}) collective-permute-start(f32[128,128]{1,0:T(8,128)S(1)} %get-tuple-element.37.extra_ref), channel_id=1, source_target_pairs={{0,1},{1,0},{2,3},{3,2},{4,5},{5,4},{6,7},{7,6},{8,9},{9,8},{10,11... | collective-permute-start | bytes 196616 | tf_op jit(solution)/shard_map/ppermute | solution.py:35
  10.1 8.1 %collective-permute-start.2 = (bf16[16,3968]{1,0:T(8,128)(2,1)S(1)}, bf16[16,3968]{1,0:T(8,128)(2,1)S(1)}, u32[]{:S(2)}, u32[]{:S(2)}) collective-permute-start(bf16[16,3968]{1,0:T(8,128)(2,1)S(1)} %get-tuple-element.39), channel_id=1, source_target_pairs={{0,6},{1,7},{2,4},{3,5},{4,2},{5,3},{6,0},{7,1},{8,14},{9,15},{10,... | collective-permute-start | bytes 380936 | tf_op jit(solution)/shard_map/ppermute | solution.py:35
  14.0 7.2 %collective-permute-start.3 = (bf16[16,3968]{1,0:T(8,128)(2,1)S(1)}, bf16[16,3968]{1,0:T(8,128)(2,1)S(1)}, u32[]{:S(2)}, u32[]{:S(2)}) collective-permute-start(bf16[16,3968]{1,0:T(8,128)(2,1)S(1)} %get-tuple-element.42), channel_id=1, source_target_pairs={{0,2},{1,3},{2,0},{3,1},{4,6},{5,7},{6,4},{7,5},{8,10},{9,11},{10,... | collective-permute-start | bytes 380936 | tf_op jit(solution)/shard_map/ppermute | solution.py:35
  14.5 6.9 %collective-permute-start.4 = (bf16[16,3968]{1,0:T(8,128)(2,1)S(1)}, bf16[16,3968]{1,0:T(8,128)(2,1)S(1)}, u32[]{:S(2)}, u32[]{:S(2)}) collective-permute-start(bf16[16,3968]{1,0:T(8,128)(2,1)S(1)} %get-tuple-element.43), channel_id=1, source_target_pairs={{0,4},{1,5},{2,6},{3,7},{4,0},{5,1},{6,2},{7,3},{8,12},{9,13},{10,... | collective-permute-start | bytes 380936 | tf_op jit(solution)/shard_map/ppermute | solution.py:35
  14.7 13.9 %collective-permute-start.5 = (bf16[16,3456]{1,0:T(8,128)(2,1)S(1)}, bf16[16,3456]{1,0:T(8,128)(2,1)S(1)}, u32[]{:S(2)}, u32[]{:S(2)}) collective-permute-start(bf16[16,3456]{1,0:T(8,128)(2,1)S(1)} %get-tuple-element.49), channel_id=1, source_target_pairs={{0,2},{1,3},{2,0},{3,1},{4,6},{5,7},{6,4},{7,5},{8,10},{9,11},{10,... | collective-permute-start | bytes 331784 | tf_op jit(solution)/shard_map/ppermute | solution.py:35
  16.6 12.0 %collective-permute-start.6 = (bf16[16,3456]{1,0:T(8,128)(2,1)S(1)}, bf16[16,3456]{1,0:T(8,128)(2,1)S(1)}, u32[]{:S(2)}, u32[]{:S(2)}) collective-permute-start(bf16[16,3456]{1,0:T(8,128)(2,1)S(1)} %get-tuple-element.50), channel_id=1, source_target_pairs={{0,4},{1,5},{2,6},{3,7},{4,0},{5,1},{6,2},{7,3},{8,12},{9,13},{10,... | collective-permute-start | bytes 331784 | tf_op jit(solution)/shard_map/ppermute | solution.py:35
  18.2 10.4 %collective-permute-start.7 = (bf16[16,3456]{1,0:T(8,128)(2,1)S(1)}, bf16[16,3456]{1,0:T(8,128)(2,1)S(1)}, u32[]{:S(2)}, u32[]{:S(2)}) collective-permute-start(bf16[16,3456]{1,0:T(8,128)(2,1)S(1)} %get-tuple-element.51), channel_id=1, source_target_pairs={{0,6},{1,7},{2,4},{3,5},{4,2},{5,3},{6,0},{7,1},{8,14},{9,15},{10,... | collective-permute-start | bytes 331784 | tf_op jit(solution)/shard_map/ppermute | solution.py:35
  21.8 8.6 %collective-permute-start.8 = (bf16[16,3968]{1,0:T(8,128)(2,1)S(1)}, bf16[16,3968]{1,0:T(8,128)(2,1)S(1)}, u32[]{:S(2)}, u32[]{:S(2)}) collective-permute-start(bf16[16,3968]{1,0:T(8,128)(2,1)S(1)} %get-tuple-element.52), channel_id=1, source_target_pairs={{0,8},{1,9},{2,10},{3,11},{4,12},{5,13},{6,14},{7,15},{8,0},{9,1},... | collective-permute-start | bytes 380936 | tf_op jit(solution)/shard_map/ppermute | solution.py:35
  24.5 5.8 %copy-start.3 = (s32[8]{0:T(128)S(1)}, s32[8]{0:T(128)}, u32[]{:S(2)}) copy-start(s32[8]{0:T(128)} %param.16) | copy-start | bytes 100
  24.5 5.9 %copy-start = (bf16[8,512,256]{2,1,0:T(8,128)(2,1)S(1)}, bf16[8,512,256]{2,1,0:T(8,128)(2,1)}, u32[]{:S(2)}) copy-start(bf16[8,512,256]{2,1,0:T(8,128)(2,1)} %key_ref.1) | copy-start | bytes 6291460
  24.6 5.9 %copy-start.1 = (bf16[8,512,256]{2,1,0:T(8,128)(2,1)S(1)}, bf16[8,512,256]{2,1,0:T(8,128)(2,1)}, u32[]{:S(2)}) copy-start(bf16[8,512,256]{2,1,0:T(8,128)(2,1)} %value_ref.1) | copy-start | bytes 6291460
  31.9 6.4 %collective-permute-start.9 = (bf16[16,3072]{1,0:T(8,128)(2,1)S(1)}, bf16[16,3072]{1,0:T(8,128)(2,1)S(1)}, u32[]{:S(2)}, u32[]{:S(2)}) collective-permute-start(bf16[16,3072]{1,0:T(8,128)(2,1)S(1)} %get-tuple-element.57.refs_0_), channel_id=1, source_target_pairs={{0,8},{1,9},{2,10},{3,11},{4,12},{5,13},{6,14},{7,15},{8,0},{9,1},... | collective-permute-start | bytes 294920 | tf_op jit(solution)/shard_map/ppermute | solution.py:35
  32.3 8.7 %collective-permute-start.15 = (bf16[16,3072]{1,0:T(8,128)(2,1)S(1)}, bf16[16,3072]{1,0:T(8,128)(2,1)S(1)}, u32[]{:S(2)}, u32[]{:S(2)}) collective-permute-start(bf16[16,3072]{1,0:T(8,128)(2,1)S(1)} %get-tuple-element.57.refs_0_), channel_id=1, source_target_pairs={{0,6},{1,7},{2,4},{3,5},{4,2},{5,3},{6,0},{7,1},{8,14},{9,15},{10,... | collective-permute-start | bytes 294920 | tf_op jit(solution)/shard_map/ppermute | solution.py:35
  35.2 9.5 %collective-permute-start.11 = (bf16[16,3072]{1,0:T(8,128)(2,1)S(1)}, bf16[16,3072]{1,0:T(8,128)(2,1)S(1)}, u32[]{:S(2)}, u32[]{:S(2)}) collective-permute-start(bf16[16,3072]{1,0:T(8,128)(2,1)S(1)} %get-tuple-element.57.refs_0_), channel_id=1, source_target_pairs={{0,4},{1,5},{2,6},{3,7},{4,0},{5,1},{6,2},{7,3},{8,12},{9,13},{10,... | collective-permute-start | bytes 294920 | tf_op jit(solution)/shard_map/ppermute | solution.py:35
  35.7 9.1 %collective-permute-start.10 = (bf16[16,3072]{1,0:T(8,128)(2,1)S(1)}, bf16[16,3072]{1,0:T(8,128)(2,1)S(1)}, u32[]{:S(2)}, u32[]{:S(2)}) collective-permute-start(bf16[16,3072]{1,0:T(8,128)(2,1)S(1)} %get-tuple-element.57.refs_0_), channel_id=1, source_target_pairs={{0,2},{1,3},{2,0},{3,1},{4,6},{5,7},{6,4},{7,5},{8,10},{9,11},{10,... | collective-permute-start | bytes 294920 | tf_op jit(solution)/shard_map/ppermute | solution.py:35
  38.3 6.6 %collective-permute-start.16 = (bf16[16,3072]{1,0:T(8,128)(2,1)S(1)}, bf16[16,3072]{1,0:T(8,128)(2,1)S(1)}, u32[]{:S(2)}, u32[]{:S(2)}) collective-permute-start(bf16[16,3072]{1,0:T(8,128)(2,1)S(1)} %collective-permute-done.9.after_ref.refs_3_), channel_id=1, source_target_pairs={{0,6},{1,7},{2,4},{3,5},{4,2},{5,3},{6,0},{7,1},{8,14},{9,15},{10,... | collective-permute-start | bytes 294920 | tf_op jit(solution)/shard_map/ppermute | solution.py:35
  38.8 6.1 %collective-permute-start.14 = (bf16[16,3072]{1,0:T(8,128)(2,1)S(1)}, bf16[16,3072]{1,0:T(8,128)(2,1)S(1)}, u32[]{:S(2)}, u32[]{:S(2)}) collective-permute-start(bf16[16,3072]{1,0:T(8,128)(2,1)S(1)} %collective-permute-done.9.after_ref.refs_3_), channel_id=1, source_target_pairs={{0,4},{1,5},{2,6},{3,7},{4,0},{5,1},{6,2},{7,3},{8,12},{9,13},{10,... | collective-permute-start | bytes 294920 | tf_op jit(solution)/shard_map/ppermute | solution.py:35
  41.1 4.6 %collective-permute-start.13 = (bf16[16,3072]{1,0:T(8,128)(2,1)S(1)}, bf16[16,3072]{1,0:T(8,128)(2,1)S(1)}, u32[]{:S(2)}, u32[]{:S(2)}) collective-permute-start(bf16[16,3072]{1,0:T(8,128)(2,1)S(1)} %collective-permute-done.9.after_ref.refs_3_), channel_id=1, source_target_pairs={{0,2},{1,3},{2,0},{3,1},{4,6},{5,7},{6,4},{7,5},{8,10},{9,11},{10,... | collective-permute-start | bytes 294920 | tf_op jit(solution)/shard_map/ppermute | solution.py:35
  41.8 5.7 %copy-start.2 = (bf16[128,1152]{1,0:T(8,128)(2,1)S(1)}, bf16[128,1152]{1,0:T(8,128)(2,1)}, u32[]{:S(2)}) copy-start(bf16[128,1152]{1,0:T(8,128)(2,1)} %x_ref.1) | copy-start | bytes 884740
  44.8 1.8 %collective-permute-start.12 = (bf16[32,6144]{1,0:T(8,128)(2,1)S(1)}, bf16[32,6144]{1,0:T(8,128)(2,1)S(1)}, u32[]{:S(2)}, u32[]{:S(2)}) collective-permute-start(bf16[32,6144]{1,0:T(8,128)(2,1)S(1)} %unfold_rows.2.refs_2_), channel_id=1, source_target_pairs={{0,1},{1,0},{2,3},{3,2},{4,5},{5,4},{6,7},{7,6},{8,9},{9,8},{10,11... | collective-permute-start | bytes 1179656 | tf_op jit(solution)/shard_map/ppermute | solution.py:35
  45.7 1.8 %collective-permute-start.17 = (bf16[32,6144]{1,0:T(8,128)(2,1)S(1)}, bf16[32,6144]{1,0:T(8,128)(2,1)S(1)}, u32[]{:S(2)}, u32[]{:S(2)}) collective-permute-start(bf16[32,6144]{1,0:T(8,128)(2,1)S(1)} %unfold_rows.3.refs_4_), channel_id=1, source_target_pairs={{0,1},{1,0},{2,3},{3,2},{4,5},{5,4},{6,7},{7,6},{8,9},{9,8},{10,11... | collective-permute-start | bytes 1179656 | tf_op jit(solution)/shard_map/ppermute | solution.py:35
